TPU v7x, 32 devices: a whole 2x2x4 slice. The times are simulated.
32 devices in a mesh: gx: 4 (over z), gy: 8 (over y, x, core).
Axes of the slice: x: 2, y: 2, z: 4, core: 2. Of those that a mesh axis runs over, the one named last changes fastest.
Arguments:
- tokens: bfloat16 [256, 14, 20, 384], P(('gx', 'gy')), may hold values from -6 to 6
- bucket: int32 [256], P(('gx', 'gy')), may hold values from 0 to 1
- counts: int32 [32], P(('gx', 'gy')), may hold values from 4 to 8, as said below
- mod_weights: bfloat16 [591360], P(('gx', 'gy')), may hold values from -0.3125 to 0.3125
- mlp_weights: bfloat16 [1179648], P(('gx', 'gy')), may hold values from -0.3125 to 0.3125
- small_params: bfloat16 [37664], P(('gx', 'gy')), as said below
- cotangent: bfloat16 [256, 14, 20, 384], P(('gx', 'gy')), may hold values from -6 to 6
Outputs:
- out_tokens: bfloat16 [256, 14, 20, 384], P(('gx', 'gy'))
- grad_tokens: float32 [256, 14, 20, 384], P(('gx', 'gy'))
- grad_mod: float32 [591360], P(('gx', 'gy'))
- grad_mlp: float32 [1179648], P(('gx', 'gy'))
- grad_small: float32 [37664], P(('gx', 'gy'))
Inputs may be any that keep to these rules, and one draw needn't show every extreme that they name: `counts`: each device's live slots; some device holds exactly 8. `small_params`: Gains, biases, depthwise kernels and layer scales in the stated layout.
All inputs are finite; a program needn't handle non-finite values.
Results may differ from a plain program's by a relative error of at most 0.0084.
Values may be sent and summed in bfloat16 or wider, within the bound.
No kernel may reach another device: no remote copies, remote signals or barrier semaphores. Data moves between devices by JAX's collectives and lax.ppermute only.
A program may use at most 448 MiB of HBM per device.

v0:
```python
import functools

import jax
import jax.numpy as jnp
import numpy as np
from jax import lax
from jax.experimental import pallas as pl
from jax.experimental.pallas import tpu as pltpu
from jax.sharding import PartitionSpec as P

C = 384
HID = 1536
GH = 14
GW = 20
HALF = 144
IMG = 2 * HALF
PAIR = 2 * IMG
C2 = 2 * C
NY = 17
NX = 23
NV = 12
NU = 8
Q = NU * NV
AR = 2 * (Q + 16)
BR = 2 * Q
SR = 4 * Q + 32
LEVELS = (3, 5, 7)
TAPS = 64
GATES = 128
MERGED = C2 + GATES
BROWS = 768
HCHUNK = 512
AXES = ("gx", "gy")
f32 = jnp.float32
bf16 = jnp.bfloat16
EPS = 1e-05
ROOT_HALF = 0.7071067811865476
INV_ROOT_2PI = 0.3989422804014327


def _hi(a):
    return a.astype(bf16)


def _lo(a):
    return (a - a.astype(bf16).astype(np.float64)).astype(bf16)


@functools.lru_cache(maxsize=None)
def constants():
    row = np.arange(HALF)
    real = (row < 7 * GW).astype(np.float64)
    yy = np.minimum(row // GW, 6) - (GH - 1) / 2
    xx = row % GW - (GW - 1) / 2
    uv = [(u, v) for u in range(1, NU + 1) for v in range(NV)]
    u0 = [(0, v) for v in range(NV)]
    wu = 2 * np.pi / NY
    wv = 2 * np.pi / NX

    def trig(pairs, pad):
        u = np.array([p[0] for p in pairs] + [0] * pad, np.float64)[:, None]
        v = np.array([p[1] for p in pairs] + [0] * pad, np.float64)[:, None]
        use = np.array([1.0] * len(pairs) + [0.0] * pad)[:, None] * real[None]
        cy, sy = np.cos(wu * u * yy) * use, np.sin(wu * u * yy) * use
        cx, sx = np.cos(wv * v * xx), np.sin(wv * v * xx)
        weight = np.where(u > 0, 2.0, 1.0) * np.where(v > 0, 2.0, 1.0) / (NY * NX)
        return cy * cx, -cy * sx, sy * cx, -sy * sx, weight

    e_re, e_im, o_re, o_im, w1 = trig(uv, 0)
    z_re, z_im, _, _, w0 = trig(u0, 16 - NV)
    fe = np.concatenate([e_re, z_re, e_im, z_im], 0)
    fo = np.concatenate([o_re, o_im], 0)
    half = np.concatenate([0.5 * w1, w0, 0.5 * w1, w0], 0)
    ge = (fe * half).T
    go = (fo * np.concatenate([0.5 * w1, 0.5 * w1], 0)).T

    u = np.array([p[0] for p in uv], np.float64)[:, None]
    v = np.array([p[1] for p in uv], np.float64)[:, None]
    v0 = np.array(list(range(NV)) + [0] * (16 - NV), np.float64)[:, None]
    use0 = np.array([1.0] * NV + [0.0] * (16 - NV))[:, None]
    wp = np.where(v > 0, 2.0, 1.0) / (NY * NX)
    wz = np.where(v0 > 0, 2.0, 1.0) * use0 / (NY * NX)
    weights = np.concatenate([wp, -wp, wp, -wp, wz, -wz], 0)
    es = []
    for k in LEVELS:
        h = k // 2
        ty, tx = np.meshgrid(np.arange(k) - h, np.arange(k) - h, indexing="ij")
        for bucket in (0, 1):
            sy, sx = (ty, tx) if bucket == 0 else (tx, ty)
            py = sy.reshape(1, -1) * wu
            px = sx.reshape(1, -1) * wv
            plus = u * py + v * px
            minus = -u * py + v * px
            zero = v0 * px
            e = [np.cos(plus), np.sin(plus), np.cos(minus), np.sin(minus), np.cos(zero) * use0, np.sin(zero) * use0]
            whole_e = np.zeros((SR, TAPS))
            whole_e[:, : k * k] = np.concatenate(e, 0)
            es.append(np.concatenate([_hi(whole_e), _lo(whole_e)], 1))
    return dict(
        fe=np.concatenate([_hi(fe), _lo(fe), _hi(fe)], 1),
        fo=np.concatenate([_hi(fo), _lo(fo), _hi(fo)], 1),
        ge=np.concatenate([_hi(ge), _lo(ge), _hi(ge)], 1),
        go=np.concatenate([_hi(go), _lo(go), _hi(go)], 1),
        es=np.stack(es),
        weights=np.broadcast_to(weights, (SR, 128)).astype(np.float32),
    )


def dot(a, b):
    return jnp.dot(a, b, preferred_element_type=f32)


def dot_nt(a, b):
    return lax.dot_general(a, b, (((1,), (1,)), ((), ())), preferred_element_type=f32)


def dot_tn(a, b):
    return lax.dot_general(a, b, (((0,), (0,)), ((), ())), preferred_element_type=f32)


def gelu_pair(x):
    cdf = 0.5 * lax.erf(x * ROOT_HALF) + 0.5
    return x * cdf, cdf + x * (jnp.exp(x * x * -0.5) * INV_ROOT_2PI)


def split(x):
    hi = x.astype(bf16)
    return hi, (x - hi.astype(f32)).astype(bf16)


def at(base, i, n=16):
    return slice(base + i * n, base + i * n + n)


def norm_stats(x):
    mean = jnp.mean(x, axis=-1, keepdims=True)
    centred = x - mean
    var = jnp.mean(centred * centred, axis=-1, keepdims=True)
    r = lax.rsqrt(var + EPS)
    return centred * r, r


def sum8(x):
    total = x[0:8]
    for k in range(1, x.shape[0] // 8):
        total = total + x[8 * k : 8 * k + 8]
    return total


def grid_rows(im, y):
    return im * IMG + (y * GW if y < 7 else HALF + (GH - 1 - y) * GW)


def lanes(im):
    return slice(im * C, im * C + C)


(V_G1, V_B1, V_BQ, V_BC, V_HB, V_PB, V_S1, V_G2, V_B2, V_BM2, V_S2, V_BG) = range(12)
VROWS = 16
(S_HB, S_PB, S_S1, S_G2, S_B2, S_BM2, S_S2, S_BQ) = range(8)


def from_native(src, native):
    slots = src.shape[2]
    line = GW * slots
    for y in range(GH):
        for lt in range(C // 128):
            ls = slice(128 * lt, 128 * lt + 128)
            native[lt, line * y : line * (y + 1), :] = src[y, :, :, ls].astype(f32).reshape(line, 128)


def image_rows(native, image, slot, slots, gain):
    for h in (GH // 2 * GW, HALF + GH // 2 * GW):
        image[h : h + 4, :] = jnp.zeros((4, C), f32)
    for y in range(GH):
        a = grid_rows(0, y)
        for lt in range(C // 128):
            v = native[lt, pl.ds(GW * slots * y + slot, GW, stride=slots), :]
            image[a : a + GW, 128 * lt : 128 * lt + 128] = v if gain is None else v * gain


def kernel_prep(x_ref, xrow_o, nb_o, stat_o, native, image):
    slot = pl.program_id(0)

    @pl.when(slot == 0)
    def _():
        from_native(x_ref, native)

    image_rows(native, image, slot, x_ref.shape[2], None)
    lane = lax.broadcasted_iota(jnp.int32, (32, 128), 1)
    for i in range(IMG // 32):
        s = at(0, i, 32)
        x = image[s, :]
        xrow_o[s, :] = x.astype(bf16)
        mean = jnp.mean(x, axis=-1, keepdims=True)
        centred = x - mean
        r = lax.rsqrt(jnp.mean(centred * centred, axis=-1, keepdims=True) + EPS)
        nb_o[s, :] = (centred * r).astype(bf16)
        stat_o[s, :] = jnp.where(lane == 0, mean, r)


def kernel_upstream(counts, cot_ref, up_o, native, image):
    slot = pl.program_id(0)

    @pl.when(slot == 0)
    def _():
        from_native(cot_ref, native)

    image_rows(native, image, slot, cot_ref.shape[2], (slot < counts[0]).astype(f32))
    for i in range(IMG // 32):
        s = at(0, i, 32)
        up_o[s, :] = image[s, :].astype(bf16)


CHAINS = 3
CHAIN = C2 // CHAINS


def staggered(phases):
    lists = [phases(t) for t in range(CHAINS)]
    for turn in range(len(lists[0]) + CHAINS - 1):
        for t in range(CHAINS):
            if 0 <= turn - t < len(lists[t]):
                lists[t][turn - t]()


def sub_tiles(t):
    for k in range(t * CHAIN // 128, (t + 1) * CHAIN // 128):
        lt = k % (C // 128)
        yield k // (C // 128), slice(128 * k, 128 * k + 128), slice(128 * lt, 128 * lt + 128)


def spread_gates(gates, wide):
    for k in range(4):
        for i in range(PAIR // 32):
            s = at(0, i, 32)
            wide[k, s, :] = jnp.broadcast_to(gates[s, k : k + 1], (32, 128))


def kernel_forward(
    bucket, x_ref, stat, wf, vec, kcat, es, fe, fo, ge, go,
    q_o, gates_o, mixed_o, z_o, g_o, spec_o, mean_o,
    h_o, normed, ctx, ecat, ocat, s_a, s_b, s_e, s_o, yca, ycb, mix, wide,
):
    step = pl.program_id(0)

    @pl.when(step == 0)
    def _():
        for lb in range(6):
            h_o[lb] = dot(es[lb], kcat[lb // 2])

    g1, b1 = vec[V_G1 : V_G1 + 1, :], vec[V_B1 : V_B1 + 1, :]
    for i in range(PAIR // 32):
        s = at(0, i, 32)
        n = (x_ref[s, :].astype(f32) - stat[s, 0:1]) * stat[s, 1:2]
        normed[s, :] = (n * g1 + b1).astype(bf16)
    right = dot(normed[...], wf[:, C + 128 :])
    left = dot(normed[...], wf[:, : C + 128])
    ctx[:, :128] = left[:, C:] + vec[V_BC : V_BC + 1, :128]
    ctx[:, 128:] = right[:, : C - 128] + vec[V_BC : V_BC + 1, 128:]
    gates_o[...] = right[:, C - 128 :] + vec[V_BG : V_BG + 1, :GATES]
    q_o[...] = left[:, :C] + vec[V_BQ : V_BQ + 1, :]
    spread_gates(gates_o, wide)
    lbs = [[level * 2 + bucket[step * 2 + im] for im in range(2)] for level in range(3)]

    def put_pair(ls, i, top, bot):
        e_hi, e_lo = split(top + bot)
        o_hi, o_lo = split(top - bot)
        for base, ev, ov in ((0, e_hi, o_hi), (HALF, e_hi, o_hi), (2 * HALF, e_lo, o_lo)):
            ecat[at(base, i), ls] = ev
            ocat[at(base, i), ls] = ov

    def first(t):
        for im, ls, hs in sub_tiles(t):
            for i in range(HALF // 16):
                put_pair(ls, i, ctx[at(im * IMG, i), hs], ctx[at(im * IMG + HALF, i), hs])

    def transform(t):
        ts = slice(t * CHAIN, (t + 1) * CHAIN)
        s_a[:, ts] = dot(fe[...], ecat[:, ts])
        s_b[:, ts] = dot(fo[...], ocat[:, ts])

    def back(t):
        ts = slice(t * CHAIN, (t + 1) * CHAIN)
        s_e[:, ts] = dot(ge[...], yca[:, ts])
        s_o[:, ts] = dot(go[...], ycb[:, ts])

    def filt(t, level):
        base = level * SR
        for im, ls, hs in sub_tiles(t):
            lb = lbs[level][im]
            for i in range(Q // 16):
                a_re, a_im = s_a[at(0, i), ls], s_a[at(Q + 16, i), ls]
                b_re, b_im = s_b[at(0, i), ls], s_b[at(Q, i), ls]
                xp_re, xp_im = a_re + b_im, a_im - b_re
                xm_re, xm_im = a_re - b_im, a_im + b_re
                spec_o[at(base, i), ls] = xp_re.astype(bf16)
                spec_o[at(base + Q, i), ls] = xp_im.astype(bf16)
                spec_o[at(base + 2 * Q, i), ls] = xm_re.astype(bf16)
                spec_o[at(base + 3 * Q, i), ls] = xm_im.astype(bf16)
                p_re, p_im = h_o[lb, at(0, i), hs], h_o[lb, at(Q, i), hs]
                q_re, q_im = h_o[lb, at(2 * Q, i), hs], h_o[lb, at(3 * Q, i), hs]
                yp_re, yp_im = p_re * xp_re - p_im * xp_im, p_re * xp_im + p_im * xp_re
                ym_re, ym_im = q_re * xm_re - q_im * xm_im, q_re * xm_im + q_im * xm_re
                for dst, off, width, val in (
                    (yca, 0, AR, yp_re + ym_re),
                    (yca, Q + 16, AR, yp_im + ym_im),
                    (ycb, 0, BR, ym_im - yp_im),
                    (ycb, Q, BR, yp_re - ym_re),
                ):
                    hi, lo = split(val)
                    dst[at(off, i), ls] = hi
                    dst[at(off + width, i), ls] = hi
                    dst[at(off + 2 * width, i), ls] = lo
            x_re, x_im = s_a[Q : Q + 16, ls], s_a[2 * Q + 16 : 2 * Q + 32, ls]
            spec_o[base + 4 * Q : base + 4 * Q + 16, ls] = x_re.astype(bf16)
            spec_o[base + 4 * Q + 16 : base + 4 * Q + 32, ls] = x_im.astype(bf16)
            p_re, p_im = h_o[lb, 4 * Q : 4 * Q + 16, hs], h_o[lb, 4 * Q + 16 : 4 * Q + 32, hs]
            for off, val in ((Q, p_re * x_re - p_im * x_im), (2 * Q + 16, p_re * x_im + p_im * x_re)):
                hi, lo = split(val)
                yca[off : off + 16, ls] = hi
                yca[off + AR : off + AR + 16, ls] = hi
                yca[off + 2 * AR : off + 2 * AR + 16, ls] = lo

    def act(t, level):
        for im, ls, hs in sub_tiles(t):
            total = jnp.zeros((8, 128), f32)
            for i in range(HALF // 16):
                even, odd = s_e[at(0, i), ls], s_o[at(0, i), ls]
                both = []
                for h, a in ((0, even + odd), (HALF, even - odd)):
                    z, g = gelu_pair(a)
                    z_o[at(level * IMG + h, i), ls] = z.astype(bf16)
                    g_o[at(level * IMG + h, i), ls] = g.astype(bf16)
                    s = at(im * IMG + h, i)
                    part = z * wide[level, s, :]
                    mix[s, hs] = part if level == 0 else mix[s, hs] + part
                    both.append(z)
                if level < 2:
                    put_pair(ls, i, both[0], both[1])
                else:
                    total = total + sum8(both[0]) + sum8(both[1])
            if level == 2:
                mean = jnp.sum(total, axis=0, keepdims=True) * (1.0 / (GH * GW))
                mean_o[:, ls] = jnp.broadcast_to(mean, (8, 128))
                glob, _ = gelu_pair(mean)
                for i in range(IMG // 16):
                    s = at(im * IMG, i)
                    mixed_o[s, hs] = (mix[s, hs] + wide[3, s, :] * glob).astype(bf16)

    def phases(t):
        steps = [lambda: first(t)]
        for level in range(3):
            steps += [
                lambda: transform(t),
                lambda level=level: filt(t, level),
                lambda: back(t),
                lambda level=level: act(t, level),
            ]
        return steps

    staggered(phases)


def kernel_middle(
    gx, gy, mlp_len, pos, x_ref, up, mixed, q_ref, wh, wp, w1, w2, vec, bm1,
    dmid_o, out_o, dq_o, dmix_o, own, oth, gwh, gwp, sums, bsum,
    mod, modulated, branch, mid, second, dshr, shr, dsec, act, dexp, hid, vacc, bacc, gw1, gw2, flat,
):
    step = pl.program_id(0)

    @pl.when(step == 0)
    def _():
        for ref in (gw1, gw2, gwh, gwp, vacc, bacc):
            ref[...] = jnp.zeros_like(ref)

    g2, b2 = vec[V_G2 : V_G2 + 1, :], vec[V_B2 : V_B2 + 1, :]
    s1, s2 = vec[V_S1 : V_S1 + 1, :], vec[V_S2 : V_S2 + 1, :]
    bm2 = vec[V_BM2 : V_BM2 + 1, :]
    zero = jnp.zeros((8, C), f32)

    mod[...] = dot(mixed[...], wh[...]) + vec[V_HB : V_HB + 1, :]
    for i in range(BROWS // 32):
        s = at(0, i, 32)
        modulated[s, :] = (q_ref[s, :] * mod[s, :]).astype(bf16)
        dshr[s, :] = (up[s, :].astype(f32) * s2).astype(bf16)
    branch[...] = dot(modulated[...], wp[...]) + vec[V_PB : V_PB + 1, :]
    for i in range(BROWS // 32):
        s = at(0, i, 32)
        middle = x_ref[s, :].astype(f32) + s1 * branch[s, :]
        mid[s, :] = middle
        n, _ = norm_stats(middle)
        second[s, :] = (n * g2 + b2).astype(bf16)

    for h in range(HID // HCHUNK):
        hs = slice(h * HCHUNK, (h + 1) * HCHUNK)
        hid[...] = dot(second[...], w1[:, hs]) + bm1[0:1, hs]
        dact = dot_nt(dshr[...], w2[hs, :])
        total = jnp.zeros((8, HCHUNK), f32)
        for i in range(BROWS // 16):
            s = at(0, i)
            z, g = gelu_pair(hid[s, :])
            act[s, :] = z.astype(bf16)
            d = dact[s, :] * g
            dexp[s, :] = d.astype(bf16)
            total = total + sum8(d)
        bacc[:, hs] += total
        part = dot(act[...], w2[hs, :])
        back = dot_nt(dexp[...], w1[:, hs])
        if h == 0:
            shr[...] = part
            dsec[...] = back
        else:
            shr[...] += part
            dsec[...] += back
        gw1[:, hs] += dot_tn(second[...], dexp[...])
        gw2[hs, :] += dot_tn(act[...], dshr[...])

    t_s1 = t_g2 = t_b2 = t_bm2 = t_s2 = t_pb = t_hb = t_bq = zero
    dbr = second
    for i in range(BROWS // 32):
        s = at(0, i, 32)
        middle = mid[s, :]
        u = up[s, :].astype(f32)
        shrunk = shr[s, :] + bm2
        out_o[s, :] = middle + s2 * shrunk
        n, r = norm_stats(middle)
        d = dsec[s, :]
        e = d * g2
        dn = d * n
        dv = r * (e - jnp.mean(e, axis=-1, keepdims=True) - n * jnp.mean(e * n, axis=-1, keepdims=True))
        dm = u + dv
        dmid_o[s, :] = dm
        db = s1 * dm
        dbr[s, :] = db.astype(bf16)
        t_s1 = t_s1 + sum8(dm * branch[s, :])
        t_g2 = t_g2 + sum8(dn)
        t_b2 = t_b2 + sum8(d)
        t_bm2 = t_bm2 + sum8(dshr[s, :].astype(f32))
        t_s2 = t_s2 + sum8(u * shrunk)
        t_pb = t_pb + sum8(db)

    gwp[...] += dot_tn(modulated[...], dbr[...])
    dmod = dot_nt(dbr[...], wp[...])
    dm2 = dshr
    for i in range(BROWS // 32):
        s = at(0, i, 32)
        dm = dmod[s, :]
        dq = dm * mod[s, :]
        dd = dm * q_ref[s, :]
        dq_o[s, :] = dq.astype(bf16)
        dm2[s, :] = dd.astype(bf16)
        t_bq = t_bq + sum8(dq)
        t_hb = t_hb + sum8(dd)
    gwh[...] += dot_tn(mixed[...], dm2[...])
    dmix_o[...] = dot_nt(dm2[...], wh[...])

    for k, t in ((S_HB, t_hb), (S_PB, t_pb), (S_S1, t_s1), (S_G2, t_g2), (S_B2, t_b2), (S_BM2, t_bm2), (S_S2, t_s2), (S_BQ, t_bq)):
        vacc[k] += t

    @pl.when(step == pl.num_programs(0) - 1)
    def _():
        for k in range(8):
            sums[k : k + 1, :] = jnp.sum(vacc[k], axis=0, keepdims=True)
        bsum[...] = jnp.broadcast_to(jnp.sum(bacc[...], axis=0, keepdims=True), bsum.shape)
        pack_mlp(gx, gy, mlp_len, pos, gw1, gw2, own, oth, flat)


def kernel_backward(
    gx, gy, mod_len, small_len,
    bucket, pos, nb_ref, dq_ref, dmix, gates, z_ref, g_ref, spec, mean_ref, kcat, wf, vec, sums, bsum, gwh, gwp, es, weights,
    fe, fo, ge, go,
    dmer, own, oth,
    gwf, fsum, gb, dk, h_ref, ecat, ocat, s_a, s_b, s_e, s_o, yca, ycb, acc, facc, wide, flat, small, moved, spread,
):
    step = pl.program_id(0)
    last = pl.num_programs(0) - 1

    @pl.when(step == 0)
    def _():
        for ref in (gwf, facc, acc):
            ref[...] = jnp.zeros_like(ref)
        for lb in range(6):
            h_ref[lb] = dot(es[lb], kcat[lb // 2])

    spread_gates(gates, wide)
    lbs = [[level * 2 + bucket[step * 2 + im] for im in range(2)] for level in range(3)]
    globs = [gelu_pair(mean_ref[0:1, lanes(im)]) for im in range(2)]
    lane = lax.broadcasted_iota(jnp.int32, (16, GATES), 1)
    dmeans = {}

    def mean_grad(t):
        for im, ls, hs in sub_tiles(t):
            total = jnp.zeros((8, 128), f32)
            for i in range(IMG // 16):
                s = at(im * IMG, i)
                total = total + sum8(dmix[s, hs] * wide[3, s, :])
            dmeans[ls.start] = jnp.sum(total, axis=0, keepdims=True) * globs[im][1][:, hs] * (1.0 / (GH * GW))

    def gate_grad(part):
        t_g = jnp.zeros((8, GATES), f32)
        n = 2 * (HALF // 16) // CHAINS
        for im, i in [(im, i) for im in range(2) for i in range(HALF // 16)][part * n : part * n + n]:
            for h in (0, HALF):
                s = at(im * IMG + h, i)
                dm = dmix[s, :]
                dg = jnp.zeros((16, GATES), f32)
                for k in range(4):
                    other = z_ref[at(k * IMG + h, i), lanes(im)].astype(f32) if k < 3 else globs[im][0]
                    col = jnp.sum(dm * other, axis=-1, keepdims=True)
                    dg = jnp.where(lane == k, col, dg)
                dmer[s, :C] = dq_ref[s, :]
                dmer[s, C2:] = dg.astype(bf16)
                t_g = t_g + sum8(dg)
        facc[:, C2:] += t_g

    def before(t, level):
        for im, ls, hs in sub_tiles(t):
            for i in range(HALF // 16):
                if level < 2:
                    even, odd = s_e[at(0, i), ls], s_o[at(0, i), ls]
                    through = (even + odd, even - odd)
                else:
                    through = (dmeans[ls.start], dmeans[ls.start])
                parts = []
                for k, h in enumerate((0, HALF)):
                    s = at(im * IMG + h, i)
                    dz = wide[level, s, :] * dmix[s, hs] + through[k]
                    parts.append(dz * g_ref[at(level * IMG + h, i), ls].astype(f32))
                ecat[at(0, i), ls] = (parts[0] + parts[1]).astype(bf16)
                ocat[at(0, i), ls] = (parts[0] - parts[1]).astype(bf16)

    def transform(t):
        ts = slice(t * CHAIN, (t + 1) * CHAIN)
        s_a[:, ts] = dot(fe[...], ecat[:, ts])
        s_b[:, ts] = dot(fo[...], ocat[:, ts])

    def back(t):
        ts = slice(t * CHAIN, (t + 1) * CHAIN)
        s_e[:, ts] = dot(ge[...], yca[:, ts])
        s_o[:, ts] = dot(go[...], ycb[:, ts])

    def filt(t, level):
        base = level * SR
        for im, ls, hs in sub_tiles(t):
            lb = lbs[level][im]
            for i in range(Q // 16):
                a_re, a_im = s_a[at(0, i), ls], s_a[at(Q + 16, i), ls]
                b_re, b_im = s_b[at(0, i), ls], s_b[at(Q, i), ls]
                dp_re, dp_im = a_re + b_im, a_im - b_re
                dm_re, dm_im = a_re - b_im, a_im + b_re
                xp_re, xp_im = spec[at(base, i), ls].astype(f32), spec[at(base + Q, i), ls].astype(f32)
                xm_re, xm_im = spec[at(base + 2 * Q, i), ls].astype(f32), spec[at(base + 3 * Q, i), ls].astype(f32)
                acc[lb, at(0, i), hs] += xp_re * dp_re + xp_im * dp_im
                acc[lb, at(Q, i), hs] += xp_im * dp_re - xp_re * dp_im
                acc[lb, at(2 * Q, i), hs] += xm_re * dm_re + xm_im * dm_im
                acc[lb, at(3 * Q, i), hs] += xm_im * dm_re - xm_re * dm_im
                p_re, p_im = h_ref[lb, at(0, i), hs], h_ref[lb, at(Q, i), hs]
                q_re, q_im = h_ref[lb, at(2 * Q, i), hs], h_ref[lb, at(3 * Q, i), hs]
                yp_re, yp_im = p_re * dp_re + p_im * dp_im, p_re * dp_im - p_im * dp_re
                ym_re, ym_im = q_re * dm_re + q_im * dm_im, q_re * dm_im - q_im * dm_re
                yca[at(0, i), ls] = (yp_re + ym_re).astype(bf16)
                yca[at(Q + 16, i), ls] = (yp_im + ym_im).astype(bf16)
                ycb[at(0, i), ls] = (ym_im - yp_im).astype(bf16)
                ycb[at(Q, i), ls] = (yp_re - ym_re).astype(bf16)
            d_re, d_im = s_a[Q : Q + 16, ls], s_a[2 * Q + 16 : 2 * Q + 32, ls]
            x_re = spec[base + 4 * Q : base + 4 * Q + 16, ls].astype(f32)
            x_im = spec[base + 4 * Q + 16 : base + 4 * Q + 32, ls].astype(f32)
            acc[lb, 4 * Q : 4 * Q + 16, hs] += x_re * d_re + x_im * d_im
            acc[lb, 4 * Q + 16 : 4 * Q + 32, hs] += x_im * d_re - x_re * d_im
            p_re, p_im = h_ref[lb, 4 * Q : 4 * Q + 16, hs], h_ref[lb, 4 * Q + 16 : 4 * Q + 32, hs]
            yca[Q : Q + 16, ls] = (p_re * d_re + p_im * d_im).astype(bf16)
            yca[2 * Q + 16 : 2 * Q + 32, ls] = (p_re * d_im - p_im * d_re).astype(bf16)

    def context(t):
        for im, ls, hs in sub_tiles(t):
            ds = slice(C + hs.start, C + hs.stop)
            total = jnp.zeros((8, 128), f32)
            for i in range(HALF // 16):
                even, odd = s_e[at(0, i), ls], s_o[at(0, i), ls]
                top, bot = even + odd, even - odd
                dmer[at(im * IMG, i), ds] = top.astype(bf16)
                dmer[at(im * IMG + HALF, i), ds] = bot.astype(bf16)
                total = total + sum8(top) + sum8(bot)
            facc[:, ds] += total

    def phases(t):
        steps = [lambda: mean_grad(t)]
        for level in (2, 1, 0):
            steps += [
                lambda level=level: before(t, level),
                lambda: transform(t),
                lambda level=level: filt(t, level),
                lambda: back(t),
            ]
            if level == 2:
                steps.append(lambda: gate_grad(t))
        return steps + [lambda: context(t)]

    staggered(phases)
    gwf[...] += dot_tn(nb_ref[...], dmer[...])

    @pl.when(step == last)
    def _():
        facc[:, :C] = jnp.broadcast_to(sums[S_BQ : S_BQ + 1, :] * 0.125, (8, C))
        colsum = jnp.sum(facc[...], axis=0, keepdims=True)
        fsum[...] = jnp.broadcast_to(colsum, fsum.shape)
        wide = wf[...].astype(f32)
        t_hi, t_lo = split(wide * gwf[...])
        ones = jnp.ones((8, MERGED), bf16)
        gb[0:8, :] = dot_nt(ones, t_hi) + dot_nt(ones, t_lo)
        c_hi, c_lo = split(fsum[...])
        gb[8:16, :] = dot_nt(c_hi, wf[...]) + dot_nt(c_lo, wf[...])
        g1 = jnp.transpose(jnp.broadcast_to(vec[V_G1 : V_G1 + 1, :], (128, C)))
        b1 = jnp.transpose(jnp.broadcast_to(vec[V_B1 : V_B1 + 1, :], (128, C)))
        for t in range(MERGED // 128):
            ls = slice(128 * t, 128 * t + 128)
            gwf[:, ls] = gwf[:, ls] * g1 + b1 * fsum[0:1, ls]
        for level in range(3):
            total = None
            for lb in (level * 2, level * 2 + 1):
                hi, lo = split(acc[lb] * jnp.concatenate([weights[...]] * (C // 128), 1))
                first = dot_tn(es[lb], hi)
                term = first[:TAPS] + first[TAPS:] + dot_tn(es[lb][:, :TAPS], lo)
                total = term if total is None else total + term
            dk[level] = total
        pack_mod(gx, gy, mod_len, small_len, pos, gwf, gwh, gwp, sums, bsum, fsum, gb, dk, own, oth, flat, small, moved, spread)


def to_native(rows_ref, first, native, slot, slots, gain):
    line = GW * slots
    for y in range(GH):
        a = first + grid_rows(0, y)
        for lt in range(C // 128):
            v = rows_ref[a : a + GW, 128 * lt : 128 * lt + 128]
            native[lt, pl.ds(line * y + slot, GW, stride=slots), :] = v if gain is None else v * gain


def write_native(native, out, slots):
    line = GW * slots
    for y in range(GH):
        for lt in range(C // 128):
            v = native[lt, line * y : line * (y + 1), :].reshape(GW, slots, 128)
            out[y, :, :, 128 * lt : 128 * lt + 128] = v.astype(out.dtype)


def kernel_tail(dmer, wf, x_ref, stat, dmid, vec, gtok_o, stage, native):
    step = pl.program_id(0)
    slots = gtok_o.shape[2]
    g1 = vec[V_G1 : V_G1 + 1, :]
    d_normed = dot_nt(dmer[...], wf[...])
    for i in range(PAIR // 32):
        s = at(0, i, 32)
        r = stat[s, 1:2]
        n = (x_ref[s, :].astype(f32) - stat[s, 0:1]) * r
        e = d_normed[s, :] * g1
        dv = e - jnp.mean(e, axis=-1, keepdims=True) - n * jnp.mean(e * n, axis=-1, keepdims=True)
        stage[s, :] = dmid[s, :] + r * dv
    for im in range(2):
        to_native(stage, im * IMG, native, step * 2 + im, slots, None)

    @pl.when(step == pl.num_programs(0) - 1)
    def _():
        write_native(native, gtok_o, slots)


def kernel_out(counts, rows_ref, out_o, native):
    slots = out_o.shape[2]
    for im in range(slots):
        to_native(rows_ref, im * IMG, native, im, slots, (im < counts[0]).astype(f32))
    write_native(native, out_o, slots)


def block_rows(length):
    return 8 * (length // 1024 if length % 1024 == 0 else (length + 1022) // 1024 + 1)


def place(shard, device):
    length = shard.shape[0]
    n = block_rows(length) * 128
    if n == length:
        return shard.reshape(-1, 128)
    offset = lax.rem(device * length, 1024)
    return lax.dynamic_update_slice(jnp.zeros((n,), shard.dtype), shard, (offset,)).reshape(-1, 128)


def take(block, length, device):
    flat = block.reshape(-1)
    if flat.shape[0] == length:
        return flat
    return lax.dynamic_slice(flat, (lax.rem(device * length, 1024),), (length,))


def first_row(length, device):
    return pl.multiple_of((device * length) // 1024 * 8, 8)


def device_at(pos, gy, i, j, c):
    return (pos[0] ^ j) * gy + (pos[1] ^ (2 * i + c))


def shift_left(first, second, sh):
    if sh == 0:
        return first
    lane = lax.broadcasted_iota(jnp.int32, first.shape, 1)
    return jnp.where(lane < 128 - sh, pltpu.roll(first, 128 - sh, 1), pltpu.roll(second, 128 - sh, 1))


def shift_right(first, second, sh):
    lane = lax.broadcasted_iota(jnp.int32, first.shape, 1)
    return jnp.where(lane < sh, pltpu.roll(first, sh, 1), pltpu.roll(second, sh, 1))


WIDE = C2 + 4
WF_ROWS = C * WIDE // 128
W_ROWS = C * C // 128
PERIOD = 32
STRIDE = PERIOD * WIDE // 128
K_ROW = 12
TAIL_ROW = K_ROW + 83 * C // 128
B_HB, B_PB, B_S1, B_G2, B_B2, B_BM1 = (TAIL_ROW + 3 * k for k in range(6))
B_BM2 = B_BM1 + HID // 128
B_S2 = B_BM2 + 3
END_ROW = B_S2 + 3


def kernel_unpack_mod(gx, gy, mod_len, small_len, pos, own, oth, wf_o, wh_o, wp_o, vec_o, bm1_o, kcat_o, flat, small, moved, wide):
    flat[...] = jnp.zeros_like(flat)
    small[...] = jnp.zeros_like(small)
    mr, sr = block_rows(mod_len), block_rows(small_len)
    for i in range(gy // 2):
        for j in range(gx):
            for c, src in enumerate((own, oth)):
                d = device_at(pos, gy, i, j, c)
                block = src[i, j].astype(f32)
                flat[pl.ds(first_row(mod_len, d), mr), :] += block[:mr]
                small[pl.ds(first_row(small_len, d), sr), :] += block[mr : mr + sr]
    lane = lax.broadcasted_iota(jnp.int32, (16, 128), 1)
    for p in range(PERIOD):
        for j in range(MERGED // 128):
            f = WIDE * p + 128 * j
            row, sh = f // 128, f % 128
            a = flat[pl.ds(row, 16, stride=STRIDE), :]
            b = flat[pl.ds(row + 1, 16, stride=STRIDE), :] if sh else a
            v = shift_left(a, b, sh)
            if j == MERGED // 128 - 1:
                v = jnp.where(lane < 4, v, 0.0)
            wide[j, pl.ds(p, 16, stride=PERIOD), :] = v
    for j in range(MERGED // 128):
        wf_o[:, 128 * j : 128 * j + 128] = wide[j, :C, :].astype(bf16)
    for j in range(3):
        ls = slice(128 * j, 128 * j + 128)
        wh_o[:, ls] = flat[pl.ds(WF_ROWS + j, C, stride=3), :].astype(bf16)
        wp_o[:, ls] = flat[pl.ds(WF_ROWS + W_ROWS + j, C, stride=3), :].astype(bf16)
    n = moved.shape[0]
    moved[...] = shift_left(small[0:n, :], small[1 : n + 1, :], 4)
    vec_o[...] = jnp.zeros_like(vec_o)
    for row, src, start in (
        (V_G1, small, 0), (V_B1, small, 3), (V_BQ, small, 6), (V_BC, small, 9),
        (V_HB, moved, B_HB), (V_PB, moved, B_PB), (V_S1, moved, B_S1), (V_G2, moved, B_G2), (V_B2, moved, B_B2),
        (V_BM2, moved, B_BM2), (V_S2, moved, B_S2),
    ):
        for j in range(3):
            vec_o[row : row + 1, 128 * j : 128 * j + 128] = src[start + j : start + j + 1, :]
    vec_o[V_BG : V_BG + 1, 0:128] = jnp.where(lane[0:1] < 4, small[K_ROW : K_ROW + 1, :], 0.0)
    for t in range(HID // 128):
        bm1_o[:, 128 * t : 128 * t + 128] = jnp.broadcast_to(moved[B_BM1 + t : B_BM1 + t + 1, :], (8, 128))
    start = 0
    for level, k in enumerate(LEVELS):
        for j in range(3):
            taps = moved[pl.ds(K_ROW + 3 * start + j, TAPS, stride=3), :].astype(bf16)
            kcat_o[level, 0:TAPS, 128 * j : 128 * j + 128] = taps
            kcat_o[level, TAPS:, 128 * j : 128 * j + 128] = taps
        start += k * k


def kernel_unpack_mlp(gx, gy, mlp_len, pos, *refs):
    blocks, (w1_o, w2_o, flat) = refs[: gy // 2], refs[gy // 2 :]
    mr = block_rows(mlp_len)
    aligned = mr * 128 == mlp_len
    if not aligned:
        flat[...] = jnp.zeros_like(flat)
    for i, src in enumerate(blocks):
        for j in range(gx):
            for c in range(2):
                rows_at = pl.ds(first_row(mlp_len, device_at(pos, gy, i, j, c)), mr)
                if aligned:
                    flat[rows_at, :] = src[c, j].astype(f32)
                else:
                    flat[rows_at, :] += src[c, j].astype(f32)
    for t in range(HID // 128):
        w1_o[:, 128 * t : 128 * t + 128] = flat[pl.ds(t, C, stride=HID // 128), :].astype(bf16)
    for t in range(C // 128):
        w2_o[:, 128 * t : 128 * t + 128] = flat[pl.ds(C * HID // 128 + t, HID, stride=C // 128), :].astype(bf16)


def send_slots(gx, gy, pos, flat, length, base, own, oth):
    mr = block_rows(length)
    for i in range(gy // 2):
        for j in range(gx):
            for c, dst in enumerate((own, oth)):
                d = device_at(pos, gy, i, j, c)
                dst[i, j, base : base + mr, :] = flat[pl.ds(first_row(length, d), mr), :].astype(bf16)


def pack_mlp(gx, gy, mlp_len, pos, gw1, gw2, own, oth, flat):
    used = 2 * C * HID // 128
    if flat.shape[0] > used:
        flat[used:, :] = jnp.zeros_like(flat[used:, :])
    for t in range(HID // 128):
        flat[pl.ds(t, C, stride=HID // 128), :] = gw1[:, 128 * t : 128 * t + 128]
    for t in range(C // 128):
        flat[pl.ds(C * HID // 128 + t, HID, stride=C // 128), :] = gw2[:, 128 * t : 128 * t + 128]
    send_slots(gx, gy, pos, flat, mlp_len, 0, own, oth)


def pack_mod(gx, gy, mod_len, small_len, pos, gwf, gwh, gwp, sums, bsum, fsum, gb, dk, own, oth, flat, small, moved, wide):
    lane = lax.broadcasted_iota(jnp.int32, (16, 128), 1)
    used = WF_ROWS + 2 * W_ROWS
    if flat.shape[0] > used:
        flat[used:, :] = jnp.zeros_like(flat[used:, :])
    for j in range(MERGED // 128):
        wide[j, :C, :] = gwf[:, 128 * j : 128 * j + 128]
    for f in range(STRIDE):
        p = 128 * f // WIDE
        col = 128 * f - WIDE * p
        t, sh = col // 128, col % 128

        def piece(row, tile):
            tile = min(tile, MERGED // 128 - 1)
            return wide[tile, pl.ds(row, 16, stride=PERIOD), :]

        v = shift_left(piece(p, t), piece(p, t + 1), sh)
        left = WIDE - col
        if left < 128:
            v = jnp.where(lane < left, v, pltpu.roll(piece(p + 1, 0), left, 1))
        flat[pl.ds(f, 16, stride=STRIDE), :] = v
    for j in range(3):
        ls = slice(128 * j, 128 * j + 128)
        flat[pl.ds(WF_ROWS + j, C, stride=3), :] = gwh[:, ls]
        flat[pl.ds(WF_ROWS + W_ROWS + j, C, stride=3), :] = gwp[:, ls]
    moved[...] = jnp.zeros_like(moved)
    small[...] = jnp.zeros_like(small)
    start = 0
    for level, k in enumerate(LEVELS):
        for j in range(3):
            moved[pl.ds(K_ROW + 3 * start + j, k * k, stride=3), :] = dk[level, 0 : k * k, 128 * j : 128 * j + 128]
        start += k * k
    for start, row in (
        (B_HB, S_HB), (B_PB, S_PB), (B_S1, S_S1), (B_G2, S_G2), (B_B2, S_B2), (B_BM2, S_BM2), (B_S2, S_S2),
    ):
        for j in range(3):
            moved[start + j : start + j + 1, :] = sums[row : row + 1, 128 * j : 128 * j + 128]
    for t in range(HID // 128):
        moved[B_BM1 + t : B_BM1 + t + 1, :] = bsum[0:1, 128 * t : 128 * t + 128]
    n = moved.shape[0]
    small[8:n, :] = shift_right(moved[7 : n - 1, :], moved[8:n, :], 4)
    for j in range(3):
        ls = slice(128 * j, 128 * j + 128)
        small[j : j + 1, :] = gb[0:1, ls]
        small[3 + j : 4 + j, :] = gb[8:9, ls]
        small[6 + j : 7 + j, :] = fsum[0:1, ls]
        small[9 + j : 10 + j, :] = fsum[0:1, C + 128 * j : C + 128 * j + 128]
    gate_lane = lane[0:1] < 4
    small[K_ROW : K_ROW + 1, :] = jnp.where(gate_lane, fsum[0:1, C2:], small[K_ROW : K_ROW + 1, :])
    mr, sr = block_rows(mod_len), block_rows(small_len)
    send_slots(gx, gy, pos, flat, mod_len, 0, own, oth)
    for i in range(gy // 2):
        for j in range(gx):
            for c, dst in enumerate((own, oth)):
                block = small[pl.ds(first_row(small_len, device_at(pos, gy, i, j, c)), sr), :]
                pad = own.shape[2] - mr - sr
                if pad:
                    block = jnp.concatenate([block, jnp.zeros((pad, 128), f32)], 0)
                dst[i, j, mr:, :] = block.astype(bf16)


def kernel_add(n_in, *refs):
    for k, o in enumerate(refs[n_in:]):
        total = None
        for ref in refs[:n_in]:
            v = ref[k].astype(f32)
            total = v if total is None else total + v
        o[...] = total.astype(o.dtype)


def kernel_cut(cuts, *refs):
    outs = refs[-len(cuts) :]
    for o, (first, n) in zip(outs, cuts):
        total = None
        for ref in refs[: -len(cuts)]:
            v = ref[first : first + n, :].astype(f32)
            total = v if total is None else total + v
        o[...] = total


def full(shape):
    return pl.BlockSpec(shape, lambda *i, n=len(shape): (0,) * n)


def rows(n, width):
    return pl.BlockSpec((n, width), lambda i: (i, 0))


def smem():
    return pl.BlockSpec(memory_space=pltpu.SMEM)


def sds(shape, dtype):
    return jax.ShapeDtypeStruct(shape, dtype)


def call(kernel, name, grid, ins, outs, scratch, mib, micros):
    return pl.pallas_call(
        kernel,
        grid=grid,
        in_specs=[s for _, s in ins],
        out_shape=[o for o, _ in outs],
        out_specs=[s for _, s in outs],
        scratch_shapes=[pltpu.VMEM(shape, dtype) for shape, dtype in scratch],
        compiler_params=pltpu.CompilerParams(vmem_limit_bytes=mib * 2**20),
        cost_estimate=pl.CostEstimate(flops=int(micros * 1e9), bytes_accessed=int(micros * 1e6), transcendentals=0),
        name=name,
    )(*[a for a, _ in ins])


def whole(*arrays):
    return [(a, full(a.shape)) for a in arrays]


def by_rows(n, *arrays):
    return [(a, rows(n, a.shape[1])) for a in arrays]


def native_rows(slots):
    return ((C // 128, GH * GW * slots, 128), f32)


def prep(tokens):
    slots = tokens.shape[2]
    n = slots * IMG
    outs = [(sds((n, w), t), rows(IMG, w)) for w, t in ((C, bf16), (C, bf16), (128, f32))]
    return call(kernel_prep, "prep", (slots,), whole(tokens), outs, [native_rows(slots), ((IMG, C), f32)], 60, 6)


def upstream(counts, cotangent):
    slots = cotangent.shape[2]
    ins = [(counts, smem())] + whole(cotangent)
    outs = [(sds((slots * IMG, C), bf16), rows(IMG, C))]
    return call(kernel_upstream, "upstream", (slots,), ins, outs, [native_rows(slots), ((IMG, C), f32)], 60, 5)[0]


def forward(xrow, stat, bucket, wf, vec, kcat):
    con = constants()
    pairs = xrow.shape[0] // PAIR
    n = pairs * PAIR
    outs = [
        (sds((n, C), f32), rows(PAIR, C)),
        (sds((n, GATES), f32), rows(PAIR, GATES)),
        (sds((n, C), bf16), rows(PAIR, C)),
        (sds((pairs * 3 * IMG, C2), bf16), rows(3 * IMG, C2)),
        (sds((pairs * 3 * IMG, C2), bf16), rows(3 * IMG, C2)),
        (sds((pairs * 3 * SR, C2), bf16), rows(3 * SR, C2)),
        (sds((pairs * 8, C2), f32), rows(8, C2)),
    ]
    mats = [jnp.asarray(con[k]) for k in ("es", "fe", "fo", "ge", "go")]
    ins = [(bucket, smem())] + by_rows(PAIR, xrow, stat) + whole(wf, vec, kcat, *mats)
    scratch = [
        ((6, SR, C), f32), ((PAIR, C), bf16), ((PAIR, C), f32), ((3 * HALF, C2), bf16), ((3 * HALF, C2), bf16), ((AR, C2), f32), ((BR, C2), f32),
        ((HALF, C2), f32), ((HALF, C2), f32), ((3 * AR, C2), bf16), ((3 * BR, C2), bf16), ((PAIR, C), f32),
        ((4, PAIR, 128), f32),
    ]
    return call(kernel_forward, "focal_forward", (pairs,), ins, outs, scratch, 60, 32)


def middle(gx, gy, pos, xrow, up, mixed, q, wh, wp, w1, w2, vec, bm1, mlp_len):
    n = xrow.shape[0]
    outs = [
        (sds((n, C), f32), rows(BROWS, C)),
        (sds((n, C), f32), rows(BROWS, C)),
        (sds((n, C), bf16), rows(BROWS, C)),
        (sds((n, C), f32), rows(BROWS, C)),
    ]
    slots = (gy // 2, gx, block_rows(mlp_len), 128)
    outs += [(sds(slots, bf16), full(slots))] * 2
    outs += [(sds(s, f32), full(s)) for s in ((C, C), (C, C), (8, C), (8, HID))]
    ins = [(pos, smem())] + by_rows(BROWS, xrow, up, mixed, q) + whole(wh, wp, w1, w2, vec, bm1)
    blk = (BROWS, C)
    scratch = [
        (blk, f32), (blk, bf16), (blk, f32), (blk, f32), (blk, bf16), (blk, bf16), (blk, f32), (blk, f32),
        ((BROWS, HCHUNK), bf16), ((BROWS, HCHUNK), bf16), ((BROWS, HCHUNK), f32), ((8, 8, C), f32), ((8, HID), f32),
        ((C, HID), f32), ((HID, C), f32), ((span(mlp_len, gx * gy), 128), f32),
    ]
    kernel = functools.partial(kernel_middle, gx, gy, mlp_len)
    return call(kernel, "middle", (n // BROWS,), ins, outs, scratch, 62, 42)


def backward(gx, gy, pos, bucket, nb, dq, dmix, gates, z, g, spec, mean, kcat, wf, vec, sums, bsum, gwh, gwp, mod_len, small_len):
    con = constants()
    ndev = gx * gy
    pairs = nb.shape[0] // PAIR
    mats = [jnp.asarray(con["es"]), jnp.asarray(con["weights"]), jnp.asarray(con["fe"][:, :HALF]), jnp.asarray(con["fo"][:, :HALF])]
    mats += [jnp.asarray(con["ge"][:, :AR]), jnp.asarray(con["go"][:, :BR])]
    slots = (gy // 2, gx, -(-(block_rows(mod_len) + block_rows(small_len)) // 16) * 16, 128)
    outs = [(sds((nb.shape[0], MERGED), bf16), rows(PAIR, MERGED))] + [(sds(slots, bf16), full(slots))] * 2
    ins = [(bucket, smem()), (pos, smem())] + by_rows(PAIR, nb, dq, dmix, gates) + by_rows(3 * IMG, z, g) + by_rows(3 * SR, spec)
    ins += by_rows(8, mean) + whole(kcat, wf, vec, sums, bsum, gwh, gwp, *mats)
    small_rows = -(-max(span(small_len, ndev), END_ROW + 2) // 8) * 8
    scratch = [
        ((C, MERGED), f32), ((8, MERGED), f32), ((16, C), f32), ((3, TAPS, C), f32), ((6, SR, C), f32),
        ((HALF, C2), bf16), ((HALF, C2), bf16), ((AR, C2), f32), ((BR, C2), f32), ((HALF, C2), f32), ((HALF, C2), f32),
        ((AR, C2), bf16), ((BR, C2), bf16), ((6, SR, C), f32), ((8, MERGED), f32), ((4, PAIR, 128), f32),
        ((max(span(mod_len, ndev), STRIDE * 16 + 8), 128), f32), ((small_rows, 128), f32), ((small_rows, 128), f32),
        ((MERGED // 128, PERIOD * 16, 128), f32),
    ]
    kernel = functools.partial(kernel_backward, gx, gy, mod_len, small_len)
    return call(kernel, "focal_backward", (pairs,), ins, outs, scratch, 62, 28)


def tail(shape, dmer, wf, xrow, stat, dmid, vec):
    slots = shape[2]
    ins = by_rows(PAIR, dmer) + whole(wf) + by_rows(PAIR, xrow, stat, dmid) + whole(vec)
    return call(kernel_tail, "tail", (slots // 2,), ins, [(sds(shape, f32), full(shape))], [((PAIR, C), f32), native_rows(slots)], 60, 8)[0]


def out_tokens(shape, counts, out_rows):
    ins = [(counts, smem())] + whole(out_rows)
    return call(kernel_out, "out_tokens", (), ins, [(sds(shape, bf16), full(shape))], [native_rows(shape[2])], 60, 5)[0]


def span(length, ndev):
    return ((ndev - 1) * length) // 1024 * 8 + block_rows(length)


def unpack_mod(gx, gy, pos, own, oth, mod_len, small_len):
    ndev = gx * gy
    outs = [sds((C, MERGED), bf16), sds((C, C), bf16), sds((C, C), bf16), sds((VROWS, C), f32), sds((8, HID), f32), sds((3, 2 * TAPS, C), bf16)]
    top = STRIDE * 15 + STRIDE + 8
    flat_rows = max(span(mod_len, ndev), top)
    small_rows = max(span(small_len, ndev), END_ROW + 26)
    scratch = [((flat_rows, 128), f32), ((small_rows + 8, 128), f32), ((small_rows, 128), f32), ((MERGED // 128, PERIOD * 16, 128), f32)]
    kernel = functools.partial(kernel_unpack_mod, gx, gy, mod_len, small_len)
    return call(kernel, "unpack_mod", (), [(pos, smem())] + whole(own, oth), [(o, full(o.shape)) for o in outs], scratch, 60, 4)


def unpack_mlp(gx, gy, pos, blocks, mlp_len):
    outs = [sds((C, HID), bf16), sds((HID, C), bf16)]
    kernel = functools.partial(kernel_unpack_mlp, gx, gy, mlp_len)
    scratch = [((span(mlp_len, gx * gy), 128), f32)]
    return call(kernel, "unpack_mlp", (), [(pos, smem())] + whole(*blocks), [(o, full(o.shape)) for o in outs], scratch, 60, 3)


def add(arrays, outs, name):
    return call(functools.partial(kernel_add, len(arrays)), name, (), whole(*arrays), [(o, full(o.shape)) for o in outs], [], 24, 2)


def swap(x, mask, ndev):
    return lax.ppermute(x, AXES, [(k, k ^ mask) for k in range(ndev)])


def around(x, step, count, ndev):
    return [x] + [swap(x, step * k, ndev) for k in range(1, count)]


def after(values):
    return lax.optimization_barrier(values)


def travel(parts, step, ndev):
    return [parts[0]] + [swap(p, step * k, ndev) for k, p in enumerate(parts) if k]


def sum_core(own, oth, gx, gy, name):
    got = swap(oth, 1, gx * gy)
    return add([own, got], [sds(own.shape[1:], f32 if k == 0 else bf16) for k in range(gy // 2)], name + "_sum_core")


def sum_plane(parts, gx, name):
    shape = parts[0].shape[1:]
    return add(parts, [sds(shape, f32 if k == 0 else bf16) for k in range(gx)], name + "_sum_plane")


def sum_line(parts, cuts, name):
    outs = [(sds((n, 128), f32), full((n, 128))) for _, n in cuts]
    return call(functools.partial(kernel_cut, cuts), name + "_sum_line", (), whole(*parts), outs, [], 24, 2)


def local(gx, gy, tokens, bucket, counts, mod_weights, mlp_weights, small_params, cotangent):
    ndev = gx * gy
    gxi, gyi = lax.axis_index("gx"), lax.axis_index("gy")
    device = gxi * gy + gyi
    pos = jnp.stack([gxi, gyi]).astype(jnp.int32)
    mod_len, small_len, mlp_len = mod_weights.shape[0], small_params.shape[0], mlp_weights.shape[0]
    mr, sr = block_rows(mod_len), block_rows(small_len)

    blocks = [place(mod_weights, device), place(small_params, device)]
    pad = -(mr + sr) % 16
    if pad:
        blocks.append(jnp.zeros((pad, 128), bf16))
    cut = mr + sr + pad
    line = around(jnp.concatenate(blocks + [place(mlp_weights, device)], 0), gy, gx, ndev)
    native, back = (1, 2, 0, 3), (2, 0, 1, 3)
    shape = (GH, GW) + tokens.shape[:1] + (C,)
    prepared = prep(jnp.transpose(tokens, native))
    line, prepared = after((line, prepared))
    xrow, nb, stat = prepared
    plane = around(jnp.stack([v[:cut] for v in line]), 2, gy // 2, ndev)
    mlp_line = jnp.stack([v[cut:] for v in line])
    mlp_other = swap(mlp_line, 1, ndev)
    up = upstream(counts, jnp.transpose(cotangent, native))
    plane, mlp_other, up = after((plane, mlp_other, up))
    plane = jnp.stack(plane)
    other = swap(plane, 1, ndev)
    mlp_both = jnp.stack([mlp_line, mlp_other])
    other, mlp_both = after((other, mlp_both))
    mlp_blocks = around(mlp_both, 2, gy // 2, ndev)

    wf, wh, wp, vec, bm1, kcat = unpack_mod(gx, gy, pos, plane, other, mod_len, small_len)
    q, gates, mixed, z, g, spec, mean = forward(xrow, stat, bucket, wf, vec, kcat)
    mlp_blocks, mixed = after((mlp_blocks, mixed))
    w1, w2 = unpack_mlp(gx, gy, pos, mlp_blocks, mlp_len)
    dmid, out_rows, dq, dmix, own, oth, gwh, gwp, sums, bsum = middle(
        gx, gy, pos, xrow, up, mixed, q, wh, wp, w1, w2, vec, bm1, mlp_len
    )
    parts = sum_core(own, oth, gx, gy, "mlp")
    parts, dmix = after((parts, dmix))
    mlp_plane = travel(parts, 2, ndev)
    dmer, own, oth = backward(
        gx, gy, pos, bucket, nb, dq, dmix, gates, z, g, spec, mean, kcat, wf, vec, sums, bsum, gwh, gwp, mod_len, small_len
    )
    mlp_plane, own, oth = after((mlp_plane, own, oth))
    parts = sum_plane(mlp_plane, gx, "mlp")
    mod_parts = sum_core(own, oth, gx, gy, "mod")
    mlp_line = travel(parts, gy, ndev)
    mod_plane = travel(mod_parts, 2, ndev)
    gtok = tail(shape, dmer, wf, xrow, stat, dmid, vec)
    mod_plane, mlp_line, gtok, out_rows = after((mod_plane, mlp_line, gtok, out_rows))
    mod_line = travel(sum_plane(mod_plane, gx, "mod"), gy, ndev)
    grad_mlp = take(sum_line(mlp_line, [(0, mlp_line[0].shape[0])], "mlp")[0], mlp_len, device)
    out = out_tokens(shape, counts, out_rows)
    mod_line, out, grad_mlp = after((mod_line, out, grad_mlp))
    total_mod, total_small = sum_line(mod_line, [(0, mr), (mr, sr)], "mod")
    grad_mod = take(total_mod, mod_len, device)
    grad_small = take(total_small, small_len, device)
    return jnp.transpose(out, back), jnp.transpose(gtok, back), grad_mod, grad_mlp, grad_small


def solution(mesh):
    images = P(AXES, None, None, None)
    flat = P(AXES)
    return jax.shard_map(
        functools.partial(local, mesh.shape["gx"], mesh.shape["gy"]),
        mesh=mesh,
        in_specs=(images, flat, flat, flat, flat, flat, images),
        out_specs=(images, images, flat, flat, flat),
        check_vma=False,
    )
```

profile of v0, /device:TPU:0, one launch (start us, length us, event | category | flops | bytes accessed | tf_op | source)
XLA Modules:
  0.0 179.2 jit_solution(18411291042417318323)
XLA Ops:
  0.7 0.9 dynamic_update_slice.7
  1.6 1.1 dynamic_update_slice.6
  2.8 1.0 pad_maximum_fusion.4
  3.8 5.1 %collective-permute-start.2 = (bf16[480,128]{1,0:T(8,128)(2,1)S(1)}, bf16[480,128]{1,0:T(8,128)(2,1)S(1)}, u32[]{:S(2)}, u32[]{:S(2)}) collective-permute-start(bf16[480,128]{1,0:T(8,128)(2,1)S(1)} %pad_maximum_fusion.4), channel_id=1, source_target_pairs={{0,24},{1,25},{2,26},{3,27},{4,28},{5,29},{6,30},{7,31},{8,16},{9,... | collective-permute-start | bytes 368648 | tf_op jit(solution)/shard_map/ppermute | solution.py:1058
  8.9 0.6 collective-permute-start
  9.5 6.2 %prep.1 = (bf16[2304,384]{1,0:T(8,128)(2,1)}, bf16[2304,384]{1,0:T(8,128)(2,1)}, f32[2304,128]{1,0:T(8,128)}) custom-call(bf16[14,20,8,384]{3,2,1,0:T(8,128)(2,1)} %bitcast.45), custom_call_target="tpu_custom_call" | custom-call | flops 6000000000 | bytes 6000000 | tf_op jit(solution)/shard_map/prep/pallas_call | solution.py:914
  16.4 2.9 %collective-permute-done.1 = bf16[480,128]{1,0:T(8,128)(2,1)S(1)} collective-permute-done((bf16[480,128]{1,0:T(8,128)(2,1)S(1)}, bf16[480,128]{1,0:T(8,128)(2,1)S(1)}, u32[]{:S(2)}, u32[]{:S(2)}) %collective-permute-start.1) | collective-permute-done | bytes 122912 | tf_op jit(solution)/shard_map/ppermute | solution.py:1058
  19.4 2.5 %collective-permute-start.5 = (bf16[4,192,128]{2,1,0:T(8,128)(2,1)S(1)}, bf16[4,192,128]{2,1,0:T(8,128)(2,1)S(1)}, u32[]{:S(2)}, u32[]{:S(2)}) collective-permute-start(bf16[4,192,128]{2,1,0:T(8,128)(2,1)S(1)} %pad_maximum_fusion.3), channel_id=1, source_target_pairs={{0,6},{1,7},{2,4},{3,5},{4,2},{5,3},{6,0},{7,1},{8,14},{9,15},{10,... | collective-permute-start | bytes 589832 | tf_op jit(solution)/shard_map/ppermute | solution.py:1058
  21.9 0.5 collective-permute-start.4
  22.4 0.5 collective-permute-start.3
  23.1 5.2 %upstream.1.up = bf16[2304,384]{1,0:T(8,128)(2,1)} custom-call(s32[1]{0:T(128)S(6)} %copy.24.counts, bf16[14,20,8,384]{3,2,1,0:T(8,128)(2,1)} %bitcast.46), custom_call_target="tpu_custom_call" | custom-call | flops 5000000000 | bytes 5000000 | tf_op jit(solution)/shard_map/upstream/pallas_call | solution.py:914
  28.2 2.3 %collective-permute-done.4 = bf16[4,192,128]{2,1,0:T(8,128)(2,1)S(1)} collective-permute-done((bf16[4,192,128]{2,1,0:T(8,128)(2,1)S(1)}, bf16[4,192,128]{2,1,0:T(8,128)(2,1)S(1)}, u32[]{:S(2)}, u32[]{:S(2)}) %collective-permute-start.4) | collective-permute-done | bytes 196640 | tf_op jit(solution)/shard_map/ppermute | solution.py:1058
  30.5 0.1 collective-permute-done.3
  30.8 0.8 pad_add_fusion.pos
  31.7 1.4 collective-permute-done.7.oth
  33.1 1.6 collective-permute-start.10
  34.7 1.3 collective-permute-start.9
  36.0 0.5 collective-permute-start.8
  36.6 4.7 %unpack_mod.1 = (bf16[384,896]{1,0:T(8,128)(2,1)}, bf16[384,384]{1,0:T(8,128)(2,1)}, bf16[384,384]{1,0:T(8,128)(2,1)}, f32[16,384]{1,0:T(8,128)}, f32[8,1536]{1,0:T(8,128)}, /*index=5*/bf16[3,128,384]{2,1,0:T(8,128)(2,1)}) custom-call(s32[2]{0:T(128)} %pad_add_fusion.pos, bf16[4,4,192,128]{3,2,1,0:T(8,128)(2,1)} %copy-done.4, bf16[4,4,192,128]{3,2,1,0:T(8,128)(2,1)} %copy-done.6), custom_call_target="tpu_custom_call" | custom-call | flops 4000000000 | bytes 4000000 | tf_op jit(solution)/shard_map/unpack_mod/pallas_call | solution.py:914
  41.3 24.8 %focal_forward.1 = (f32[2304,384]{1,0:T(8,128)}, f32[2304,128]{1,0:T(8,128)}, bf16[2304,384]{1,0:T(8,128)(2,1)}, bf16[3456,768]{1,0:T(8,128)(2,1)}, bf16[3456,76...) custom-call(s32[8]{0:T(128)} %bucket.3, bf16[2304,384]{1,0:T(8,128)(2,1)} %get-tuple-element.104.x_ref, ...), custom_call_target="tpu_custom_call" | custom-call | flops 32000000000 | bytes 32000000 | tf_op jit(solution)/shard_map/focal_forward/pallas_call | solution.py:914
  66.1 0.7 copy-done.7
  66.9 0.3 copy-done.8
  67.1 0.2 copy-done.9
  67.3 3.8 %unpack_mlp.1 = (bf16[384,1536]{1,0:T(8,128)(2,1)}, bf16[1536,384]{1,0:T(8,128)(2,1)}) custom-call(s32[2]{0:T(128)} %pad_add_fusion.pos, bf16[2,4,288,128]{3,2,1,0:T(8,128)(2,1)} %copy-done.5, bf16[2,4,288,128]{3,2,1,0:T(8,128)(2,1)} %copy-done.9, bf16[2,4,288,128]{3,2,1,0:T(8,128)(2,1)} %copy-done.8, bf16[2,4,288,128]{3,2,1,0:T(8,128)(2,1)} %copy-done.7), custom_call_target="tpu_custom_call" | custom-call | flops 3000000000 | bytes 3000000 | tf_op jit(solution)/shard_map/unpack_mlp/pallas_call | solution.py:914
  71.1 41.6 %middle.1 = (f32[2304,384]{1,0:T(8,128)}, f32[2304,384]{1,0:T(8,128)}, bf16[2304,384]{1,0:T(8,128)(2,1)}, f32[2304,384]{1,0:T(8,128)}, bf16[4,4,288,128]{3,2,1,0...) custom-call(s32[2]{0:T(128)} %pad_add_fusion.pos, ...), custom_call_target="tpu_custom_call" | custom-call | flops 41999998976 | bytes 42000000 | tf_op jit(solution)/shard_map/middle/pallas_call | solution.py:914
  112.8 3.0 %collective-permute-done.11.refs_1_ = bf16[4,4,288,128]{3,2,1,0:T(8,128)(2,1)S(1)} collective-permute-done((bf16[4,4,288,128]{3,2,1,0:T(8,128)(2,1)}, bf16[4,4,288,128]{3,2,1,0:T(8,128)(2,1)S(1)}, u32[]{:S(2)}, u32[]{:S(2)}) %collective-permute-start.11) | collective-permute-done | bytes 1179680 | tf_op jit(solution)/shard_map/ppermute | solution.py:1058
  115.9 1.3 copy-done
  117.1 0.3 mlp_sum_core.1
  117.4 0.8 copy-done.1
  118.2 1.5 collective-permute-start.12
  119.7 0.7 collective-permute-start.13
  120.5 1.3 collective-permute-start.14
  121.7 27.4 %focal_backward.1 = (bf16[2304,896]{1,0:T(8,128)(2,1)}, bf16[4,4,192,128]{3,2,1,0:T(8,128)(2,1)}, bf16[4,4,192,128]{3,2,1,0:T(8,128)(2,1)}) custom-call(s32[8]{0:T(128)} %bucket.3, s32[2]{0:T(128)} %pad_add_fusion.pos, bf16[2304,384]{1,0:T(8,128)(2,1)} %get-tuple-element.144.nb_ref, bf16[2304,384]{1,0:T(8,128)(2,1)} %get-tuple-element.145.dq_ref, ...), custom_call_target="tpu_custom_call" | custom-call | flops 28000000000 | bytes 28000000 | tf_op jit(solution)/shard_map/focal_backward/pallas_call | solution.py:914
  149.2 1.1 copy-done.2
  150.3 0.1 mlp_sum_plane.1
  150.5 2.9 %collective-permute-start.20 = (bf16[288,128]{1,0:T(8,128)(2,1)S(1)}, bf16[288,128]{1,0:T(8,128)(2,1)S(1)}, u32[]{:S(2)}, u32[]{:S(2)}) collective-permute-start(bf16[288,128]{1,0:T(8,128)(2,1)S(1)} %get-tuple-element.170), channel_id=1, source_target_pairs={{0,16},{1,17},{2,18},{3,19},{4,20},{5,21},{6,22},{7,23},{8,24},{9,... | collective-permute-start | bytes 221192 | tf_op jit(solution)/shard_map/ppermute | solution.py:1058
  153.4 1.5 collective-permute-start.21
  154.9 0.2 mod_sum_core.1
  155.1 1.6 collective-permute-start.16
  156.6 0.7 collective-permute-start.17
  157.4 1.3 collective-permute-start.18
  158.6 9.4 %tail.1 = f32[14,20,8,384]{3,2,1,0:T(8,128)} custom-call(bf16[2304,896]{1,0:T(8,128)(2,1)} %get-tuple-element.172.dmer, bf16[384,896]{1,0:T(8,128)(2,1)} %get-tuple-element.118.wf, bf16[2304,384]{1,0:T(8,128)(2,1)} %get-tuple-element.104.x_ref, f32[2304,128]{1,0:T(8,128)} %get-tuple-element.116.stat, f32[2304,384]{1,0:T(8,128)} %get-tuple-element.173.dmid, ...), custom_call_target="tpu_custom_call" | custom-call | flops 8000000000 | bytes 8000000 | tf_op jit(solution)/shard_map/tail/pallas_call | solution.py:914
  168.2 2.9 %collective-permute-start.23 = (bf16[192,128]{1,0:T(8,128)(2,1)S(1)}, bf16[192,128]{1,0:T(8,128)(2,1)S(1)}, u32[]{:S(2)}, u32[]{:S(2)}) collective-permute-start(bf16[192,128]{1,0:T(8,128)(2,1)S(1)} %get-tuple-element.181), channel_id=1, source_target_pairs={{0,16},{1,17},{2,18},{3,19},{4,20},{5,21},{6,22},{7,23},{8,24},{9,... | collective-permute-start | bytes 147464 | tf_op jit(solution)/shard_map/ppermute | solution.py:1058
  171.1 1.5 collective-permute-start.24
  172.6 4.4 %out_tokens.1 = bf16[14,20,8,384]{3,2,1,0:T(8,128)(2,1)} custom-call(s32[1]{0:T(128)S(6)} %copy.24.counts, f32[2304,384]{1,0:T(8,128)} %get-tuple-element.183.rows_ref), custom_call_target="tpu_custom_call" | custom-call | flops 5000000000 | bytes 5000000 | tf_op jit(solution)/shard_map/out_tokens/pallas_call | solution.py:914
  177.0 0.7 mlp_sum_line.1
  177.8 0.7 dynamic_slice.6
  178.5 0.7 dynamic_slice.7
  (55 shorter events, 1.0 us)
Async XLA Ops:
  3.8 12.6 %collective-permute-start.2 = (bf16[480,128]{1,0:T(8,128)(2,1)S(1)}, bf16[480,128]{1,0:T(8,128)(2,1)S(1)}, u32[]{:S(2)}, u32[]{:S(2)}) collective-permute-start(bf16[480,128]{1,0:T(8,128)(2,1)S(1)} %pad_maximum_fusion.4), channel_id=1, source_target_pairs={{0,24},{1,25},{2,26},{3,27},{4,28},{5,29},{6,30},{7,31},{8,16},{9,... | collective-permute-start | bytes 368648 | tf_op jit(solution)/shard_map/ppermute | solution.py:1058
  8.9 10.4 %collective-permute-start.1 = (bf16[480,128]{1,0:T(8,128)(2,1)S(1)}, bf16[480,128]{1,0:T(8,128)(2,1)S(1)}, u32[]{:S(2)}, u32[]{:S(2)}) collective-permute-start(bf16[480,128]{1,0:T(8,128)(2,1)S(1)} %pad_maximum_fusion.4), channel_id=1, source_target_pairs={{0,16},{1,17},{2,18},{3,19},{4,20},{5,21},{6,22},{7,23},{8,24},{9,... | collective-permute-start | bytes 368648 | tf_op jit(solution)/shard_map/ppermute | solution.py:1058
  8.9 10.4 %collective-permute-start = (bf16[480,128]{1,0:T(8,128)(2,1)S(1)}, bf16[480,128]{1,0:T(8,128)(2,1)S(1)}, u32[]{:S(2)}, u32[]{:S(2)}) collective-permute-start(bf16[480,128]{1,0:T(8,128)(2,1)S(1)} %pad_maximum_fusion.4), channel_id=1, source_target_pairs={{0,8},{1,9},{2,10},{3,11},{4,12},{5,13},{6,14},{7,15},{8,0},{9,1},... | collective-permute-start | bytes 368648 | tf_op jit(solution)/shard_map/ppermute | solution.py:1058
  19.4 8.8 %collective-permute-start.5 = (bf16[4,192,128]{2,1,0:T(8,128)(2,1)S(1)}, bf16[4,192,128]{2,1,0:T(8,128)(2,1)S(1)}, u32[]{:S(2)}, u32[]{:S(2)}) collective-permute-start(bf16[4,192,128]{2,1,0:T(8,128)(2,1)S(1)} %pad_maximum_fusion.3), channel_id=1, source_target_pairs={{0,6},{1,7},{2,4},{3,5},{4,2},{5,3},{6,0},{7,1},{8,14},{9,15},{10,... | collective-permute-start | bytes 589832 | tf_op jit(solution)/shard_map/ppermute | solution.py:1058
  21.9 8.6 %collective-permute-start.4 = (bf16[4,192,128]{2,1,0:T(8,128)(2,1)S(1)}, bf16[4,192,128]{2,1,0:T(8,128)(2,1)S(1)}, u32[]{:S(2)}, u32[]{:S(2)}) collective-permute-start(bf16[4,192,128]{2,1,0:T(8,128)(2,1)S(1)} %pad_maximum_fusion.3), channel_id=1, source_target_pairs={{0,4},{1,5},{2,6},{3,7},{4,0},{5,1},{6,2},{7,3},{8,12},{9,13},{10,... | collective-permute-start | bytes 589832 | tf_op jit(solution)/shard_map/ppermute | solution.py:1058
  22.4 8.2 %collective-permute-start.3 = (bf16[4,192,128]{2,1,0:T(8,128)(2,1)S(1)}, bf16[4,192,128]{2,1,0:T(8,128)(2,1)S(1)}, u32[]{:S(2)}, u32[]{:S(2)}) collective-permute-start(bf16[4,192,128]{2,1,0:T(8,128)(2,1)S(1)} %pad_maximum_fusion.3), channel_id=1, source_target_pairs={{0,2},{1,3},{2,0},{3,1},{4,6},{5,7},{6,4},{7,5},{8,10},{9,11},{10,... | collective-permute-start | bytes 589832 | tf_op jit(solution)/shard_map/ppermute | solution.py:1058
  23.0 7.6 %collective-permute-start.6 = (bf16[4,288,128]{2,1,0:T(8,128)(2,1)S(1)}, bf16[4,288,128]{2,1,0:T(8,128)(2,1)S(1)}, u32[]{:S(2)}, u32[]{:S(2)}) collective-permute-start(bf16[4,288,128]{2,1,0:T(8,128)(2,1)S(1)} %get-tuple-element.198), channel_id=1, source_target_pairs={{0,1},{1,0},{2,3},{3,2},{4,5},{5,4},{6,7},{7,6},{8,9},{9,8},{10,11... | collective-permute-start | bytes 884744 | tf_op jit(solution)/shard_map/ppermute | solution.py:1058
  30.7 5.9 %copy-start.4 = (bf16[4,4,192,128]{3,2,1,0:T(8,128)(2,1)}, bf16[4,4,192,128]{3,2,1,0:T(8,128)(2,1)S(1)}, u32[]{:S(2)}) copy-start(bf16[4,4,192,128]{3,2,1,0:T(8,128)(2,1)S(1)} %pad_maximum_fusion.own) | copy-start | bytes 2359300
  30.7 2.4 %collective-permute-start.7 = (bf16[4,4,192,128]{3,2,1,0:T(8,128)(2,1)S(1)}, bf16[4,4,192,128]{3,2,1,0:T(8,128)(2,1)S(1)}, u32[]{:S(2)}, u32[]{:S(2)}) collective-permute-start(bf16[4,4,192,128]{3,2,1,0:T(8,128)(2,1)S(1)} %pad_maximum_fusion.own), channel_id=1, source_target_pairs={{0,1},{1,0},{2,3},{3,2},{4,5},{5,4},{6,7},{7,6},{8,9},{9,8},{10,11... | collective-permute-start | bytes 2359304 | tf_op jit(solution)/shard_map/ppermute | solution.py:1058
  31.7 9.6 %copy-start.5 = (bf16[2,4,288,128]{3,2,1,0:T(8,128)(2,1)}, bf16[2,4,288,128]{3,2,1,0:T(8,128)(2,1)S(1)}, u32[]{:S(2)}) copy-start(bf16[2,4,288,128]{3,2,1,0:T(8,128)(2,1)S(1)} %pad_maximum_fusion.1.refs_0_) | copy-start | bytes 1769476
  33.1 3.5 %copy-start.6 = (bf16[4,4,192,128]{3,2,1,0:T(8,128)(2,1)}, bf16[4,4,192,128]{3,2,1,0:T(8,128)(2,1)S(1)}, u32[]{:S(2)}) copy-start(bf16[4,4,192,128]{3,2,1,0:T(8,128)(2,1)S(1)} %collective-permute-done.7.oth) | copy-start | bytes 2359300
  33.1 33.0 %collective-permute-start.10 = (bf16[2,4,288,128]{3,2,1,0:T(8,128)(2,1)S(1)}, bf16[2,4,288,128]{3,2,1,0:T(8,128)(2,1)S(1)}, u32[]{:S(2)}, u32[]{:S(2)}) collective-permute-start(bf16[2,4,288,128]{3,2,1,0:T(8,128)(2,1)S(1)} %pad_maximum_fusion.1.refs_0_), channel_id=1, source_target_pairs={{0,6},{1,7},{2,4},{3,5},{4,2},{5,3},{6,0},{7,1},{8,14},{9,15},{10,... | collective-permute-start | bytes 1769480 | tf_op jit(solution)/shard_map/ppermute | solution.py:1058
  34.7 31.4 %collective-permute-start.9 = (bf16[2,4,288,128]{3,2,1,0:T(8,128)(2,1)S(1)}, bf16[2,4,288,128]{3,2,1,0:T(8,128)(2,1)S(1)}, u32[]{:S(2)}, u32[]{:S(2)}) collective-permute-start(bf16[2,4,288,128]{3,2,1,0:T(8,128)(2,1)S(1)} %pad_maximum_fusion.1.refs_0_), channel_id=1, source_target_pairs={{0,4},{1,5},{2,6},{3,7},{4,0},{5,1},{6,2},{7,3},{8,12},{9,13},{10,... | collective-permute-start | bytes 1769480 | tf_op jit(solution)/shard_map/ppermute | solution.py:1058
  36.0 30.1 %collective-permute-start.8 = (bf16[2,4,288,128]{3,2,1,0:T(8,128)(2,1)S(1)}, bf16[2,4,288,128]{3,2,1,0:T(8,128)(2,1)S(1)}, u32[]{:S(2)}, u32[]{:S(2)}) collective-permute-start(bf16[2,4,288,128]{3,2,1,0:T(8,128)(2,1)S(1)} %pad_maximum_fusion.1.refs_0_), channel_id=1, source_target_pairs={{0,2},{1,3},{2,0},{3,1},{4,6},{5,7},{6,4},{7,5},{8,10},{9,11},{10,... | collective-permute-start | bytes 1769480 | tf_op jit(solution)/shard_map/ppermute | solution.py:1058
  66.1 0.8 copy-start.7
  66.1 1.0 copy-start.8
  66.1 1.2 copy-start.9
  112.8 3.1 %collective-permute-start.11 = (bf16[4,4,288,128]{3,2,1,0:T(8,128)(2,1)}, bf16[4,4,288,128]{3,2,1,0:T(8,128)(2,1)S(1)}, u32[]{:S(2)}, u32[]{:S(2)}) collective-permute-start(bf16[4,4,288,128]{3,2,1,0:T(8,128)(2,1)} %get-tuple-element.134), channel_id=1, source_target_pairs={{0,1},{1,0},{2,3},{3,2},{4,5},{5,4},{6,7},{7,6},{8,9},{9,8},{10,11... | collective-permute-start | bytes 3538952 | tf_op jit(solution)/shard_map/ppermute | solution.py:1058
  115.9 1.3 copy-start
  117.4 0.8 copy-start.1
  118.2 30.9 %collective-permute-start.12 = (bf16[4,288,128]{2,1,0:T(8,128)(2,1)S(1)}, bf16[4,288,128]{2,1,0:T(8,128)(2,1)S(1)}, u32[]{:S(2)}, u32[]{:S(2)}) collective-permute-start(bf16[4,288,128]{2,1,0:T(8,128)(2,1)S(1)} %get-tuple-element.141), channel_id=1, source_target_pairs={{0,2},{1,3},{2,0},{3,1},{4,6},{5,7},{6,4},{7,5},{8,10},{9,11},{10,... | collective-permute-start | bytes 884744 | tf_op jit(solution)/shard_map/ppermute | solution.py:1058
  119.7 29.4 %collective-permute-start.13 = (bf16[4,288,128]{2,1,0:T(8,128)(2,1)S(1)}, bf16[4,288,128]{2,1,0:T(8,128)(2,1)S(1)}, u32[]{:S(2)}, u32[]{:S(2)}) collective-permute-start(bf16[4,288,128]{2,1,0:T(8,128)(2,1)S(1)} %get-tuple-element.142), channel_id=1, source_target_pairs={{0,4},{1,5},{2,6},{3,7},{4,0},{5,1},{6,2},{7,3},{8,12},{9,13},{10,... | collective-permute-start | bytes 884744 | tf_op jit(solution)/shard_map/ppermute | solution.py:1058
  120.5 28.7 %collective-permute-start.14 = (bf16[4,288,128]{2,1,0:T(8,128)(2,1)S(1)}, bf16[4,288,128]{2,1,0:T(8,128)(2,1)S(1)}, u32[]{:S(2)}, u32[]{:S(2)}) collective-permute-start(bf16[4,288,128]{2,1,0:T(8,128)(2,1)S(1)} %get-tuple-element.143), channel_id=1, source_target_pairs={{0,6},{1,7},{2,4},{3,5},{4,2},{5,3},{6,0},{7,1},{8,14},{9,15},{10,... | collective-permute-start | bytes 884744 | tf_op jit(solution)/shard_map/ppermute | solution.py:1058
  149.2 5.7 %collective-permute-start.15 = (bf16[4,4,192,128]{3,2,1,0:T(8,128)(2,1)}, bf16[4,4,192,128]{3,2,1,0:T(8,128)(2,1)S(1)}, u32[]{:S(2)}, u32[]{:S(2)}) collective-permute-start(bf16[4,4,192,128]{3,2,1,0:T(8,128)(2,1)} %get-tuple-element.159), channel_id=1, source_target_pairs={{0,1},{1,0},{2,3},{3,2},{4,5},{5,4},{6,7},{7,6},{8,9},{9,8},{10,11... | collective-permute-start | bytes 2359304 | tf_op jit(solution)/shard_map/ppermute | solution.py:1058
  149.2 1.1 copy-start.2
  150.3 4.6 %copy-start.3 = (bf16[4,4,192,128]{3,2,1,0:T(8,128)(2,1)S(1)}, bf16[4,4,192,128]{3,2,1,0:T(8,128)(2,1)}, u32[]{:S(2)}) copy-start(bf16[4,4,192,128]{3,2,1,0:T(8,128)(2,1)} %get-tuple-element.158.refs_0_) | copy-start | bytes 2359300
  150.4 6.9 %collective-permute-start.19 = (bf16[288,128]{1,0:T(8,128)(2,1)S(1)}, bf16[288,128]{1,0:T(8,128)(2,1)S(1)}, u32[]{:S(2)}, u32[]{:S(2)}) collective-permute-start(bf16[288,128]{1,0:T(8,128)(2,1)S(1)} %get-tuple-element.169), channel_id=1, source_target_pairs={{0,8},{1,9},{2,10},{3,11},{4,12},{5,13},{6,14},{7,15},{8,0},{9,1},... | collective-permute-start | bytes 221192 | tf_op jit(solution)/shard_map/ppermute | solution.py:1058
  150.5 17.5 %collective-permute-start.20 = (bf16[288,128]{1,0:T(8,128)(2,1)S(1)}, bf16[288,128]{1,0:T(8,128)(2,1)S(1)}, u32[]{:S(2)}, u32[]{:S(2)}) collective-permute-start(bf16[288,128]{1,0:T(8,128)(2,1)S(1)} %get-tuple-element.170), channel_id=1, source_target_pairs={{0,16},{1,17},{2,18},{3,19},{4,20},{5,21},{6,22},{7,23},{8,24},{9,... | collective-permute-start | bytes 221192 | tf_op jit(solution)/shard_map/ppermute | solution.py:1058
  153.4 14.6 %collective-permute-start.21 = (bf16[288,128]{1,0:T(8,128)(2,1)S(1)}, bf16[288,128]{1,0:T(8,128)(2,1)S(1)}, u32[]{:S(2)}, u32[]{:S(2)}) collective-permute-start(bf16[288,128]{1,0:T(8,128)(2,1)S(1)} %get-tuple-element.171), channel_id=1, source_target_pairs={{0,24},{1,25},{2,26},{3,27},{4,28},{5,29},{6,30},{7,31},{8,16},{9,... | collective-permute-start | bytes 221192 | tf_op jit(solution)/shard_map/ppermute | solution.py:1058
  155.1 13.0 %collective-permute-start.16 = (bf16[4,192,128]{2,1,0:T(8,128)(2,1)S(1)}, bf16[4,192,128]{2,1,0:T(8,128)(2,1)S(1)}, u32[]{:S(2)}, u32[]{:S(2)}) collective-permute-start(bf16[4,192,128]{2,1,0:T(8,128)(2,1)S(1)} %get-tuple-element.161), channel_id=1, source_target_pairs={{0,2},{1,3},{2,0},{3,1},{4,6},{5,7},{6,4},{7,5},{8,10},{9,11},{10,... | collective-permute-start | bytes 589832 | tf_op jit(solution)/shard_map/ppermute | solution.py:1058
  156.6 11.4 %collective-permute-start.17 = (bf16[4,192,128]{2,1,0:T(8,128)(2,1)S(1)}, bf16[4,192,128]{2,1,0:T(8,128)(2,1)S(1)}, u32[]{:S(2)}, u32[]{:S(2)}) collective-permute-start(bf16[4,192,128]{2,1,0:T(8,128)(2,1)S(1)} %get-tuple-element.162), channel_id=1, source_target_pairs={{0,4},{1,5},{2,6},{3,7},{4,0},{5,1},{6,2},{7,3},{8,12},{9,13},{10,... | collective-permute-start | bytes 589832 | tf_op jit(solution)/shard_map/ppermute | solution.py:1058
  157.4 10.7 %collective-permute-start.18 = (bf16[4,192,128]{2,1,0:T(8,128)(2,1)S(1)}, bf16[4,192,128]{2,1,0:T(8,128)(2,1)S(1)}, u32[]{:S(2)}, u32[]{:S(2)}) collective-permute-start(bf16[4,192,128]{2,1,0:T(8,128)(2,1)S(1)} %get-tuple-element.163), channel_id=1, source_target_pairs={{0,6},{1,7},{2,4},{3,5},{4,2},{5,3},{6,0},{7,1},{8,14},{9,15},{10,... | collective-permute-start | bytes 589832 | tf_op jit(solution)/shard_map/ppermute | solution.py:1058
  168.1 9.6 %collective-permute-start.22 = (bf16[192,128]{1,0:T(8,128)(2,1)S(1)}, bf16[192,128]{1,0:T(8,128)(2,1)S(1)}, u32[]{:S(2)}, u32[]{:S(2)}) collective-permute-start(bf16[192,128]{1,0:T(8,128)(2,1)S(1)} %get-tuple-element.180), channel_id=1, source_target_pairs={{0,8},{1,9},{2,10},{3,11},{4,12},{5,13},{6,14},{7,15},{8,0},{9,1},... | collective-permute-start | bytes 147464 | tf_op jit(solution)/shard_map/ppermute | solution.py:1058
  168.2 9.5 %collective-permute-start.23 = (bf16[192,128]{1,0:T(8,128)(2,1)S(1)}, bf16[192,128]{1,0:T(8,128)(2,1)S(1)}, u32[]{:S(2)}, u32[]{:S(2)}) collective-permute-start(bf16[192,128]{1,0:T(8,128)(2,1)S(1)} %get-tuple-element.181), channel_id=1, source_target_pairs={{0,16},{1,17},{2,18},{3,19},{4,20},{5,21},{6,22},{7,23},{8,24},{9,... | collective-permute-start | bytes 147464 | tf_op jit(solution)/shard_map/ppermute | solution.py:1058
  171.1 6.6 %collective-permute-start.24 = (bf16[192,128]{1,0:T(8,128)(2,1)S(1)}, bf16[192,128]{1,0:T(8,128)(2,1)S(1)}, u32[]{:S(2)}, u32[]{:S(2)}) collective-permute-start(bf16[192,128]{1,0:T(8,128)(2,1)S(1)} %get-tuple-element.182), channel_id=1, source_target_pairs={{0,24},{1,25},{2,26},{3,27},{4,28},{5,29},{6,30},{7,31},{8,16},{9,... | collective-permute-start | bytes 147464 | tf_op jit(solution)/shard_map/ppermute | solution.py:1058
where the time goes:
time: 180 us; the launch traced here: 179 us
  Pallas kernels  129 us (72%)
  starting transfers between devices  29 us (16%)
  waiting for transfers between devices  9.74 us (5%)
  local copies, waits for them, and re-layouts  7.91 us (4%)
  other arithmetic  2.08 us (1%)
    pallas_call x15, Pallas kernels, call(): pl.pallas_call(kernel, grid=grid, in_specs=[s for _, s in ins], out_shape...  129 us
    ppermute x25, starting transfers between devices, swap(): return lax.ppermute(x, AXES, [(k, k ^ mask) for k in range(ndev)])  29 us
    ppermute x25, waiting for transfers between devices, swap(): return lax.ppermute(x, AXES, [(k, k ^ mask) for k in range(ndev)])  9.74 us
    unnamed x20, local copies, waits for them, and re-layouts  4.38 us
  transfers between devices with their start and end apart: 25, of which 5 were waited for; matrix products, arithmetic and copies ran while one was open for 1% of the time, Pallas kernels for 46%

commit v1 on v0

--- a/solution.py
+++ b/solution.py
@@ -102,6 +102,7 @@
         ge=np.concatenate([_hi(ge), _lo(ge), _hi(ge)], 1),
         go=np.concatenate([_hi(go), _lo(go), _hi(go)], 1),
         es=np.stack(es),
+        est=np.stack([np.ascontiguousarray(e.T) for e in es]),
         weights=np.broadcast_to(weights, (SR, 128)).astype(np.float32),
     )
 
@@ -130,6 +131,17 @@
 
 def at(base, i, n=16):
     return slice(base + i * n, base + i * n + n)
+
+
+def weave(products, vector):
+    n, m = len(products), len(vector)
+    done = 0
+    for k, step in enumerate(products):
+        step()
+        upto = (k + 1) * m // n
+        for other in vector[done:upto]:
+            other()
+        done = upto
 
 
 def norm_stats(x):
@@ -169,11 +181,11 @@
             native[lt, line * y : line * (y + 1), :] = src[y, :, :, ls].astype(f32).reshape(line, 128)
 
 
-def image_rows(native, image, slot, slots, gain):
+def image_rows(native, image, first, slot, slots, gain):
     for h in (GH // 2 * GW, HALF + GH // 2 * GW):
-        image[h : h + 4, :] = jnp.zeros((4, C), f32)
+        image[first + h : first + h + 4, :] = jnp.zeros((4, C), f32)
     for y in range(GH):
-        a = grid_rows(0, y)
+        a = first + grid_rows(0, y)
         for lt in range(C // 128):
             v = native[lt, pl.ds(GW * slots * y + slot, GW, stride=slots), :]
             image[a : a + GW, 128 * lt : 128 * lt + 128] = v if gain is None else v * gain
@@ -186,9 +198,10 @@
     def _():
         from_native(x_ref, native)
 
-    image_rows(native, image, slot, x_ref.shape[2], None)
+    for im in range(2):
+        image_rows(native, image, im * IMG, slot * 2 + im, x_ref.shape[2], None)
     lane = lax.broadcasted_iota(jnp.int32, (32, 128), 1)
-    for i in range(IMG // 32):
+    for i in range(PAIR // 32):
         s = at(0, i, 32)
         x = image[s, :]
         xrow_o[s, :] = x.astype(bf16)
@@ -206,8 +219,10 @@
     def _():
         from_native(cot_ref, native)
 
-    image_rows(native, image, slot, cot_ref.shape[2], (slot < counts[0]).astype(f32))
-    for i in range(IMG // 32):
+    for im in range(2):
+        live = (slot * 2 + im < counts[0]).astype(f32)
+        image_rows(native, image, im * IMG, slot * 2 + im, cot_ref.shape[2], live)
+    for i in range(PAIR // 32):
         s = at(0, i, 32)
         up_o[s, :] = image[s, :].astype(bf16)
 
@@ -238,14 +253,15 @@
 
 
 def kernel_forward(
-    bucket, x_ref, stat, wf, vec, kcat, es, fe, fo, ge, go,
-    q_o, gates_o, mixed_o, z_o, g_o, spec_o, mean_o,
-    h_o, normed, ctx, ecat, ocat, s_a, s_b, s_e, s_o, yca, ycb, mix, wide,
+    gx, gy, mod_len, small_len, bucket, pos, x_ref, stat, own, oth, es, fe, fo, ge, go,
+    q_o, gates_o, mixed_o, z_o, g_o, spec_o, mean_o, wf, wh, wp, vec, bm1, kcat,
+    h_o, normed, ctx, ecat, ocat, s_a, s_b, s_e, s_o, yca, ycb, mix, wide, flat, small, moved, spread,
 ):
     step = pl.program_id(0)
 
     @pl.when(step == 0)
     def _():
+        unpack_mod(gx, gy, mod_len, small_len, pos, own, oth, wf, wh, wp, vec, bm1, kcat, flat, small, moved, spread)
         for lb in range(6):
             h_o[lb] = dot(es[lb], kcat[lb // 2])
 
@@ -363,21 +379,29 @@
 
 
 def kernel_middle(
-    gx, gy, mlp_len, pos, x_ref, up, mixed, q_ref, wh, wp, w1, w2, vec, bm1,
-    dmid_o, out_o, dq_o, dmix_o, own, oth, gwh, gwp, sums, bsum,
-    mod, modulated, branch, mid, second, dshr, shr, dsec, act, dexp, hid, vacc, bacc, gw1, gw2, flat,
+    gx, gy, mlp_len, pos, x_ref, up, mixed, q_ref, wh, wp, vec, bm1, *refs,
 ):
+    blocks = refs[: gy // 2]
+    (
+        dmid_o, out_o, dq_o, dmix_o, own, oth, gwh, gwp, sums, bsum,
+        mod, modulated, branch, mid, second, dshr, shr, dsec, act, dexp, hid, dact, dbr, dm2, dmod, vacc, bacc, gw1, gw2, flat,
+        w1, w2,
+    ) = refs[gy // 2 :]
     step = pl.program_id(0)
-
-    @pl.when(step == 0)
+    start = step == 0
+
+    @pl.when(start)
     def _():
-        for ref in (gw1, gw2, gwh, gwp, vacc, bacc):
+        for ref in (gwh, gwp, vacc, bacc):
             ref[...] = jnp.zeros_like(ref)
+        unpack_mlp(gx, gy, mlp_len, pos, blocks, w1, w2, flat)
+
+    def add_to(ref, rows_at, cols, v):
+        ref[rows_at, cols] = jnp.where(start, 0.0, ref[rows_at, cols]) + v
 
     g2, b2 = vec[V_G2 : V_G2 + 1, :], vec[V_B2 : V_B2 + 1, :]
     s1, s2 = vec[V_S1 : V_S1 + 1, :], vec[V_S2 : V_S2 + 1, :]
     bm2 = vec[V_BM2 : V_BM2 + 1, :]
-    zero = jnp.zeros((8, C), f32)
 
     mod[...] = dot(mixed[...], wh[...]) + vec[V_HB : V_HB + 1, :]
     for i in range(BROWS // 32):
@@ -392,38 +416,63 @@
         n, _ = norm_stats(middle)
         second[s, :] = (n * g2 + b2).astype(bf16)
 
-    for h in range(HID // HCHUNK):
-        hs = slice(h * HCHUNK, (h + 1) * HCHUNK)
-        hid[...] = dot(second[...], w1[:, hs]) + bm1[0:1, hs]
-        dact = dot_nt(dshr[...], w2[hs, :])
-        total = jnp.zeros((8, HCHUNK), f32)
-        for i in range(BROWS // 16):
+    chunks = [slice(h * HCHUNK, (h + 1) * HCHUNK) for h in range(HID // HCHUNK)]
+
+    def enter(h):
+        def into(t, k):
+            ls = slice(h * HCHUNK + 256 * t, h * HCHUNK + 256 * t + 256)
+            if k == 0:
+                hid[h % 2, :, 256 * t : 256 * t + 256] = dot(second[...], w1[:, ls]) + bm1[0:1, ls]
+            else:
+                dact[h % 2, :, 256 * t : 256 * t + 256] = dot_nt(dshr[...], w2[ls, :])
+
+        return [functools.partial(into, t, k) for t in range(HCHUNK // 256) for k in range(2)]
+
+    def gelu(h):
+        totals = []
+
+        def rows_of(i):
             s = at(0, i)
-            z, g = gelu_pair(hid[s, :])
-            act[s, :] = z.astype(bf16)
-            d = dact[s, :] * g
-            dexp[s, :] = d.astype(bf16)
-            total = total + sum8(d)
-        bacc[:, hs] += total
-        part = dot(act[...], w2[hs, :])
-        back = dot_nt(dexp[...], w1[:, hs])
-        if h == 0:
-            shr[...] = part
-            dsec[...] = back
-        else:
-            shr[...] += part
-            dsec[...] += back
-        gw1[:, hs] += dot_tn(second[...], dexp[...])
-        gw2[hs, :] += dot_tn(act[...], dshr[...])
-
-    t_s1 = t_g2 = t_b2 = t_bm2 = t_s2 = t_pb = t_hb = t_bq = zero
-    dbr = second
-    for i in range(BROWS // 32):
+            z, g = gelu_pair(hid[h % 2, s, :])
+            act[s, chunks[h]] = z.astype(bf16)
+            d = dact[h % 2, s, :] * g
+            dexp[s, chunks[h]] = d.astype(bf16)
+            totals.append(sum8(d) if not totals else totals.pop() + sum8(d))
+
+        def close():
+            bacc[:, chunks[h]] += totals[0]
+
+        return [functools.partial(rows_of, i) for i in range(BROWS // 16)] + [close]
+
+    def weight_grads(h):
+        def one(t):
+            ls = slice(h * HCHUNK + 256 * t, h * HCHUNK + 256 * t + 256)
+            add_to(gw1, slice(None), ls, dot_tn(second[...], dexp[:, ls]))
+
+        def two():
+            add_to(gw2, chunks[h], slice(None), dot_tn(act[:, chunks[h]], dshr[...]))
+
+        return [functools.partial(one, t) for t in range(HCHUNK // 256)] + [two]
+
+    for step_of in enter(0):
+        step_of()
+    weave(enter(1), gelu(0))
+    weave(enter(2) + weight_grads(0), gelu(1))
+    weave(weight_grads(1), gelu(2))
+    shr[...] = dot(act[...], w2[...])
+    dsec[...] = dot_nt(dexp[...], w1[...])
+
+    tally = {}
+
+    def count(key, v):
+        tally[key] = tally[key] + sum8(v) if key in tally else sum8(v)
+
+    def finish(i):
         s = at(0, i, 32)
         middle = mid[s, :]
         u = up[s, :].astype(f32)
         shrunk = shr[s, :] + bm2
-        out_o[s, :] = middle + s2 * shrunk
+        out_o[s, :] = (middle + s2 * shrunk).astype(bf16)
         n, r = norm_stats(middle)
         d = dsec[s, :]
         e = d * g2
@@ -433,30 +482,35 @@
         dmid_o[s, :] = dm
         db = s1 * dm
         dbr[s, :] = db.astype(bf16)
-        t_s1 = t_s1 + sum8(dm * branch[s, :])
-        t_g2 = t_g2 + sum8(dn)
-        t_b2 = t_b2 + sum8(d)
-        t_bm2 = t_bm2 + sum8(dshr[s, :].astype(f32))
-        t_s2 = t_s2 + sum8(u * shrunk)
-        t_pb = t_pb + sum8(db)
-
-    gwp[...] += dot_tn(modulated[...], dbr[...])
-    dmod = dot_nt(dbr[...], wp[...])
-    dm2 = dshr
-    for i in range(BROWS // 32):
+        count(S_S1, dm * branch[s, :])
+        count(S_G2, dn)
+        count(S_B2, d)
+        count(S_BM2, dshr[s, :].astype(f32))
+        count(S_S2, u * shrunk)
+        count(S_PB, db)
+
+    weave(weight_grads(2), [functools.partial(finish, i) for i in range(BROWS // 32)])
+    dmod[...] = dot_nt(dbr[...], wp[...])
+
+    def demod(i):
         s = at(0, i, 32)
         dm = dmod[s, :]
         dq = dm * mod[s, :]
         dd = dm * q_ref[s, :]
         dq_o[s, :] = dq.astype(bf16)
         dm2[s, :] = dd.astype(bf16)
-        t_bq = t_bq + sum8(dq)
-        t_hb = t_hb + sum8(dd)
+        count(S_BQ, dq)
+        count(S_HB, dd)
+
+    def grad_wp():
+        gwp[...] += dot_tn(modulated[...], dbr[...])
+
+    weave([grad_wp], [functools.partial(demod, i) for i in range(BROWS // 32)])
+    dmix_o[...] = dot_nt(dm2[...], wh[...])
     gwh[...] += dot_tn(mixed[...], dm2[...])
-    dmix_o[...] = dot_nt(dm2[...], wh[...])
-
-    for k, t in ((S_HB, t_hb), (S_PB, t_pb), (S_S1, t_s1), (S_G2, t_g2), (S_B2, t_b2), (S_BM2, t_bm2), (S_S2, t_s2), (S_BQ, t_bq)):
-        vacc[k] += t
+
+    for key, v in tally.items():
+        vacc[key] += v
 
     @pl.when(step == pl.num_programs(0) - 1)
     def _():
@@ -468,16 +522,23 @@
 
 def kernel_backward(
     gx, gy, mod_len, small_len,
-    bucket, pos, nb_ref, dq_ref, dmix, gates, z_ref, g_ref, spec, mean_ref, kcat, wf, vec, sums, bsum, gwh, gwp, es, weights,
-    fe, fo, ge, go,
+    bucket, pos, nb_ref, dq_ref, dmix, gates, z_ref, g_ref, spec, mean_ref, kcat, vec, sums, bsum, es, weights,
+    fe, fo, ge, go, wf_far, gwh_far, gwp_far, est_far,
     dmer, own, oth,
     gwf, fsum, gb, dk, h_ref, ecat, ocat, s_a, s_b, s_e, s_o, yca, ycb, acc, facc, wide, flat, small, moved, spread,
+    wf, gwh, gwp, est, sems,
 ):
     step = pl.program_id(0)
     last = pl.num_programs(0) - 1
+    late = [
+        pltpu.make_async_copy(src, dst, sems.at[k])
+        for k, (src, dst) in enumerate(((wf_far, wf), (gwh_far, gwh), (gwp_far, gwp), (est_far, est)))
+    ]
 
     @pl.when(step == 0)
     def _():
+        for copy in late:
+            copy.start()
         for ref in (gwf, facc, acc):
             ref[...] = jnp.zeros_like(ref)
         for lb in range(6):
@@ -602,6 +663,8 @@
 
     @pl.when(step == last)
     def _():
+        for copy in late:
+            copy.wait()
         facc[:, :C] = jnp.broadcast_to(sums[S_BQ : S_BQ + 1, :] * 0.125, (8, C))
         colsum = jnp.sum(facc[...], axis=0, keepdims=True)
         fsum[...] = jnp.broadcast_to(colsum, fsum.shape)
@@ -620,8 +683,8 @@
             total = None
             for lb in (level * 2, level * 2 + 1):
                 hi, lo = split(acc[lb] * jnp.concatenate([weights[...]] * (C // 128), 1))
-                first = dot_tn(es[lb], hi)
-                term = first[:TAPS] + first[TAPS:] + dot_tn(es[lb][:, :TAPS], lo)
+                first = dot(est[lb], hi)
+                term = first[:TAPS] + first[TAPS:] + dot(est[lb, :TAPS, :], lo)
                 total = term if total is None else total + term
             dk[level] = total
         pack_mod(gx, gy, mod_len, small_len, pos, gwf, gwh, gwp, sums, bsum, fsum, gb, dk, own, oth, flat, small, moved, spread)
@@ -664,10 +727,11 @@
         write_native(native, gtok_o, slots)
 
 
-def kernel_out(counts, rows_ref, out_o, native):
+def kernel_out(counts, rows_ref, out_o, native, wide):
     slots = out_o.shape[2]
+    wide[...] = rows_ref[...].astype(f32)
     for im in range(slots):
-        to_native(rows_ref, im * IMG, native, im, slots, (im < counts[0]).astype(f32))
+        to_native(wide, im * IMG, native, im, slots, (im < counts[0]).astype(f32))
     write_native(native, out_o, slots)
 
 
@@ -699,11 +763,13 @@
     return (pos[0] ^ j) * gy + (pos[1] ^ (2 * i + c))
 
 
-def shift_left(first, second, sh):
-    if sh == 0:
-        return first
+def join(first, second, sh):
     lane = lax.broadcasted_iota(jnp.int32, first.shape, 1)
-    return jnp.where(lane < 128 - sh, pltpu.roll(first, 128 - sh, 1), pltpu.roll(second, 128 - sh, 1))
+    return jnp.where(lane < 128 - sh, first, second)
+
+
+def turn(v, sh):
+    return pltpu.roll(v, 128 - sh, 1) if sh else v
 
 
 def shift_right(first, second, sh):
@@ -724,7 +790,7 @@
 END_ROW = B_S2 + 3
 
 
-def kernel_unpack_mod(gx, gy, mod_len, small_len, pos, own, oth, wf_o, wh_o, wp_o, vec_o, bm1_o, kcat_o, flat, small, moved, wide):
+def unpack_mod(gx, gy, mod_len, small_len, pos, own, oth, wf_o, wh_o, wp_o, vec_o, bm1_o, kcat_o, flat, small, moved, wide):
     flat[...] = jnp.zeros_like(flat)
     small[...] = jnp.zeros_like(small)
     mr, sr = block_rows(mod_len), block_rows(small_len)
@@ -737,12 +803,10 @@
                 small[pl.ds(first_row(small_len, d), sr), :] += block[mr : mr + sr]
     lane = lax.broadcasted_iota(jnp.int32, (16, 128), 1)
     for p in range(PERIOD):
+        row, sh = WIDE * p // 128, WIDE * p % 128
+        tiles = [turn(flat[pl.ds(row + j, 16, stride=STRIDE), :], sh) for j in range(MERGED // 128 + (1 if sh else 0))]
         for j in range(MERGED // 128):
-            f = WIDE * p + 128 * j
-            row, sh = f // 128, f % 128
-            a = flat[pl.ds(row, 16, stride=STRIDE), :]
-            b = flat[pl.ds(row + 1, 16, stride=STRIDE), :] if sh else a
-            v = shift_left(a, b, sh)
+            v = join(tiles[j], tiles[j + 1], sh) if sh else tiles[j]
             if j == MERGED // 128 - 1:
                 v = jnp.where(lane < 4, v, 0.0)
             wide[j, pl.ds(p, 16, stride=PERIOD), :] = v
@@ -753,7 +817,7 @@
         wh_o[:, ls] = flat[pl.ds(WF_ROWS + j, C, stride=3), :].astype(bf16)
         wp_o[:, ls] = flat[pl.ds(WF_ROWS + W_ROWS + j, C, stride=3), :].astype(bf16)
     n = moved.shape[0]
-    moved[...] = shift_left(small[0:n, :], small[1 : n + 1, :], 4)
+    moved[...] = join(turn(small[0:n, :], 4), turn(small[1 : n + 1, :], 4), 4)
     vec_o[...] = jnp.zeros_like(vec_o)
     for row, src, start in (
         (V_G1, small, 0), (V_B1, small, 3), (V_BQ, small, 6), (V_BC, small, 9),
@@ -774,8 +838,7 @@
         start += k * k
 
 
-def kernel_unpack_mlp(gx, gy, mlp_len, pos, *refs):
-    blocks, (w1_o, w2_o, flat) = refs[: gy // 2], refs[gy // 2 :]
+def unpack_mlp(gx, gy, mlp_len, pos, blocks, w1_o, w2_o, flat):
     mr = block_rows(mlp_len)
     aligned = mr * 128 == mlp_len
     if not aligned:
@@ -821,19 +884,22 @@
         flat[used:, :] = jnp.zeros_like(flat[used:, :])
     for j in range(MERGED // 128):
         wide[j, :C, :] = gwf[:, 128 * j : 128 * j + 128]
+    turned = {}
+
+    def piece(p, tile):
+        tile = min(tile, MERGED // 128 - 1)
+        if (p, tile) not in turned:
+            turned[p, tile] = turn(wide[tile, pl.ds(p, 16, stride=PERIOD), :], -WIDE * p % 128)
+        return turned[p, tile]
+
     for f in range(STRIDE):
         p = 128 * f // WIDE
         col = 128 * f - WIDE * p
         t, sh = col // 128, col % 128
-
-        def piece(row, tile):
-            tile = min(tile, MERGED // 128 - 1)
-            return wide[tile, pl.ds(row, 16, stride=PERIOD), :]
-
-        v = shift_left(piece(p, t), piece(p, t + 1), sh)
+        v = join(piece(p, t), piece(p, t + 1), sh) if sh else piece(p, t)
         left = WIDE - col
         if left < 128:
-            v = jnp.where(lane < left, v, pltpu.roll(piece(p + 1, 0), left, 1))
+            v = jnp.where(lane < left, v, piece(p + 1, 0))
         flat[pl.ds(f, 16, stride=STRIDE), :] = v
     for j in range(3):
         ls = slice(128 * j, 128 * j + 128)
@@ -917,7 +983,7 @@
         in_specs=[s for _, s in ins],
         out_shape=[o for o, _ in outs],
         out_specs=[s for _, s in outs],
-        scratch_shapes=[pltpu.VMEM(shape, dtype) for shape, dtype in scratch],
+        scratch_shapes=[pltpu.VMEM(*v) if isinstance(v, tuple) else v for v in scratch],
         compiler_params=pltpu.CompilerParams(vmem_limit_bytes=mib * 2**20),
         cost_estimate=pl.CostEstimate(flops=int(micros * 1e9), bytes_accessed=int(micros * 1e6), transcendentals=0),
         name=name,
@@ -939,18 +1005,18 @@
 def prep(tokens):
     slots = tokens.shape[2]
     n = slots * IMG
-    outs = [(sds((n, w), t), rows(IMG, w)) for w, t in ((C, bf16), (C, bf16), (128, f32))]
-    return call(kernel_prep, "prep", (slots,), whole(tokens), outs, [native_rows(slots), ((IMG, C), f32)], 60, 6)
+    outs = [(sds((n, w), t), rows(PAIR, w)) for w, t in ((C, bf16), (C, bf16), (128, f32))]
+    return call(kernel_prep, "prep", (slots // 2,), whole(tokens), outs, [native_rows(slots), ((PAIR, C), f32)], 60, 5)
 
 
 def upstream(counts, cotangent):
     slots = cotangent.shape[2]
     ins = [(counts, smem())] + whole(cotangent)
-    outs = [(sds((slots * IMG, C), bf16), rows(IMG, C))]
-    return call(kernel_upstream, "upstream", (slots,), ins, outs, [native_rows(slots), ((IMG, C), f32)], 60, 5)[0]
-
-
-def forward(xrow, stat, bucket, wf, vec, kcat):
+    outs = [(sds((slots * IMG, C), bf16), rows(PAIR, C))]
+    return call(kernel_upstream, "upstream", (slots // 2,), ins, outs, [native_rows(slots), ((PAIR, C), f32)], 60, 4)[0]
+
+
+def forward(gx, gy, pos, xrow, stat, bucket, own, oth, mod_len, small_len):
     con = constants()
     pairs = xrow.shape[0] // PAIR
     n = pairs * PAIR
@@ -963,33 +1029,42 @@
         (sds((pairs * 3 * SR, C2), bf16), rows(3 * SR, C2)),
         (sds((pairs * 8, C2), f32), rows(8, C2)),
     ]
+    weights = [((C, MERGED), bf16), ((C, C), bf16), ((C, C), bf16), ((VROWS, C), f32), ((8, HID), f32), ((3, 2 * TAPS, C), bf16)]
+    outs += [(sds(shape, dtype), full(shape)) for shape, dtype in weights]
     mats = [jnp.asarray(con[k]) for k in ("es", "fe", "fo", "ge", "go")]
-    ins = [(bucket, smem())] + by_rows(PAIR, xrow, stat) + whole(wf, vec, kcat, *mats)
+    ins = [(bucket, smem()), (pos, smem())] + by_rows(PAIR, xrow, stat) + whole(own, oth, *mats)
     scratch = [
         ((6, SR, C), f32), ((PAIR, C), bf16), ((PAIR, C), f32), ((3 * HALF, C2), bf16), ((3 * HALF, C2), bf16), ((AR, C2), f32), ((BR, C2), f32),
         ((HALF, C2), f32), ((HALF, C2), f32), ((3 * AR, C2), bf16), ((3 * BR, C2), bf16), ((PAIR, C), f32),
         ((4, PAIR, 128), f32),
     ]
-    return call(kernel_forward, "focal_forward", (pairs,), ins, outs, scratch, 60, 32)
-
-
-def middle(gx, gy, pos, xrow, up, mixed, q, wh, wp, w1, w2, vec, bm1, mlp_len):
+    ndev = gx * gy
+    flat_rows = max(span(mod_len, ndev), STRIDE * 16 + 8)
+    small_rows = max(span(small_len, ndev), END_ROW + 26)
+    scratch += [((flat_rows, 128), f32), ((small_rows + 8, 128), f32), ((small_rows, 128), f32)]
+    scratch += [((MERGED // 128, PERIOD * 16, 128), f32)]
+    kernel = functools.partial(kernel_forward, gx, gy, mod_len, small_len)
+    return call(kernel, "focal_forward", (pairs,), ins, outs, scratch, 62, 28)
+
+
+def middle(gx, gy, pos, xrow, up, mixed, q, wh, wp, vec, bm1, mlp_blocks, mlp_len):
     n = xrow.shape[0]
     outs = [
         (sds((n, C), f32), rows(BROWS, C)),
-        (sds((n, C), f32), rows(BROWS, C)),
+        (sds((n, C), bf16), rows(BROWS, C)),
         (sds((n, C), bf16), rows(BROWS, C)),
         (sds((n, C), f32), rows(BROWS, C)),
     ]
     slots = (gy // 2, gx, block_rows(mlp_len), 128)
     outs += [(sds(slots, bf16), full(slots))] * 2
     outs += [(sds(s, f32), full(s)) for s in ((C, C), (C, C), (8, C), (8, HID))]
-    ins = [(pos, smem())] + by_rows(BROWS, xrow, up, mixed, q) + whole(wh, wp, w1, w2, vec, bm1)
+    ins = [(pos, smem())] + by_rows(BROWS, xrow, up, mixed, q) + whole(wh, wp, vec, bm1, *mlp_blocks)
     blk = (BROWS, C)
     scratch = [
         (blk, f32), (blk, bf16), (blk, f32), (blk, f32), (blk, bf16), (blk, bf16), (blk, f32), (blk, f32),
-        ((BROWS, HCHUNK), bf16), ((BROWS, HCHUNK), bf16), ((BROWS, HCHUNK), f32), ((8, 8, C), f32), ((8, HID), f32),
-        ((C, HID), f32), ((HID, C), f32), ((span(mlp_len, gx * gy), 128), f32),
+        ((BROWS, HID), bf16), ((BROWS, HID), bf16), ((2, BROWS, HCHUNK), f32), ((2, BROWS, HCHUNK), f32), (blk, bf16), (blk, bf16), (blk, f32),
+        ((8, 8, C), f32), ((8, HID), f32),
+        ((C, HID), f32), ((HID, C), f32), ((span(mlp_len, gx * gy), 128), f32), ((C, HID), bf16), ((HID, C), bf16),
     ]
     kernel = functools.partial(kernel_middle, gx, gy, mlp_len)
     return call(kernel, "middle", (n // BROWS,), ins, outs, scratch, 62, 42)
@@ -999,12 +1074,15 @@
     con = constants()
     ndev = gx * gy
     pairs = nb.shape[0] // PAIR
-    mats = [jnp.asarray(con["es"]), jnp.asarray(con["weights"]), jnp.asarray(con["fe"][:, :HALF]), jnp.asarray(con["fo"][:, :HALF])]
+    mats = [jnp.asarray(con[k]) for k in ("es", "weights")]
+    mats += [jnp.asarray(con["fe"][:, :HALF]), jnp.asarray(con["fo"][:, :HALF])]
     mats += [jnp.asarray(con["ge"][:, :AR]), jnp.asarray(con["go"][:, :BR])]
     slots = (gy // 2, gx, -(-(block_rows(mod_len) + block_rows(small_len)) // 16) * 16, 128)
     outs = [(sds((nb.shape[0], MERGED), bf16), rows(PAIR, MERGED))] + [(sds(slots, bf16), full(slots))] * 2
     ins = [(bucket, smem()), (pos, smem())] + by_rows(PAIR, nb, dq, dmix, gates) + by_rows(3 * IMG, z, g) + by_rows(3 * SR, spec)
-    ins += by_rows(8, mean) + whole(kcat, wf, vec, sums, bsum, gwh, gwp, *mats)
+    ins += by_rows(8, mean) + whole(kcat, vec, sums, bsum, *mats)
+    late = (wf, gwh, gwp, jnp.asarray(con["est"]))
+    ins += [(v, pl.BlockSpec(memory_space=pl.ANY)) for v in late]
     small_rows = -(-max(span(small_len, ndev), END_ROW + 2) // 8) * 8
     scratch = [
         ((C, MERGED), f32), ((8, MERGED), f32), ((16, C), f32), ((3, TAPS, C), f32), ((6, SR, C), f32),
@@ -1013,6 +1091,7 @@
         ((max(span(mod_len, ndev), STRIDE * 16 + 8), 128), f32), ((small_rows, 128), f32), ((small_rows, 128), f32),
         ((MERGED // 128, PERIOD * 16, 128), f32),
     ]
+    scratch += [(v.shape, v.dtype) for v in late] + [pltpu.SemaphoreType.DMA((len(late),))]
     kernel = functools.partial(kernel_backward, gx, gy, mod_len, small_len)
     return call(kernel, "focal_backward", (pairs,), ins, outs, scratch, 62, 28)
 
@@ -1020,34 +1099,16 @@
 def tail(shape, dmer, wf, xrow, stat, dmid, vec):
     slots = shape[2]
     ins = by_rows(PAIR, dmer) + whole(wf) + by_rows(PAIR, xrow, stat, dmid) + whole(vec)
-    return call(kernel_tail, "tail", (slots // 2,), ins, [(sds(shape, f32), full(shape))], [((PAIR, C), f32), native_rows(slots)], 60, 8)[0]
+    return call(kernel_tail, "tail", (slots // 2,), ins, [(sds(shape, f32), full(shape))], [((PAIR, C), f32), native_rows(slots)], 24, 8)[0]
 
 
 def out_tokens(shape, counts, out_rows):
     ins = [(counts, smem())] + whole(out_rows)
-    return call(kernel_out, "out_tokens", (), ins, [(sds(shape, bf16), full(shape))], [native_rows(shape[2])], 60, 5)[0]
+    return call(kernel_out, "out_tokens", (), ins, [(sds(shape, bf16), full(shape))], [native_rows(shape[2]), ((shape[2] * IMG, C), f32)], 24, 5)[0]
 
 
 def span(length, ndev):
     return ((ndev - 1) * length) // 1024 * 8 + block_rows(length)
-
-
-def unpack_mod(gx, gy, pos, own, oth, mod_len, small_len):
-    ndev = gx * gy
-    outs = [sds((C, MERGED), bf16), sds((C, C), bf16), sds((C, C), bf16), sds((VROWS, C), f32), sds((8, HID), f32), sds((3, 2 * TAPS, C), bf16)]
-    top = STRIDE * 15 + STRIDE + 8
-    flat_rows = max(span(mod_len, ndev), top)
-    small_rows = max(span(small_len, ndev), END_ROW + 26)
-    scratch = [((flat_rows, 128), f32), ((small_rows + 8, 128), f32), ((small_rows, 128), f32), ((MERGED // 128, PERIOD * 16, 128), f32)]
-    kernel = functools.partial(kernel_unpack_mod, gx, gy, mod_len, small_len)
-    return call(kernel, "unpack_mod", (), [(pos, smem())] + whole(own, oth), [(o, full(o.shape)) for o in outs], scratch, 60, 4)
-
-
-def unpack_mlp(gx, gy, pos, blocks, mlp_len):
-    outs = [sds((C, HID), bf16), sds((HID, C), bf16)]
-    kernel = functools.partial(kernel_unpack_mlp, gx, gy, mlp_len)
-    scratch = [((span(mlp_len, gx * gy), 128), f32)]
-    return call(kernel, "unpack_mlp", (), [(pos, smem())] + whole(*blocks), [(o, full(o.shape)) for o in outs], scratch, 60, 3)
 
 
 def add(arrays, outs, name):
@@ -1097,30 +1158,29 @@
     pad = -(mr + sr) % 16
     if pad:
         blocks.append(jnp.zeros((pad, 128), bf16))
-    cut = mr + sr + pad
-    line = around(jnp.concatenate(blocks + [place(mlp_weights, device)], 0), gy, gx, ndev)
+    line = around(jnp.concatenate(blocks, 0), gy, gx, ndev)
     native, back = (1, 2, 0, 3), (2, 0, 1, 3)
     shape = (GH, GW) + tokens.shape[:1] + (C,)
     prepared = prep(jnp.transpose(tokens, native))
-    line, prepared = after((line, prepared))
+    line, mlp_mine, prepared = after((line, place(mlp_weights, device), prepared))
     xrow, nb, stat = prepared
-    plane = around(jnp.stack([v[:cut] for v in line]), 2, gy // 2, ndev)
-    mlp_line = jnp.stack([v[cut:] for v in line])
+    plane = around(jnp.stack(line), 2, gy // 2, ndev)
+    mlp_line = jnp.stack(around(mlp_mine, gy, gx, ndev))
+    up = upstream(counts, jnp.transpose(cotangent, native))
+    plane, mlp_line, up = after((plane, mlp_line, up))
     mlp_other = swap(mlp_line, 1, ndev)
-    up = upstream(counts, jnp.transpose(cotangent, native))
-    plane, mlp_other, up = after((plane, mlp_other, up))
     plane = jnp.stack(plane)
     other = swap(plane, 1, ndev)
     mlp_both = jnp.stack([mlp_line, mlp_other])
     other, mlp_both = after((other, mlp_both))
     mlp_blocks = around(mlp_both, 2, gy // 2, ndev)
 
-    wf, wh, wp, vec, bm1, kcat = unpack_mod(gx, gy, pos, plane, other, mod_len, small_len)
-    q, gates, mixed, z, g, spec, mean = forward(xrow, stat, bucket, wf, vec, kcat)
+    q, gates, mixed, z, g, spec, mean, wf, wh, wp, vec, bm1, kcat = forward(
+        gx, gy, pos, xrow, stat, bucket, plane, other, mod_len, small_len
+    )
     mlp_blocks, mixed = after((mlp_blocks, mixed))
-    w1, w2 = unpack_mlp(gx, gy, pos, mlp_blocks, mlp_len)
     dmid, out_rows, dq, dmix, own, oth, gwh, gwp, sums, bsum = middle(
-        gx, gy, pos, xrow, up, mixed, q, wh, wp, w1, w2, vec, bm1, mlp_len
+        gx, gy, pos, xrow, up, mixed, q, wh, wp, vec, bm1, mlp_blocks, mlp_len
     )
     parts = sum_core(own, oth, gx, gy, "mlp")
     parts, dmix = after((parts, dmix))

time: 180 us -> 171 us (0.950)
  Pallas kernels: 129 us -> 116 us
  starting transfers between devices: 29 us -> 34 us
    pallas_call x15 -> x13, Pallas kernels: 129 us -> 116 us  [call(): pl.pallas_call(kernel, grid=grid, in_specs=[s for _, s in ins], out_shape...]
    ppermute x25 -> x28, starting transfers between devices: 29 us -> 34 us  [swap(): return lax.ppermute(x, AXES, [(k, k ^ mask) for k in range(ndev)])]
    ppermute x25 -> x28, waiting for transfers between devices: 9.74 us -> 11.3 us  [swap(): return lax.ppermute(x, AXES, [(k, k ^ mask) for k in range(ndev)])]
    unnamed x20 -> x32, local copies, waits for them, and re-layouts: 4.38 us -> 3.98 us
  transfers between devices with their start and end apart: 25 -> 28, of which waited for: 5 -> 7; matrix products, arithmetic and copies ran while one was open for 1% -> 0% of each run, Pallas kernels for 46% -> 43%
where the time goes in v1:
time: 171 us
  Pallas kernels  116 us (68%)
  starting transfers between devices  34 us (20%)
  waiting for transfers between devices  11.3 us (7%)
  local copies, waits for them, and re-layouts  7.47 us (4%)
    pallas_call x13, Pallas kernels, call(): pl.pallas_call(kernel, grid=grid, in_specs=[s for _, s in ins], out_shape...  116 us
    ppermute x28, starting transfers between devices, swap(): return lax.ppermute(x, AXES, [(k, k ^ mask) for k in range(ndev)])  34 us
    ppermute x28, waiting for transfers between devices, swap(): return lax.ppermute(x, AXES, [(k, k ^ mask) for k in range(ndev)])  11.3 us
    unnamed x32, local copies, waits for them, and re-layouts  3.98 us
  transfers between devices with their start and end apart: 28, of which 7 were waited for; matrix products, arithmetic and copies ran while one was open for 0% of the time, Pallas kernels for 43%

profile of v1, /device:TPU:0, one launch (start us, length us, event | category | flops | bytes accessed | tf_op | source)
XLA Modules:
  0.0 170.9 jit_solution(1852914772487803153)
XLA Ops:
  0.7 0.9 dynamic_update_slice.7
  1.6 1.1 dynamic_update_slice.6
  2.8 5.1 %collective-permute-start.2 = (bf16[192,128]{1,0:T(8,128)(2,1)S(1)}, bf16[192,128]{1,0:T(8,128)(2,1)S(1)}, u32[]{:S(2)}, u32[]{:S(2)}) collective-permute-start(bf16[192,128]{1,0:T(8,128)(2,1)S(1)} %maximum_maximum_fusion), channel_id=1, source_target_pairs={{0,24},{1,25},{2,26},{3,27},{4,28},{5,29},{6,30},{7,31},{8,16},{9,... | collective-permute-start | bytes 147464 | tf_op jit(solution)/shard_map/ppermute | solution.py:1119
  8.0 0.6 collective-permute-start
  8.6 4.9 %prep.1 = (bf16[2304,384]{1,0:T(8,128)(2,1)}, bf16[2304,384]{1,0:T(8,128)(2,1)}, f32[2304,128]{1,0:T(8,128)}) custom-call(bf16[14,20,8,384]{3,2,1,0:T(8,128)(2,1)} %bitcast.47), custom_call_target="tpu_custom_call" | custom-call | flops 5000000000 | bytes 5000000 | tf_op jit(solution)/shard_map/prep/pallas_call | solution.py:980
  14.2 3.8 %collective-permute-start.8 = (bf16[288,128]{1,0:T(8,128)(2,1)S(1)}, bf16[288,128]{1,0:T(8,128)(2,1)S(1)}, u32[]{:S(2)}, u32[]{:S(2)}) collective-permute-start(bf16[288,128]{1,0:T(8,128)(2,1)S(1)} %bitcast.36), channel_id=1, source_target_pairs={{0,24},{1,25},{2,26},{3,27},{4,28},{5,29},{6,30},{7,31},{8,16},{9,... | collective-permute-start | bytes 221192 | tf_op jit(solution)/shard_map/ppermute | solution.py:1119
  18.0 0.6 collective-permute-start.6
  18.7 2.7 %collective-permute-start.5 = (bf16[4,192,128]{2,1,0:T(8,128)(2,1)S(1)}, bf16[4,192,128]{2,1,0:T(8,128)(2,1)S(1)}, u32[]{:S(2)}, u32[]{:S(2)}) collective-permute-start(bf16[4,192,128]{2,1,0:T(8,128)(2,1)S(1)} %pad_maximum_fusion.3), channel_id=1, source_target_pairs={{0,6},{1,7},{2,4},{3,5},{4,2},{5,3},{6,0},{7,1},{8,14},{9,15},{10,... | collective-permute-start | bytes 589832 | tf_op jit(solution)/shard_map/ppermute | solution.py:1119
  21.3 0.5 collective-permute-start.4
  21.8 0.4 collective-permute-start.3
  22.2 4.1 %upstream.1.up = bf16[2304,384]{1,0:T(8,128)(2,1)} custom-call(s32[1]{0:T(128)S(6)} %copy.25.counts, bf16[14,20,8,384]{3,2,1,0:T(8,128)(2,1)} %bitcast.48), custom_call_target="tpu_custom_call" | custom-call | flops 4000000000 | bytes 4000000 | tf_op jit(solution)/shard_map/upstream/pallas_call | solution.py:980
  26.3 1.0 collective-permute-done.5
  27.3 1.7 %collective-permute-done.4 = bf16[4,192,128]{2,1,0:T(8,128)(2,1)S(1)} collective-permute-done((bf16[4,192,128]{2,1,0:T(8,128)(2,1)S(1)}, bf16[4,192,128]{2,1,0:T(8,128)(2,1)S(1)}, u32[]{:S(2)}, u32[]{:S(2)}) %collective-permute-start.4) | collective-permute-done | bytes 196640 | tf_op jit(solution)/shard_map/ppermute | solution.py:1119
  29.4 0.5 collective-permute-start.10
  29.9 0.6 pad_add_fusion.pos
  30.4 1.6 collective-permute-done.10
  32.1 1.7 %collective-permute-start.13 = (bf16[2,4,288,128]{3,2,1,0:T(8,128)(2,1)S(1)}, bf16[2,4,288,128]{3,2,1,0:T(8,128)(2,1)S(1)}, u32[]{:S(2)}, u32[]{:S(2)}) collective-permute-start(bf16[2,4,288,128]{3,2,1,0:T(8,128)(2,1)S(1)} %pad_maximum_fusion.1.refs_0_), channel_id=1, source_target_pairs={{0,6},{1,7},{2,4},{3,5},{4,2},{5,3},{6,0},{7,1},{8,14},{9,15},{10,... | collective-permute-start | bytes 1769480 | tf_op jit(solution)/shard_map/ppermute | solution.py:1119
  33.9 1.3 collective-permute-start.12
  35.2 0.5 collective-permute-start.11
  35.7 27.7 %focal_forward.1 = (f32[2304,384]{1,0:T(8,128)}, f32[2304,128]{1,0:T(8,128)}, bf16[2304,384]{1,0:T(8,128)(2,1)}, bf16[3456,768]{1,0:T(8,128)(2,1)}, bf16[3456,76...) custom-call(s32[8]{0:T(128)} %bucket.3, ...), custom_call_target="tpu_custom_call" | custom-call | flops 28000000000 | bytes 28000000 | tf_op jit(solution)/shard_map/focal_forward/pallas_call | solution.py:980
  63.4 0.8 copy-done.15
  64.2 41.3 %middle.1 = (f32[2304,384]{1,0:T(8,128)}, bf16[2304,384]{1,0:T(8,128)(2,1)}, bf16[2304,384]{1,0:T(8,128)(2,1)}, f32[2304,384]{1,0:T(8,128)}, bf16[4,4,288,128]{3...) custom-call(s32[2]{0:T(128)} %pad_add_fusion.pos, ...), custom_call_target="tpu_custom_call" | custom-call | flops 41999998976 | bytes 42000000 | tf_op jit(solution)/shard_map/middle/pallas_call | solution.py:980
  105.6 3.0 %collective-permute-done.14.refs_1_ = bf16[4,4,288,128]{3,2,1,0:T(8,128)(2,1)S(1)} collective-permute-done((bf16[4,4,288,128]{3,2,1,0:T(8,128)(2,1)}, bf16[4,4,288,128]{3,2,1,0:T(8,128)(2,1)S(1)}, u32[]{:S(2)}, u32[]{:S(2)}) %collective-permute-start.14) | collective-permute-done | bytes 1179680 | tf_op jit(solution)/shard_map/ppermute | solution.py:1119
  108.7 1.3 copy-done
  109.9 0.3 mlp_sum_core.1
  110.2 0.8 copy-done.1
  111.0 1.5 collective-permute-start.15
  112.5 0.7 collective-permute-start.16
  113.3 1.3 collective-permute-start.17
  114.5 26.9 %focal_backward.1 = (bf16[2304,896]{1,0:T(8,128)(2,1)}, bf16[4,4,192,128]{3,2,1,0:T(8,128)(2,1)}, bf16[4,4,192,128]{3,2,1,0:T(8,128)(2,1)}) custom-call(s32[8]{0:T(128)} %bucket.3, s32[2]{0:T(128)} %pad_add_fusion.pos, bf16[2304,384]{1,0:T(8,128)(2,1)} %get-tuple-element.140.nb_ref, bf16[2304,384]{1,0:T(8,128)(2,1)} %get-tuple-element.141.dq_ref, ...), custom_call_target="tpu_custom_call" | custom-call | flops 28000000000 | bytes 28000000 | tf_op jit(solution)/shard_map/focal_backward/pallas_call | solution.py:980
  141.5 1.1 copy-done.2
  142.7 1.4 collective-permute-start.22
  144.1 2.6 %collective-permute-start.23 = (bf16[288,128]{1,0:T(8,128)(2,1)S(1)}, bf16[288,128]{1,0:T(8,128)(2,1)S(1)}, u32[]{:S(2)}, u32[]{:S(2)}) collective-permute-start(bf16[288,128]{1,0:T(8,128)(2,1)S(1)} %get-tuple-element.168), channel_id=1, source_target_pairs={{0,16},{1,17},{2,18},{3,19},{4,20},{5,21},{6,22},{7,23},{8,24},{9,... | collective-permute-start | bytes 221192 | tf_op jit(solution)/shard_map/ppermute | solution.py:1119
  146.8 0.4 collective-permute-start.24
  147.2 0.2 mod_sum_core.1
  147.4 1.6 collective-permute-start.19
  149.0 0.7 collective-permute-start.20
  149.7 1.3 collective-permute-start.21
  151.0 6.8 %tail.1 = f32[14,20,8,384]{3,2,1,0:T(8,128)} custom-call(bf16[2304,896]{1,0:T(8,128)(2,1)S(1)} %copy-done.4, bf16[384,896]{1,0:T(8,128)(2,1)S(1)} %copy-done.9, bf16[2304,384]{1,0:T(8,128)(2,1)S(1)} %copy-done.6, f32[2304,128]{1,0:T(8,128)S(1)} %copy-done.8, f32[2304,384]{1,0:T(8,128)S(1)} %copy-done.5, f32[16,384]{1,0:T(8,128)S(1)} %copy-done.10), custom_call_target="tpu_custom_call" | custom-call | flops 8000000000 | bytes 8000000 | tf_op jit(solution)/shard_map/tail/pallas_call | solution.py:980
  157.8 1.5 collective-permute-done.20.refs_2_
  159.5 0.6 collective-permute-start.25
  160.0 3.5 %collective-permute-start.26 = (bf16[192,128]{1,0:T(8,128)(2,1)S(1)}, bf16[192,128]{1,0:T(8,128)(2,1)S(1)}, u32[]{:S(2)}, u32[]{:S(2)}) collective-permute-start(bf16[192,128]{1,0:T(8,128)(2,1)S(1)} %get-tuple-element.179), channel_id=1, source_target_pairs={{0,16},{1,17},{2,18},{3,19},{4,20},{5,21},{6,22},{7,23},{8,24},{9,... | collective-permute-start | bytes 147464 | tf_op jit(solution)/shard_map/ppermute | solution.py:1119
  163.5 0.4 collective-permute-start.27
  163.9 2.6 %out_tokens.1 = bf16[14,20,8,384]{3,2,1,0:T(8,128)(2,1)} custom-call(s32[1]{0:T(128)S(6)} %copy.25.counts, bf16[2304,384]{1,0:T(8,128)(2,1)S(1)} %copy-done.7), custom_call_target="tpu_custom_call" | custom-call | flops 5000000000 | bytes 5000000 | tf_op jit(solution)/shard_map/out_tokens/pallas_call | solution.py:980
  166.6 0.7 mlp_sum_line.1
  167.3 2.2 %collective-permute-done.27.refs_3_ = bf16[192,128]{1,0:T(8,128)(2,1)S(1)} collective-permute-done((bf16[192,128]{1,0:T(8,128)(2,1)S(1)}, bf16[192,128]{1,0:T(8,128)(2,1)S(1)}, u32[]{:S(2)}, u32[]{:S(2)}) %collective-permute-start.27) | collective-permute-done | bytes 49184 | tf_op jit(solution)/shard_map/ppermute | solution.py:1119
  169.5 0.7 dynamic_slice.6
  170.2 0.7 dynamic_slice.7
  (67 shorter events, 1.1 us)
Async XLA Ops:
  2.8 11.3 %collective-permute-start.2 = (bf16[192,128]{1,0:T(8,128)(2,1)S(1)}, bf16[192,128]{1,0:T(8,128)(2,1)S(1)}, u32[]{:S(2)}, u32[]{:S(2)}) collective-permute-start(bf16[192,128]{1,0:T(8,128)(2,1)S(1)} %maximum_maximum_fusion), channel_id=1, source_target_pairs={{0,24},{1,25},{2,26},{3,27},{4,28},{5,29},{6,30},{7,31},{8,16},{9,... | collective-permute-start | bytes 147464 | tf_op jit(solution)/shard_map/ppermute | solution.py:1119
  8.0 6.2 %collective-permute-start.1 = (bf16[192,128]{1,0:T(8,128)(2,1)S(1)}, bf16[192,128]{1,0:T(8,128)(2,1)S(1)}, u32[]{:S(2)}, u32[]{:S(2)}) collective-permute-start(bf16[192,128]{1,0:T(8,128)(2,1)S(1)} %maximum_maximum_fusion), channel_id=1, source_target_pairs={{0,16},{1,17},{2,18},{3,19},{4,20},{5,21},{6,22},{7,23},{8,24},{9,... | collective-permute-start | bytes 147464 | tf_op jit(solution)/shard_map/ppermute | solution.py:1119
  8.0 6.2 %collective-permute-start = (bf16[192,128]{1,0:T(8,128)(2,1)S(1)}, bf16[192,128]{1,0:T(8,128)(2,1)S(1)}, u32[]{:S(2)}, u32[]{:S(2)}) collective-permute-start(bf16[192,128]{1,0:T(8,128)(2,1)S(1)} %maximum_maximum_fusion), channel_id=1, source_target_pairs={{0,8},{1,9},{2,10},{3,11},{4,12},{5,13},{6,14},{7,15},{8,0},{9,1},... | collective-permute-start | bytes 147464 | tf_op jit(solution)/shard_map/ppermute | solution.py:1119
  8.6 5.6 %copy-start.13 = (bf16[36864]{0:T(1024)(128)(2,1)S(1)}, bf16[36864]{0:T(1024)(128)(2,1)}, u32[]{:S(2)}) copy-start(bf16[36864]{0:T(1024)(128)(2,1)} %param.22) | copy-start | bytes 221188
  14.2 7.7 %collective-permute-start.8 = (bf16[288,128]{1,0:T(8,128)(2,1)S(1)}, bf16[288,128]{1,0:T(8,128)(2,1)S(1)}, u32[]{:S(2)}, u32[]{:S(2)}) collective-permute-start(bf16[288,128]{1,0:T(8,128)(2,1)S(1)} %bitcast.36), channel_id=1, source_target_pairs={{0,24},{1,25},{2,26},{3,27},{4,28},{5,29},{6,30},{7,31},{8,16},{9,... | collective-permute-start | bytes 221192 | tf_op jit(solution)/shard_map/ppermute | solution.py:1119
  18.0 8.3 %collective-permute-start.7 = (bf16[288,128]{1,0:T(8,128)(2,1)S(1)}, bf16[288,128]{1,0:T(8,128)(2,1)S(1)}, u32[]{:S(2)}, u32[]{:S(2)}) collective-permute-start(bf16[288,128]{1,0:T(8,128)(2,1)S(1)} %bitcast.37), channel_id=1, source_target_pairs={{0,16},{1,17},{2,18},{3,19},{4,20},{5,21},{6,22},{7,23},{8,24},{9,... | collective-permute-start | bytes 221192 | tf_op jit(solution)/shard_map/ppermute | solution.py:1119
  18.0 8.3 %collective-permute-start.6 = (bf16[288,128]{1,0:T(8,128)(2,1)S(1)}, bf16[288,128]{1,0:T(8,128)(2,1)S(1)}, u32[]{:S(2)}, u32[]{:S(2)}) collective-permute-start(bf16[288,128]{1,0:T(8,128)(2,1)S(1)} %bitcast.38), channel_id=1, source_target_pairs={{0,8},{1,9},{2,10},{3,11},{4,12},{5,13},{6,14},{7,15},{8,0},{9,1},... | collective-permute-start | bytes 221192 | tf_op jit(solution)/shard_map/ppermute | solution.py:1119
  18.7 8.7 %collective-permute-start.5 = (bf16[4,192,128]{2,1,0:T(8,128)(2,1)S(1)}, bf16[4,192,128]{2,1,0:T(8,128)(2,1)S(1)}, u32[]{:S(2)}, u32[]{:S(2)}) collective-permute-start(bf16[4,192,128]{2,1,0:T(8,128)(2,1)S(1)} %pad_maximum_fusion.3), channel_id=1, source_target_pairs={{0,6},{1,7},{2,4},{3,5},{4,2},{5,3},{6,0},{7,1},{8,14},{9,15},{10,... | collective-permute-start | bytes 589832 | tf_op jit(solution)/shard_map/ppermute | solution.py:1119
  21.3 7.8 %collective-permute-start.4 = (bf16[4,192,128]{2,1,0:T(8,128)(2,1)S(1)}, bf16[4,192,128]{2,1,0:T(8,128)(2,1)S(1)}, u32[]{:S(2)}, u32[]{:S(2)}) collective-permute-start(bf16[4,192,128]{2,1,0:T(8,128)(2,1)S(1)} %pad_maximum_fusion.3), channel_id=1, source_target_pairs={{0,4},{1,5},{2,6},{3,7},{4,0},{5,1},{6,2},{7,3},{8,12},{9,13},{10,... | collective-permute-start | bytes 589832 | tf_op jit(solution)/shard_map/ppermute | solution.py:1119
  21.8 7.3 %collective-permute-start.3 = (bf16[4,192,128]{2,1,0:T(8,128)(2,1)S(1)}, bf16[4,192,128]{2,1,0:T(8,128)(2,1)S(1)}, u32[]{:S(2)}, u32[]{:S(2)}) collective-permute-start(bf16[4,192,128]{2,1,0:T(8,128)(2,1)S(1)} %pad_maximum_fusion.3), channel_id=1, source_target_pairs={{0,2},{1,3},{2,0},{3,1},{4,6},{5,7},{6,4},{7,5},{8,10},{9,11},{10,... | collective-permute-start | bytes 589832 | tf_op jit(solution)/shard_map/ppermute | solution.py:1119
  29.3 6.4 %copy-start.11 = (bf16[4,4,192,128]{3,2,1,0:T(8,128)(2,1)}, bf16[4,4,192,128]{3,2,1,0:T(8,128)(2,1)S(1)}, u32[]{:S(2)}) copy-start(bf16[4,4,192,128]{3,2,1,0:T(8,128)(2,1)S(1)} %pad_maximum_fusion.own) | copy-start | bytes 2359300
  29.3 2.8 %collective-permute-start.9 = (bf16[4,4,192,128]{3,2,1,0:T(8,128)(2,1)S(1)}, bf16[4,4,192,128]{3,2,1,0:T(8,128)(2,1)S(1)}, u32[]{:S(2)}, u32[]{:S(2)}) collective-permute-start(bf16[4,4,192,128]{3,2,1,0:T(8,128)(2,1)S(1)} %pad_maximum_fusion.own), channel_id=1, source_target_pairs={{0,1},{1,0},{2,3},{3,2},{4,5},{5,4},{6,7},{7,6},{8,9},{9,8},{10,11... | collective-permute-start | bytes 2359304 | tf_op jit(solution)/shard_map/ppermute | solution.py:1119
  29.4 2.7 %collective-permute-start.10 = (bf16[4,288,128]{2,1,0:T(8,128)(2,1)S(1)}, bf16[4,288,128]{2,1,0:T(8,128)(2,1)S(1)}, u32[]{:S(2)}, u32[]{:S(2)}) collective-permute-start(bf16[4,288,128]{2,1,0:T(8,128)(2,1)S(1)} %pad_maximum_fusion.2), channel_id=1, source_target_pairs={{0,1},{1,0},{2,3},{3,2},{4,5},{5,4},{6,7},{7,6},{8,9},{9,8},{10,11... | collective-permute-start | bytes 884744 | tf_op jit(solution)/shard_map/ppermute | solution.py:1119
  32.1 31.3 %copy-start.12 = (bf16[2,4,288,128]{3,2,1,0:T(8,128)(2,1)}, bf16[2,4,288,128]{3,2,1,0:T(8,128)(2,1)S(1)}, u32[]{:S(2)}) copy-start(bf16[2,4,288,128]{3,2,1,0:T(8,128)(2,1)S(1)} %pad_maximum_fusion.1.refs_0_) | copy-start | bytes 1769476
  32.1 1.7 %copy-start.14 = (bf16[4,4,192,128]{3,2,1,0:T(8,128)(2,1)}, bf16[4,4,192,128]{3,2,1,0:T(8,128)(2,1)S(1)}, u32[]{:S(2)}) copy-start(bf16[4,4,192,128]{3,2,1,0:T(8,128)(2,1)S(1)} %collective-permute-done.9.oth) | copy-start | bytes 2359300
  32.1 31.3 %collective-permute-start.13 = (bf16[2,4,288,128]{3,2,1,0:T(8,128)(2,1)S(1)}, bf16[2,4,288,128]{3,2,1,0:T(8,128)(2,1)S(1)}, u32[]{:S(2)}, u32[]{:S(2)}) collective-permute-start(bf16[2,4,288,128]{3,2,1,0:T(8,128)(2,1)S(1)} %pad_maximum_fusion.1.refs_0_), channel_id=1, source_target_pairs={{0,6},{1,7},{2,4},{3,5},{4,2},{5,3},{6,0},{7,1},{8,14},{9,15},{10,... | collective-permute-start | bytes 1769480 | tf_op jit(solution)/shard_map/ppermute | solution.py:1119
  33.9 29.6 %collective-permute-start.12 = (bf16[2,4,288,128]{3,2,1,0:T(8,128)(2,1)S(1)}, bf16[2,4,288,128]{3,2,1,0:T(8,128)(2,1)}, u32[]{:S(2)}, u32[]{:S(2)}) collective-permute-start(bf16[2,4,288,128]{3,2,1,0:T(8,128)(2,1)S(1)} %pad_maximum_fusion.1.refs_0_), channel_id=1, source_target_pairs={{0,4},{1,5},{2,6},{3,7},{4,0},{5,1},{6,2},{7,3},{8,12},{9,13},{10,... | collective-permute-start | bytes 1769480 | tf_op jit(solution)/shard_map/ppermute | solution.py:1119
  35.2 28.3 %collective-permute-start.11 = (bf16[2,4,288,128]{3,2,1,0:T(8,128)(2,1)S(1)}, bf16[2,4,288,128]{3,2,1,0:T(8,128)(2,1)}, u32[]{:S(2)}, u32[]{:S(2)}) collective-permute-start(bf16[2,4,288,128]{3,2,1,0:T(8,128)(2,1)S(1)} %pad_maximum_fusion.1.refs_0_), channel_id=1, source_target_pairs={{0,2},{1,3},{2,0},{3,1},{4,6},{5,7},{6,4},{7,5},{8,10},{9,11},{10,... | collective-permute-start | bytes 1769480 | tf_op jit(solution)/shard_map/ppermute | solution.py:1119
  63.4 0.8 copy-start.15
  105.5 3.1 %collective-permute-start.14 = (bf16[4,4,288,128]{3,2,1,0:T(8,128)(2,1)}, bf16[4,4,288,128]{3,2,1,0:T(8,128)(2,1)S(1)}, u32[]{:S(2)}, u32[]{:S(2)}) collective-permute-start(bf16[4,4,288,128]{3,2,1,0:T(8,128)(2,1)} %get-tuple-element.130), channel_id=1, source_target_pairs={{0,1},{1,0},{2,3},{3,2},{4,5},{5,4},{6,7},{7,6},{8,9},{9,8},{10,11... | collective-permute-start | bytes 3538952 | tf_op jit(solution)/shard_map/ppermute | solution.py:1119
  108.7 1.3 copy-start
  110.2 0.8 copy-start.1
  111.0 30.4 %collective-permute-start.15 = (bf16[4,288,128]{2,1,0:T(8,128)(2,1)S(1)}, bf16[4,288,128]{2,1,0:T(8,128)(2,1)S(1)}, u32[]{:S(2)}, u32[]{:S(2)}) collective-permute-start(bf16[4,288,128]{2,1,0:T(8,128)(2,1)S(1)} %get-tuple-element.137), channel_id=1, source_target_pairs={{0,2},{1,3},{2,0},{3,1},{4,6},{5,7},{6,4},{7,5},{8,10},{9,11},{10,... | collective-permute-start | bytes 884744 | tf_op jit(solution)/shard_map/ppermute | solution.py:1119
  112.5 28.9 %collective-permute-start.16 = (bf16[4,288,128]{2,1,0:T(8,128)(2,1)S(1)}, bf16[4,288,128]{2,1,0:T(8,128)(2,1)S(1)}, u32[]{:S(2)}, u32[]{:S(2)}) collective-permute-start(bf16[4,288,128]{2,1,0:T(8,128)(2,1)S(1)} %get-tuple-element.138), channel_id=1, source_target_pairs={{0,4},{1,5},{2,6},{3,7},{4,0},{5,1},{6,2},{7,3},{8,12},{9,13},{10,... | collective-permute-start | bytes 884744 | tf_op jit(solution)/shard_map/ppermute | solution.py:1119
  113.3 28.1 %collective-permute-start.17 = (bf16[4,288,128]{2,1,0:T(8,128)(2,1)S(1)}, bf16[4,288,128]{2,1,0:T(8,128)(2,1)S(1)}, u32[]{:S(2)}, u32[]{:S(2)}) collective-permute-start(bf16[4,288,128]{2,1,0:T(8,128)(2,1)S(1)} %get-tuple-element.139), channel_id=1, source_target_pairs={{0,6},{1,7},{2,4},{3,5},{4,2},{5,3},{6,0},{7,1},{8,14},{9,15},{10,... | collective-permute-start | bytes 884744 | tf_op jit(solution)/shard_map/ppermute | solution.py:1119
  141.4 5.8 %collective-permute-start.18 = (bf16[4,4,192,128]{3,2,1,0:T(8,128)(2,1)}, bf16[4,4,192,128]{3,2,1,0:T(8,128)(2,1)S(1)}, u32[]{:S(2)}, u32[]{:S(2)}) collective-permute-start(bf16[4,4,192,128]{3,2,1,0:T(8,128)(2,1)} %get-tuple-element.157), channel_id=1, source_target_pairs={{0,1},{1,0},{2,3},{3,2},{4,5},{5,4},{6,7},{7,6},{8,9},{9,8},{10,11... | collective-permute-start | bytes 2359304 | tf_op jit(solution)/shard_map/ppermute | solution.py:1119
  141.5 1.1 copy-start.2
  142.6 4.7 %copy-start.3 = (bf16[4,4,192,128]{3,2,1,0:T(8,128)(2,1)S(1)}, bf16[4,4,192,128]{3,2,1,0:T(8,128)(2,1)}, u32[]{:S(2)}) copy-start(bf16[4,4,192,128]{3,2,1,0:T(8,128)(2,1)} %get-tuple-element.156.refs_0_) | copy-start | bytes 2359300
  142.6 8.4 %copy-start.5 = (f32[2304,384]{1,0:T(8,128)S(1)}, f32[2304,384]{1,0:T(8,128)}, u32[]{:S(2)}) copy-start(f32[2304,384]{1,0:T(8,128)} %get-tuple-element.171.dmid) | copy-start | bytes 10616836
  142.6 8.4 %copy-start.9 = (bf16[384,896]{1,0:T(8,128)(2,1)S(1)}, bf16[384,896]{1,0:T(8,128)(2,1)}, u32[]{:S(2)}) copy-start(bf16[384,896]{1,0:T(8,128)(2,1)} %get-tuple-element.151.wf_far.wf) | copy-start | bytes 2064388
  142.7 7.0 %collective-permute-start.22 = (bf16[288,128]{1,0:T(8,128)(2,1)S(1)}, bf16[288,128]{1,0:T(8,128)(2,1)S(1)}, u32[]{:S(2)}, u32[]{:S(2)}) collective-permute-start(bf16[288,128]{1,0:T(8,128)(2,1)S(1)} %get-tuple-element.167), channel_id=1, source_target_pairs={{0,8},{1,9},{2,10},{3,11},{4,12},{5,13},{6,14},{7,15},{8,0},{9,1},... | collective-permute-start | bytes 221192 | tf_op jit(solution)/shard_map/ppermute | solution.py:1119
  144.1 13.7 %collective-permute-start.23 = (bf16[288,128]{1,0:T(8,128)(2,1)S(1)}, bf16[288,128]{1,0:T(8,128)(2,1)S(1)}, u32[]{:S(2)}, u32[]{:S(2)}) collective-permute-start(bf16[288,128]{1,0:T(8,128)(2,1)S(1)} %get-tuple-element.168), channel_id=1, source_target_pairs={{0,16},{1,17},{2,18},{3,19},{4,20},{5,21},{6,22},{7,23},{8,24},{9,... | collective-permute-start | bytes 221192 | tf_op jit(solution)/shard_map/ppermute | solution.py:1119
  146.8 4.2 %copy-start.4 = (bf16[2304,896]{1,0:T(8,128)(2,1)S(1)}, bf16[2304,896]{1,0:T(8,128)(2,1)}, u32[]{:S(2)}) copy-start(bf16[2304,896]{1,0:T(8,128)(2,1)} %get-tuple-element.170.dmer) | copy-start | bytes 12386308
  146.8 4.2 %copy-start.6 = (bf16[2304,384]{1,0:T(8,128)(2,1)S(1)}, bf16[2304,384]{1,0:T(8,128)(2,1)}, u32[]{:S(2)}) copy-start(bf16[2304,384]{1,0:T(8,128)(2,1)} %get-tuple-element.103.x_ref) | copy-start | bytes 5308420
  146.8 4.2 %copy-start.8 = (f32[2304,128]{1,0:T(8,128)S(1)}, f32[2304,128]{1,0:T(8,128)}, u32[]{:S(2)}) copy-start(f32[2304,128]{1,0:T(8,128)} %get-tuple-element.116.stat) | copy-start | bytes 3538948
  146.8 4.2 %copy-start.10 = (f32[16,384]{1,0:T(8,128)S(1)}, f32[16,384]{1,0:T(8,128)}, u32[]{:S(2)}) copy-start(f32[16,384]{1,0:T(8,128)} %get-tuple-element.123.vec) | copy-start | bytes 73732
  146.8 11.0 %collective-permute-start.24 = (bf16[288,128]{1,0:T(8,128)(2,1)S(1)}, bf16[288,128]{1,0:T(8,128)(2,1)S(1)}, u32[]{:S(2)}, u32[]{:S(2)}) collective-permute-start(bf16[288,128]{1,0:T(8,128)(2,1)S(1)} %get-tuple-element.169), channel_id=1, source_target_pairs={{0,24},{1,25},{2,26},{3,27},{4,28},{5,29},{6,30},{7,31},{8,16},{9,... | collective-permute-start | bytes 221192 | tf_op jit(solution)/shard_map/ppermute | solution.py:1119
  147.4 10.4 %collective-permute-start.19 = (bf16[4,192,128]{2,1,0:T(8,128)(2,1)S(1)}, bf16[4,192,128]{2,1,0:T(8,128)(2,1)S(1)}, u32[]{:S(2)}, u32[]{:S(2)}) collective-permute-start(bf16[4,192,128]{2,1,0:T(8,128)(2,1)S(1)} %get-tuple-element.159), channel_id=1, source_target_pairs={{0,2},{1,3},{2,0},{3,1},{4,6},{5,7},{6,4},{7,5},{8,10},{9,11},{10,... | collective-permute-start | bytes 589832 | tf_op jit(solution)/shard_map/ppermute | solution.py:1119
  149.0 10.4 %collective-permute-start.20 = (bf16[4,192,128]{2,1,0:T(8,128)(2,1)S(1)}, bf16[4,192,128]{2,1,0:T(8,128)(2,1)S(1)}, u32[]{:S(2)}, u32[]{:S(2)}) collective-permute-start(bf16[4,192,128]{2,1,0:T(8,128)(2,1)S(1)} %get-tuple-element.160), channel_id=1, source_target_pairs={{0,4},{1,5},{2,6},{3,7},{4,0},{5,1},{6,2},{7,3},{8,12},{9,13},{10,... | collective-permute-start | bytes 589832 | tf_op jit(solution)/shard_map/ppermute | solution.py:1119
  149.7 9.7 %collective-permute-start.21 = (bf16[4,192,128]{2,1,0:T(8,128)(2,1)S(1)}, bf16[4,192,128]{2,1,0:T(8,128)(2,1)S(1)}, u32[]{:S(2)}, u32[]{:S(2)}) collective-permute-start(bf16[4,192,128]{2,1,0:T(8,128)(2,1)S(1)} %get-tuple-element.161), channel_id=1, source_target_pairs={{0,6},{1,7},{2,4},{3,5},{4,2},{5,3},{6,0},{7,1},{8,14},{9,15},{10,... | collective-permute-start | bytes 589832 | tf_op jit(solution)/shard_map/ppermute | solution.py:1119
  159.4 4.5 %copy-start.7 = (bf16[2304,384]{1,0:T(8,128)(2,1)S(1)}, bf16[2304,384]{1,0:T(8,128)(2,1)}, u32[]{:S(2)}) copy-start(bf16[2304,384]{1,0:T(8,128)(2,1)} %get-tuple-element.181.rows_ref) | copy-start | bytes 5308420
  159.5 7.8 %collective-permute-start.25 = (bf16[192,128]{1,0:T(8,128)(2,1)S(1)}, bf16[192,128]{1,0:T(8,128)(2,1)S(1)}, u32[]{:S(2)}, u32[]{:S(2)}) collective-permute-start(bf16[192,128]{1,0:T(8,128)(2,1)S(1)} %get-tuple-element.178), channel_id=1, source_target_pairs={{0,8},{1,9},{2,10},{3,11},{4,12},{5,13},{6,14},{7,15},{8,0},{9,1},... | collective-permute-start | bytes 147464 | tf_op jit(solution)/shard_map/ppermute | solution.py:1119
  160.0 7.2 %collective-permute-start.26 = (bf16[192,128]{1,0:T(8,128)(2,1)S(1)}, bf16[192,128]{1,0:T(8,128)(2,1)S(1)}, u32[]{:S(2)}, u32[]{:S(2)}) collective-permute-start(bf16[192,128]{1,0:T(8,128)(2,1)S(1)} %get-tuple-element.179), channel_id=1, source_target_pairs={{0,16},{1,17},{2,18},{3,19},{4,20},{5,21},{6,22},{7,23},{8,24},{9,... | collective-permute-start | bytes 147464 | tf_op jit(solution)/shard_map/ppermute | solution.py:1119
  163.5 5.9 %collective-permute-start.27 = (bf16[192,128]{1,0:T(8,128)(2,1)S(1)}, bf16[192,128]{1,0:T(8,128)(2,1)S(1)}, u32[]{:S(2)}, u32[]{:S(2)}) collective-permute-start(bf16[192,128]{1,0:T(8,128)(2,1)S(1)} %get-tuple-element.180), channel_id=1, source_target_pairs={{0,24},{1,25},{2,26},{3,27},{4,28},{5,29},{6,30},{7,31},{8,16},{9,... | collective-permute-start | bytes 147464 | tf_op jit(solution)/shard_map/ppermute | solution.py:1119

commit v2 on v1

--- a/solution.py
+++ b/solution.py
@@ -36,6 +36,7 @@
 EPS = 1e-05
 ROOT_HALF = 0.7071067811865476
 INV_ROOT_2PI = 0.3989422804014327
+LOG2_E = 1.4426950408889634
 
 
 def _hi(a):
@@ -44,6 +45,10 @@
 
 def _lo(a):
     return (a - a.astype(bf16).astype(np.float64)).astype(bf16)
+
+
+def three(a):
+    return np.concatenate([_hi(a), _lo(a), _hi(a)], 1)
 
 
 @functools.lru_cache(maxsize=None)
@@ -97,10 +102,14 @@
             whole_e[:, : k * k] = np.concatenate(e, 0)
             es.append(np.concatenate([_hi(whole_e), _lo(whole_e)], 1))
     return dict(
-        fe=np.concatenate([_hi(fe), _lo(fe), _hi(fe)], 1),
-        fo=np.concatenate([_hi(fo), _lo(fo), _hi(fo)], 1),
-        ge=np.concatenate([_hi(ge), _lo(ge), _hi(ge)], 1),
-        go=np.concatenate([_hi(go), _lo(go), _hi(go)], 1),
+        fe=three(fe),
+        fo=three(fo),
+        ge=three(ge * ROOT_HALF),
+        go=three(go * ROOT_HALF),
+        fe_back=_hi(fe * ROOT_HALF),
+        fo_back=_hi(fo * ROOT_HALF),
+        ge_back=_hi(ge),
+        go_back=_hi(go),
         es=np.stack(es),
         est=np.stack([np.ascontiguousarray(e.T) for e in es]),
         weights=np.broadcast_to(weights, (SR, 128)).astype(np.float32),
@@ -121,7 +130,12 @@
 
 def gelu_pair(x):
     cdf = 0.5 * lax.erf(x * ROOT_HALF) + 0.5
-    return x * cdf, cdf + x * (jnp.exp(x * x * -0.5) * INV_ROOT_2PI)
+    return x * cdf, cdf + x * (jnp.exp2(x * x * (-0.5 * LOG2_E)) * INV_ROOT_2PI)
+
+
+def gelu_scaled(u):
+    w = lax.erf(u) * ROOT_HALF + ROOT_HALF
+    return u * w, w + u * (jnp.exp2(u * u * -LOG2_E) * (2 * INV_ROOT_2PI))
 
 
 def split(x):
@@ -172,38 +186,34 @@
 (S_HB, S_PB, S_S1, S_G2, S_B2, S_BM2, S_S2, S_BQ) = range(8)
 
 
-def from_native(src, native):
+def from_native(src, field):
     slots = src.shape[2]
-    line = GW * slots
-    for y in range(GH):
-        for lt in range(C // 128):
-            ls = slice(128 * lt, 128 * lt + 128)
-            native[lt, line * y : line * (y + 1), :] = src[y, :, :, ls].astype(f32).reshape(line, 128)
-
-
-def image_rows(native, image, first, slot, slots, gain):
-    for h in (GH // 2 * GW, HALF + GH // 2 * GW):
-        image[first + h : first + h + 4, :] = jnp.zeros((4, C), f32)
-    for y in range(GH):
-        a = first + grid_rows(0, y)
-        for lt in range(C // 128):
-            v = native[lt, pl.ds(GW * slots * y + slot, GW, stride=slots), :]
-            image[a : a + GW, 128 * lt : 128 * lt + 128] = v if gain is None else v * gain
-
-
-def kernel_prep(x_ref, xrow_o, nb_o, stat_o, native, image):
-    slot = pl.program_id(0)
-
-    @pl.when(slot == 0)
+    for lt in range(C // 128):
+        for im in range(slots):
+            for h in (GH // 2 * GW, HALF + GH // 2 * GW):
+                field[lt, im * PITCH_IMAGE + h : im * PITCH_IMAGE + h + 4, :] = jnp.zeros((4, 128), f32)
+        for y in range(GH):
+            for x in range(GW):
+                v = src[y, x, :, 128 * lt : 128 * lt + 128].astype(f32)
+                field[lt, pl.ds(grid_rows(0, y) + x, slots, stride=PITCH_IMAGE), :] = v
+
+
+def field_rows(field, first, n):
+    s = pl.ds(pl.multiple_of(first, 8), n)
+    return jnp.concatenate([field[lt, s, :] for lt in range(C // 128)], axis=1)
+
+
+def kernel_prep(x_ref, xrow_o, nb_o, stat_o, field):
+    step = pl.program_id(0)
+
+    @pl.when(step == 0)
     def _():
-        from_native(x_ref, native)
-
-    for im in range(2):
-        image_rows(native, image, im * IMG, slot * 2 + im, x_ref.shape[2], None)
+        from_native(x_ref, field)
+
     lane = lax.broadcasted_iota(jnp.int32, (32, 128), 1)
-    for i in range(PAIR // 32):
-        s = at(0, i, 32)
-        x = image[s, :]
+    for k in range(PAIR // 32):
+        s = at(0, k, 32)
+        x = field_rows(field, (step * 2 + k // (IMG // 32)) * PITCH_IMAGE + 32 * (k % (IMG // 32)), 32)
         xrow_o[s, :] = x.astype(bf16)
         mean = jnp.mean(x, axis=-1, keepdims=True)
         centred = x - mean
@@ -212,19 +222,18 @@
         stat_o[s, :] = jnp.where(lane == 0, mean, r)
 
 
-def kernel_upstream(counts, cot_ref, up_o, native, image):
-    slot = pl.program_id(0)
-
-    @pl.when(slot == 0)
+def kernel_upstream(counts, cot_ref, up_o, field):
+    step = pl.program_id(0)
+
+    @pl.when(step == 0)
     def _():
-        from_native(cot_ref, native)
+        from_native(cot_ref, field)
 
     for im in range(2):
-        live = (slot * 2 + im < counts[0]).astype(f32)
-        image_rows(native, image, im * IMG, slot * 2 + im, cot_ref.shape[2], live)
-    for i in range(PAIR // 32):
-        s = at(0, i, 32)
-        up_o[s, :] = image[s, :].astype(bf16)
+        live = (step * 2 + im < counts[0]).astype(f32)
+        for i in range(IMG // 32):
+            v = field_rows(field, (step * 2 + im) * PITCH_IMAGE + 32 * i, 32)
+            up_o[at(im * IMG, i, 32), :] = (v * live).astype(bf16)
 
 
 CHAINS = 3
@@ -255,13 +264,13 @@
 def kernel_forward(
     gx, gy, mod_len, small_len, bucket, pos, x_ref, stat, own, oth, es, fe, fo, ge, go,
     q_o, gates_o, mixed_o, z_o, g_o, spec_o, mean_o, wf, wh, wp, vec, bm1, kcat,
-    h_o, normed, ctx, ecat, ocat, s_a, s_b, s_e, s_o, yca, ycb, mix, wide, flat, small, moved, spread,
+    h_o, normed, ctx, ecat, ocat, s_a, s_b, s_e, s_o, yca, ycb, mix, wide, flat, small, moved, spread, turned,
 ):
     step = pl.program_id(0)
 
     @pl.when(step == 0)
     def _():
-        unpack_mod(gx, gy, mod_len, small_len, pos, own, oth, wf, wh, wp, vec, bm1, kcat, flat, small, moved, spread)
+        unpack_mod(gx, gy, mod_len, small_len, pos, own, oth, wf, wh, wp, vec, bm1, kcat, flat, small, moved, spread, turned)
         for lb in range(6):
             h_o[lb] = dot(es[lb], kcat[lb // 2])
 
@@ -282,7 +291,7 @@
     def put_pair(ls, i, top, bot):
         e_hi, e_lo = split(top + bot)
         o_hi, o_lo = split(top - bot)
-        for base, ev, ov in ((0, e_hi, o_hi), (HALF, e_hi, o_hi), (2 * HALF, e_lo, o_lo)):
+        for base, ev, ov in ((0, e_hi, o_hi), (HALF, e_lo, o_lo)):
             ecat[at(base, i), ls] = ev
             ocat[at(base, i), ls] = ov
 
@@ -291,15 +300,19 @@
             for i in range(HALF // 16):
                 put_pair(ls, i, ctx[at(im * IMG, i), hs], ctx[at(im * IMG + HALF, i), hs])
 
+    def terms(ref, width, ts):
+        hi = ref[:width, ts]
+        return jnp.concatenate([hi, hi, ref[width:, ts]], axis=0)
+
     def transform(t):
         ts = slice(t * CHAIN, (t + 1) * CHAIN)
-        s_a[:, ts] = dot(fe[...], ecat[:, ts])
-        s_b[:, ts] = dot(fo[...], ocat[:, ts])
+        s_a[:, ts] = dot(fe[...], terms(ecat, HALF, ts))
+        s_b[:, ts] = dot(fo[...], terms(ocat, HALF, ts))
 
     def back(t):
         ts = slice(t * CHAIN, (t + 1) * CHAIN)
-        s_e[:, ts] = dot(ge[...], yca[:, ts])
-        s_o[:, ts] = dot(go[...], ycb[:, ts])
+        s_e[:, ts] = dot(ge[...], terms(yca, AR, ts))
+        s_o[:, ts] = dot(go[...], terms(ycb, BR, ts))
 
     def filt(t, level):
         base = level * SR
@@ -326,8 +339,7 @@
                 ):
                     hi, lo = split(val)
                     dst[at(off, i), ls] = hi
-                    dst[at(off + width, i), ls] = hi
-                    dst[at(off + 2 * width, i), ls] = lo
+                    dst[at(off + width, i), ls] = lo
             x_re, x_im = s_a[Q : Q + 16, ls], s_a[2 * Q + 16 : 2 * Q + 32, ls]
             spec_o[base + 4 * Q : base + 4 * Q + 16, ls] = x_re.astype(bf16)
             spec_o[base + 4 * Q + 16 : base + 4 * Q + 32, ls] = x_im.astype(bf16)
@@ -335,8 +347,7 @@
             for off, val in ((Q, p_re * x_re - p_im * x_im), (2 * Q + 16, p_re * x_im + p_im * x_re)):
                 hi, lo = split(val)
                 yca[off : off + 16, ls] = hi
-                yca[off + AR : off + AR + 16, ls] = hi
-                yca[off + 2 * AR : off + 2 * AR + 16, ls] = lo
+                yca[off + AR : off + AR + 16, ls] = lo
 
     def act(t, level):
         for im, ls, hs in sub_tiles(t):
@@ -345,7 +356,7 @@
                 even, odd = s_e[at(0, i), ls], s_o[at(0, i), ls]
                 both = []
                 for h, a in ((0, even + odd), (HALF, even - odd)):
-                    z, g = gelu_pair(a)
+                    z, g = gelu_scaled(a)
                     z_o[at(level * IMG + h, i), ls] = z.astype(bf16)
                     g_o[at(level * IMG + h, i), ls] = g.astype(bf16)
                     s = at(im * IMG + h, i)
@@ -781,6 +792,9 @@
 WF_ROWS = C * WIDE // 128
 W_ROWS = C * C // 128
 PERIOD = 32
+PITCH_IMAGE = IMG + 8
+PITCH_Q = 24
+PITCH_P = 40
 STRIDE = PERIOD * WIDE // 128
 K_ROW = 12
 TAIL_ROW = K_ROW + 83 * C // 128
@@ -790,7 +804,22 @@
 END_ROW = B_S2 + 3
 
 
-def unpack_mod(gx, gy, mod_len, small_len, pos, own, oth, wf_o, wh_o, wp_o, vec_o, bm1_o, kcat_o, flat, small, moved, wide):
+def by_threes(flat, base, n, temp, out):
+    for g in range(n // 64):
+        room = 192 * (g % 4)
+        for k in range(8):
+            for b in range(3):
+                src = base + 192 * g + 24 * k + 8 * b
+                temp[pl.ds(room + 64 * b + k, 8, stride=8), :] = flat[src : src + 8, :]
+        for i in range(24):
+            rows_at = 768 + 64 * ((g % 4) * 3 + i % 3) + i // 3
+            temp[pl.ds(rows_at, 8, stride=8), :] = temp[room + 8 * i : room + 8 * i + 8, :]
+        for t in range(3):
+            first = 768 + 64 * ((g % 4) * 3 + t)
+            out[64 * g : 64 * g + 64, 128 * t : 128 * t + 128] = temp[first : first + 64, :].astype(bf16)
+
+
+def unpack_mod(gx, gy, mod_len, small_len, pos, own, oth, wf_o, wh_o, wp_o, vec_o, bm1_o, kcat_o, flat, small, moved, wide, turned):
     flat[...] = jnp.zeros_like(flat)
     small[...] = jnp.zeros_like(small)
     mr, sr = block_rows(mod_len), block_rows(small_len)
@@ -802,20 +831,24 @@
                 flat[pl.ds(first_row(mod_len, d), mr), :] += block[:mr]
                 small[pl.ds(first_row(small_len, d), sr), :] += block[mr : mr + sr]
     lane = lax.broadcasted_iota(jnp.int32, (16, 128), 1)
+    for q in range(C // PERIOD):
+        for f in range(0, STRIDE + 7, 8):
+            turned[pl.ds(PITCH_Q * f + q, 8, stride=PITCH_Q), :] = flat[STRIDE * q + f : STRIDE * q + f + 8, :]
     for p in range(PERIOD):
         row, sh = WIDE * p // 128, WIDE * p % 128
-        tiles = [turn(flat[pl.ds(row + j, 16, stride=STRIDE), :], sh) for j in range(MERGED // 128 + (1 if sh else 0))]
+        first = [PITCH_Q * (row + j) for j in range(MERGED // 128 + (1 if sh else 0))]
+        tiles = [turn(turned[k : k + 16, :], sh) for k in first]
         for j in range(MERGED // 128):
             v = join(tiles[j], tiles[j + 1], sh) if sh else tiles[j]
             if j == MERGED // 128 - 1:
                 v = jnp.where(lane < 4, v, 0.0)
-            wide[j, pl.ds(p, 16, stride=PERIOD), :] = v
+            wide[j, pl.ds(p, 16, stride=PITCH_P), :] = v
     for j in range(MERGED // 128):
-        wf_o[:, 128 * j : 128 * j + 128] = wide[j, :C, :].astype(bf16)
-    for j in range(3):
-        ls = slice(128 * j, 128 * j + 128)
-        wh_o[:, ls] = flat[pl.ds(WF_ROWS + j, C, stride=3), :].astype(bf16)
-        wp_o[:, ls] = flat[pl.ds(WF_ROWS + W_ROWS + j, C, stride=3), :].astype(bf16)
+        for q in range(C // PERIOD):
+            v = wide[j, PITCH_P * q : PITCH_P * q + PERIOD, :]
+            wf_o[PERIOD * q : PERIOD * q + PERIOD, 128 * j : 128 * j + 128] = v.astype(bf16)
+    by_threes(flat, WF_ROWS, C, turned, wh_o)
+    by_threes(flat, WF_ROWS + W_ROWS, C, turned, wp_o)
     n = moved.shape[0]
     moved[...] = join(turn(small[0:n, :], 4), turn(small[1 : n + 1, :], 4), 4)
     vec_o[...] = jnp.zeros_like(vec_o)
@@ -883,13 +916,15 @@
     if flat.shape[0] > used:
         flat[used:, :] = jnp.zeros_like(flat[used:, :])
     for j in range(MERGED // 128):
-        wide[j, :C, :] = gwf[:, 128 * j : 128 * j + 128]
+        for row in range(0, C, 8):
+            dst = pl.ds(PITCH_Q * (row % PERIOD) + row // PERIOD, 8, stride=PITCH_Q)
+            wide[j, dst, :] = gwf[row : row + 8, 128 * j : 128 * j + 128]
     turned = {}
 
     def piece(p, tile):
         tile = min(tile, MERGED // 128 - 1)
         if (p, tile) not in turned:
-            turned[p, tile] = turn(wide[tile, pl.ds(p, 16, stride=PERIOD), :], -WIDE * p % 128)
+            turned[p, tile] = turn(wide[tile, PITCH_Q * p : PITCH_Q * p + 16, :], -WIDE * p % 128)
         return turned[p, tile]
 
     for f in range(STRIDE):
@@ -1006,14 +1041,14 @@
     slots = tokens.shape[2]
     n = slots * IMG
     outs = [(sds((n, w), t), rows(PAIR, w)) for w, t in ((C, bf16), (C, bf16), (128, f32))]
-    return call(kernel_prep, "prep", (slots // 2,), whole(tokens), outs, [native_rows(slots), ((PAIR, C), f32)], 60, 5)
+    return call(kernel_prep, "prep", (slots // 2,), whole(tokens), outs, [((C // 128, slots * PITCH_IMAGE, 128), f32)], 60, 4)
 
 
 def upstream(counts, cotangent):
     slots = cotangent.shape[2]
     ins = [(counts, smem())] + whole(cotangent)
     outs = [(sds((slots * IMG, C), bf16), rows(PAIR, C))]
-    return call(kernel_upstream, "upstream", (slots // 2,), ins, outs, [native_rows(slots), ((PAIR, C), f32)], 60, 4)[0]
+    return call(kernel_upstream, "upstream", (slots // 2,), ins, outs, [((C // 128, slots * PITCH_IMAGE, 128), f32)], 60, 3)[0]
 
 
 def forward(gx, gy, pos, xrow, stat, bucket, own, oth, mod_len, small_len):
@@ -1034,17 +1069,17 @@
     mats = [jnp.asarray(con[k]) for k in ("es", "fe", "fo", "ge", "go")]
     ins = [(bucket, smem()), (pos, smem())] + by_rows(PAIR, xrow, stat) + whole(own, oth, *mats)
     scratch = [
-        ((6, SR, C), f32), ((PAIR, C), bf16), ((PAIR, C), f32), ((3 * HALF, C2), bf16), ((3 * HALF, C2), bf16), ((AR, C2), f32), ((BR, C2), f32),
-        ((HALF, C2), f32), ((HALF, C2), f32), ((3 * AR, C2), bf16), ((3 * BR, C2), bf16), ((PAIR, C), f32),
+        ((6, SR, C), f32), ((PAIR, C), bf16), ((PAIR, C), f32), ((2 * HALF, C2), bf16), ((2 * HALF, C2), bf16), ((AR, C2), f32), ((BR, C2), f32),
+        ((HALF, C2), f32), ((HALF, C2), f32), ((2 * AR, C2), bf16), ((2 * BR, C2), bf16), ((PAIR, C), f32),
         ((4, PAIR, 128), f32),
     ]
     ndev = gx * gy
     flat_rows = max(span(mod_len, ndev), STRIDE * 16 + 8)
     small_rows = max(span(small_len, ndev), END_ROW + 26)
     scratch += [((flat_rows, 128), f32), ((small_rows + 8, 128), f32), ((small_rows, 128), f32)]
-    scratch += [((MERGED // 128, PERIOD * 16, 128), f32)]
+    scratch += [((MERGED // 128, max(PITCH_Q * PERIOD, PITCH_P * 16), 128), f32), ((PITCH_Q * (STRIDE + 7), 128), f32)]
     kernel = functools.partial(kernel_forward, gx, gy, mod_len, small_len)
-    return call(kernel, "focal_forward", (pairs,), ins, outs, scratch, 62, 28)
+    return call(kernel, "focal_forward", (pairs,), ins, outs, scratch, 58, 28)
 
 
 def middle(gx, gy, pos, xrow, up, mixed, q, wh, wp, vec, bm1, mlp_blocks, mlp_len):
@@ -1067,16 +1102,14 @@
         ((C, HID), f32), ((HID, C), f32), ((span(mlp_len, gx * gy), 128), f32), ((C, HID), bf16), ((HID, C), bf16),
     ]
     kernel = functools.partial(kernel_middle, gx, gy, mlp_len)
-    return call(kernel, "middle", (n // BROWS,), ins, outs, scratch, 62, 42)
+    return call(kernel, "middle", (n // BROWS,), ins, outs, scratch, 60, 42)
 
 
 def backward(gx, gy, pos, bucket, nb, dq, dmix, gates, z, g, spec, mean, kcat, wf, vec, sums, bsum, gwh, gwp, mod_len, small_len):
     con = constants()
     ndev = gx * gy
     pairs = nb.shape[0] // PAIR
-    mats = [jnp.asarray(con[k]) for k in ("es", "weights")]
-    mats += [jnp.asarray(con["fe"][:, :HALF]), jnp.asarray(con["fo"][:, :HALF])]
-    mats += [jnp.asarray(con["ge"][:, :AR]), jnp.asarray(con["go"][:, :BR])]
+    mats = [jnp.asarray(con[k]) for k in ("es", "weights", "fe_back", "fo_back", "ge_back", "go_back")]
     slots = (gy // 2, gx, -(-(block_rows(mod_len) + block_rows(small_len)) // 16) * 16, 128)
     outs = [(sds((nb.shape[0], MERGED), bf16), rows(PAIR, MERGED))] + [(sds(slots, bf16), full(slots))] * 2
     ins = [(bucket, smem()), (pos, smem())] + by_rows(PAIR, nb, dq, dmix, gates) + by_rows(3 * IMG, z, g) + by_rows(3 * SR, spec)
@@ -1089,11 +1122,11 @@
         ((HALF, C2), bf16), ((HALF, C2), bf16), ((AR, C2), f32), ((BR, C2), f32), ((HALF, C2), f32), ((HALF, C2), f32),
         ((AR, C2), bf16), ((BR, C2), bf16), ((6, SR, C), f32), ((8, MERGED), f32), ((4, PAIR, 128), f32),
         ((max(span(mod_len, ndev), STRIDE * 16 + 8), 128), f32), ((small_rows, 128), f32), ((small_rows, 128), f32),
-        ((MERGED // 128, PERIOD * 16, 128), f32),
+        ((MERGED // 128, max(PITCH_Q * PERIOD, PITCH_P * 16), 128), f32),
     ]
     scratch += [(v.shape, v.dtype) for v in late] + [pltpu.SemaphoreType.DMA((len(late),))]
     kernel = functools.partial(kernel_backward, gx, gy, mod_len, small_len)
-    return call(kernel, "focal_backward", (pairs,), ins, outs, scratch, 62, 28)
+    return call(kernel, "focal_backward", (pairs,), ins, outs, scratch, 58, 28)
 
 
 def tail(shape, dmer, wf, xrow, stat, dmid, vec):

time: 171 us -> 167 us (0.977)
  Pallas kernels: 116 us -> 113 us
    pallas_call x13, Pallas kernels: 116 us -> 113 us  [call(): pl.pallas_call(kernel, grid=grid, in_specs=[s for _, s in ins], out_shape...]
where the time goes in v2:
time: 167 us
  Pallas kernels  113 us (68%)
  starting transfers between devices  34.1 us (20%)
  waiting for transfers between devices  11.4 us (7%)
  local copies, waits for them, and re-layouts  5.95 us (4%)
    pallas_call x13, Pallas kernels, call(): pl.pallas_call(kernel, grid=grid, in_specs=[s for _, s in ins], out_shape...  113 us
    ppermute x28, starting transfers between devices, swap(): return lax.ppermute(x, AXES, [(k, k ^ mask) for k in range(ndev)])  34.1 us
    ppermute x28, waiting for transfers between devices, swap(): return lax.ppermute(x, AXES, [(k, k ^ mask) for k in range(ndev)])  11.4 us
  transfers between devices with their start and end apart: 28, of which 7 were waited for; matrix products, arithmetic and copies ran while one was open for 0% of the time, Pallas kernels for 43%

profile of v2, /device:TPU:0, one launch (start us, length us, event | category | flops | bytes accessed | tf_op | source)
XLA Modules:
  0.0 166.5 jit_solution(15480960037130561584)
XLA Ops:
  0.7 0.9 dynamic_update_slice.7
  1.6 1.1 dynamic_update_slice.6
  2.8 5.1 %collective-permute-start.2 = (bf16[192,128]{1,0:T(8,128)(2,1)S(1)}, bf16[192,128]{1,0:T(8,128)(2,1)S(1)}, u32[]{:S(2)}, u32[]{:S(2)}) collective-permute-start(bf16[192,128]{1,0:T(8,128)(2,1)S(1)} %maximum_maximum_fusion), channel_id=1, source_target_pairs={{0,24},{1,25},{2,26},{3,27},{4,28},{5,29},{6,30},{7,31},{8,16},{9,... | collective-permute-start | bytes 147464 | tf_op jit(solution)/shard_map/ppermute | solution.py:1152
  8.0 0.6 collective-permute-start
  8.6 4.8 %prep.1 = (bf16[2304,384]{1,0:T(8,128)(2,1)}, bf16[2304,384]{1,0:T(8,128)(2,1)}, f32[2304,128]{1,0:T(8,128)}) custom-call(bf16[14,20,8,384]{3,2,1,0:T(8,128)(2,1)} %bitcast.47), custom_call_target="tpu_custom_call" | custom-call | flops 4000000000 | bytes 4000000 | tf_op jit(solution)/shard_map/prep/pallas_call | solution.py:1015
  14.1 3.8 %collective-permute-start.8 = (bf16[288,128]{1,0:T(8,128)(2,1)S(1)}, bf16[288,128]{1,0:T(8,128)(2,1)S(1)}, u32[]{:S(2)}, u32[]{:S(2)}) collective-permute-start(bf16[288,128]{1,0:T(8,128)(2,1)S(1)} %bitcast.36), channel_id=1, source_target_pairs={{0,24},{1,25},{2,26},{3,27},{4,28},{5,29},{6,30},{7,31},{8,16},{9,... | collective-permute-start | bytes 221192 | tf_op jit(solution)/shard_map/ppermute | solution.py:1152
  17.9 0.6 collective-permute-start.6
  18.6 2.7 %collective-permute-start.5 = (bf16[4,192,128]{2,1,0:T(8,128)(2,1)S(1)}, bf16[4,192,128]{2,1,0:T(8,128)(2,1)S(1)}, u32[]{:S(2)}, u32[]{:S(2)}) collective-permute-start(bf16[4,192,128]{2,1,0:T(8,128)(2,1)S(1)} %pad_maximum_fusion.3), channel_id=1, source_target_pairs={{0,6},{1,7},{2,4},{3,5},{4,2},{5,3},{6,0},{7,1},{8,14},{9,15},{10,... | collective-permute-start | bytes 589832 | tf_op jit(solution)/shard_map/ppermute | solution.py:1152
  21.3 0.5 collective-permute-start.4
  21.8 0.4 collective-permute-start.3
  22.2 3.9 %upstream.1.up = bf16[2304,384]{1,0:T(8,128)(2,1)} custom-call(s32[1]{0:T(128)S(6)} %copy.25.counts, bf16[14,20,8,384]{3,2,1,0:T(8,128)(2,1)} %bitcast.48), custom_call_target="tpu_custom_call" | custom-call | flops 3000000000 | bytes 3000000 | tf_op jit(solution)/shard_map/upstream/pallas_call | solution.py:1015
  26.1 1.2 collective-permute-done.5
  27.3 1.7 %collective-permute-done.4 = bf16[4,192,128]{2,1,0:T(8,128)(2,1)S(1)} collective-permute-done((bf16[4,192,128]{2,1,0:T(8,128)(2,1)S(1)}, bf16[4,192,128]{2,1,0:T(8,128)(2,1)S(1)}, u32[]{:S(2)}, u32[]{:S(2)}) %collective-permute-start.4) | collective-permute-done | bytes 196640 | tf_op jit(solution)/shard_map/ppermute | solution.py:1152
  29.3 0.5 collective-permute-start.10
  29.8 0.6 pad_add_fusion.pos
  30.4 1.6 collective-permute-done.10
  32.1 1.7 %collective-permute-start.13 = (bf16[2,4,288,128]{3,2,1,0:T(8,128)(2,1)S(1)}, bf16[2,4,288,128]{3,2,1,0:T(8,128)(2,1)S(1)}, u32[]{:S(2)}, u32[]{:S(2)}) collective-permute-start(bf16[2,4,288,128]{3,2,1,0:T(8,128)(2,1)S(1)} %pad_maximum_fusion.1.refs_0_), channel_id=1, source_target_pairs={{0,6},{1,7},{2,4},{3,5},{4,2},{5,3},{6,0},{7,1},{8,14},{9,15},{10,... | collective-permute-start | bytes 1769480 | tf_op jit(solution)/shard_map/ppermute | solution.py:1152
  33.8 1.3 collective-permute-start.12
  35.1 0.5 collective-permute-start.11
  35.7 26.3 %focal_forward.1 = (f32[2304,384]{1,0:T(8,128)}, f32[2304,128]{1,0:T(8,128)}, bf16[2304,384]{1,0:T(8,128)(2,1)}, bf16[3456,768]{1,0:T(8,128)(2,1)}, bf16[3456,76...) custom-call(s32[8]{0:T(128)} %bucket.3, ...), custom_call_target="tpu_custom_call" | custom-call | flops 28000000000 | bytes 28000000 | tf_op jit(solution)/shard_map/focal_forward/pallas_call | solution.py:1015
  62.1 0.8 copy-done.13
  62.8 0.2 copy-done.14
  63.0 0.2 copy-done.15
  63.2 41.0 %middle.1 = (f32[2304,384]{1,0:T(8,128)}, bf16[2304,384]{1,0:T(8,128)(2,1)}, bf16[2304,384]{1,0:T(8,128)(2,1)}, f32[2304,384]{1,0:T(8,128)}, bf16[4,4,288,128]{3...) custom-call(s32[2]{0:T(128)} %pad_add_fusion.pos, ...), custom_call_target="tpu_custom_call" | custom-call | flops 41999998976 | bytes 42000000 | tf_op jit(solution)/shard_map/middle/pallas_call | solution.py:1015
  104.3 3.0 %collective-permute-done.14.refs_1_ = bf16[4,4,288,128]{3,2,1,0:T(8,128)(2,1)S(1)} collective-permute-done((bf16[4,4,288,128]{3,2,1,0:T(8,128)(2,1)}, bf16[4,4,288,128]{3,2,1,0:T(8,128)(2,1)S(1)}, u32[]{:S(2)}, u32[]{:S(2)}) %collective-permute-start.14) | collective-permute-done | bytes 1179680 | tf_op jit(solution)/shard_map/ppermute | solution.py:1152
  107.4 1.3 copy-done
  108.7 0.3 mlp_sum_core.1
  108.9 1.6 collective-permute-start.15
  110.5 0.7 collective-permute-start.16
  111.2 1.3 collective-permute-start.17
  112.5 25.6 %focal_backward.1 = (bf16[2304,896]{1,0:T(8,128)(2,1)}, bf16[4,4,192,128]{3,2,1,0:T(8,128)(2,1)}, bf16[4,4,192,128]{3,2,1,0:T(8,128)(2,1)}) custom-call(s32[8]{0:T(128)} %bucket.3, s32[2]{0:T(128)} %pad_add_fusion.pos, bf16[2304,384]{1,0:T(8,128)(2,1)} %get-tuple-element.140.nb_ref, bf16[2304,384]{1,0:T(8,128)(2,1)} %get-tuple-element.141.dq_ref, ...), custom_call_target="tpu_custom_call" | custom-call | flops 28000000000 | bytes 28000000 | tf_op jit(solution)/shard_map/focal_backward/pallas_call | solution.py:1015
  138.4 1.4 collective-permute-start.22
  139.8 2.6 %collective-permute-start.23 = (bf16[288,128]{1,0:T(8,128)(2,1)S(1)}, bf16[288,128]{1,0:T(8,128)(2,1)S(1)}, u32[]{:S(2)}, u32[]{:S(2)}) collective-permute-start(bf16[288,128]{1,0:T(8,128)(2,1)S(1)} %get-tuple-element.168), channel_id=1, source_target_pairs={{0,16},{1,17},{2,18},{3,19},{4,20},{5,21},{6,22},{7,23},{8,24},{9,... | collective-permute-start | bytes 221192 | tf_op jit(solution)/shard_map/ppermute | solution.py:1152
  142.5 0.4 collective-permute-start.24
  142.9 0.2 mod_sum_core.1
  143.1 1.6 collective-permute-start.19
  144.6 0.7 collective-permute-start.20
  145.3 1.3 collective-permute-start.21
  146.7 6.8 %tail.1 = f32[14,20,8,384]{3,2,1,0:T(8,128)} custom-call(bf16[2304,896]{1,0:T(8,128)(2,1)S(1)} %copy-done.2, bf16[384,896]{1,0:T(8,128)(2,1)S(1)} %copy-done.7, bf16[2304,384]{1,0:T(8,128)(2,1)S(1)} %copy-done.4, f32[2304,128]{1,0:T(8,128)S(1)} %copy-done.6, f32[2304,384]{1,0:T(8,128)S(1)} %copy-done.3, f32[16,384]{1,0:T(8,128)S(1)} %copy-done.8), custom_call_target="tpu_custom_call" | custom-call | flops 8000000000 | bytes 8000000 | tf_op jit(solution)/shard_map/tail/pallas_call | solution.py:1015
  153.5 1.5 collective-permute-done.20.refs_2_
  155.1 0.6 collective-permute-start.25
  155.7 3.5 %collective-permute-start.26 = (bf16[192,128]{1,0:T(8,128)(2,1)S(1)}, bf16[192,128]{1,0:T(8,128)(2,1)S(1)}, u32[]{:S(2)}, u32[]{:S(2)}) collective-permute-start(bf16[192,128]{1,0:T(8,128)(2,1)S(1)} %get-tuple-element.179), channel_id=1, source_target_pairs={{0,16},{1,17},{2,18},{3,19},{4,20},{5,21},{6,22},{7,23},{8,24},{9,... | collective-permute-start | bytes 147464 | tf_op jit(solution)/shard_map/ppermute | solution.py:1152
  159.2 0.4 collective-permute-start.27
  159.6 2.6 %out_tokens.1 = bf16[14,20,8,384]{3,2,1,0:T(8,128)(2,1)} custom-call(s32[1]{0:T(128)S(6)} %copy.25.counts, bf16[2304,384]{1,0:T(8,128)(2,1)S(1)} %copy-done.5), custom_call_target="tpu_custom_call" | custom-call | flops 5000000000 | bytes 5000000 | tf_op jit(solution)/shard_map/out_tokens/pallas_call | solution.py:1015
  162.2 0.7 mlp_sum_line.1
  162.9 2.2 %collective-permute-done.27.refs_3_ = bf16[192,128]{1,0:T(8,128)(2,1)S(1)} collective-permute-done((bf16[192,128]{1,0:T(8,128)(2,1)S(1)}, bf16[192,128]{1,0:T(8,128)(2,1)S(1)}, u32[]{:S(2)}, u32[]{:S(2)}) %collective-permute-start.27) | collective-permute-done | bytes 49184 | tf_op jit(solution)/shard_map/ppermute | solution.py:1152
  165.1 0.7 dynamic_slice.6
  165.9 0.7 dynamic_slice.7
  (67 shorter events, 1.1 us)
Async XLA Ops:
  2.8 11.2 %collective-permute-start.2 = (bf16[192,128]{1,0:T(8,128)(2,1)S(1)}, bf16[192,128]{1,0:T(8,128)(2,1)S(1)}, u32[]{:S(2)}, u32[]{:S(2)}) collective-permute-start(bf16[192,128]{1,0:T(8,128)(2,1)S(1)} %maximum_maximum_fusion), channel_id=1, source_target_pairs={{0,24},{1,25},{2,26},{3,27},{4,28},{5,29},{6,30},{7,31},{8,16},{9,... | collective-permute-start | bytes 147464 | tf_op jit(solution)/shard_map/ppermute | solution.py:1152
  8.0 6.1 %collective-permute-start.1 = (bf16[192,128]{1,0:T(8,128)(2,1)S(1)}, bf16[192,128]{1,0:T(8,128)(2,1)S(1)}, u32[]{:S(2)}, u32[]{:S(2)}) collective-permute-start(bf16[192,128]{1,0:T(8,128)(2,1)S(1)} %maximum_maximum_fusion), channel_id=1, source_target_pairs={{0,16},{1,17},{2,18},{3,19},{4,20},{5,21},{6,22},{7,23},{8,24},{9,... | collective-permute-start | bytes 147464 | tf_op jit(solution)/shard_map/ppermute | solution.py:1152
  8.0 6.1 %collective-permute-start = (bf16[192,128]{1,0:T(8,128)(2,1)S(1)}, bf16[192,128]{1,0:T(8,128)(2,1)S(1)}, u32[]{:S(2)}, u32[]{:S(2)}) collective-permute-start(bf16[192,128]{1,0:T(8,128)(2,1)S(1)} %maximum_maximum_fusion), channel_id=1, source_target_pairs={{0,8},{1,9},{2,10},{3,11},{4,12},{5,13},{6,14},{7,15},{8,0},{9,1},... | collective-permute-start | bytes 147464 | tf_op jit(solution)/shard_map/ppermute | solution.py:1152
  8.6 5.5 %copy-start.11 = (bf16[36864]{0:T(1024)(128)(2,1)S(1)}, bf16[36864]{0:T(1024)(128)(2,1)}, u32[]{:S(2)}) copy-start(bf16[36864]{0:T(1024)(128)(2,1)} %param.22) | copy-start | bytes 221188
  14.1 7.7 %collective-permute-start.8 = (bf16[288,128]{1,0:T(8,128)(2,1)S(1)}, bf16[288,128]{1,0:T(8,128)(2,1)S(1)}, u32[]{:S(2)}, u32[]{:S(2)}) collective-permute-start(bf16[288,128]{1,0:T(8,128)(2,1)S(1)} %bitcast.36), channel_id=1, source_target_pairs={{0,24},{1,25},{2,26},{3,27},{4,28},{5,29},{6,30},{7,31},{8,16},{9,... | collective-permute-start | bytes 221192 | tf_op jit(solution)/shard_map/ppermute | solution.py:1152
  17.9 8.1 %collective-permute-start.7 = (bf16[288,128]{1,0:T(8,128)(2,1)S(1)}, bf16[288,128]{1,0:T(8,128)(2,1)S(1)}, u32[]{:S(2)}, u32[]{:S(2)}) collective-permute-start(bf16[288,128]{1,0:T(8,128)(2,1)S(1)} %bitcast.37), channel_id=1, source_target_pairs={{0,16},{1,17},{2,18},{3,19},{4,20},{5,21},{6,22},{7,23},{8,24},{9,... | collective-permute-start | bytes 221192 | tf_op jit(solution)/shard_map/ppermute | solution.py:1152
  17.9 8.1 %collective-permute-start.6 = (bf16[288,128]{1,0:T(8,128)(2,1)S(1)}, bf16[288,128]{1,0:T(8,128)(2,1)S(1)}, u32[]{:S(2)}, u32[]{:S(2)}) collective-permute-start(bf16[288,128]{1,0:T(8,128)(2,1)S(1)} %bitcast.38), channel_id=1, source_target_pairs={{0,8},{1,9},{2,10},{3,11},{4,12},{5,13},{6,14},{7,15},{8,0},{9,1},... | collective-permute-start | bytes 221192 | tf_op jit(solution)/shard_map/ppermute | solution.py:1152
  18.6 8.7 %collective-permute-start.5 = (bf16[4,192,128]{2,1,0:T(8,128)(2,1)S(1)}, bf16[4,192,128]{2,1,0:T(8,128)(2,1)S(1)}, u32[]{:S(2)}, u32[]{:S(2)}) collective-permute-start(bf16[4,192,128]{2,1,0:T(8,128)(2,1)S(1)} %pad_maximum_fusion.3), channel_id=1, source_target_pairs={{0,6},{1,7},{2,4},{3,5},{4,2},{5,3},{6,0},{7,1},{8,14},{9,15},{10,... | collective-permute-start | bytes 589832 | tf_op jit(solution)/shard_map/ppermute | solution.py:1152
  21.3 7.8 %collective-permute-start.4 = (bf16[4,192,128]{2,1,0:T(8,128)(2,1)S(1)}, bf16[4,192,128]{2,1,0:T(8,128)(2,1)S(1)}, u32[]{:S(2)}, u32[]{:S(2)}) collective-permute-start(bf16[4,192,128]{2,1,0:T(8,128)(2,1)S(1)} %pad_maximum_fusion.3), channel_id=1, source_target_pairs={{0,4},{1,5},{2,6},{3,7},{4,0},{5,1},{6,2},{7,3},{8,12},{9,13},{10,... | collective-permute-start | bytes 589832 | tf_op jit(solution)/shard_map/ppermute | solution.py:1152
  21.8 7.3 %collective-permute-start.3 = (bf16[4,192,128]{2,1,0:T(8,128)(2,1)S(1)}, bf16[4,192,128]{2,1,0:T(8,128)(2,1)S(1)}, u32[]{:S(2)}, u32[]{:S(2)}) collective-permute-start(bf16[4,192,128]{2,1,0:T(8,128)(2,1)S(1)} %pad_maximum_fusion.3), channel_id=1, source_target_pairs={{0,2},{1,3},{2,0},{3,1},{4,6},{5,7},{6,4},{7,5},{8,10},{9,11},{10,... | collective-permute-start | bytes 589832 | tf_op jit(solution)/shard_map/ppermute | solution.py:1152
  29.2 6.4 %copy-start.9 = (bf16[4,4,192,128]{3,2,1,0:T(8,128)(2,1)}, bf16[4,4,192,128]{3,2,1,0:T(8,128)(2,1)S(1)}, u32[]{:S(2)}) copy-start(bf16[4,4,192,128]{3,2,1,0:T(8,128)(2,1)S(1)} %pad_maximum_fusion.own) | copy-start | bytes 2359300
  29.2 2.8 %collective-permute-start.9 = (bf16[4,4,192,128]{3,2,1,0:T(8,128)(2,1)S(1)}, bf16[4,4,192,128]{3,2,1,0:T(8,128)(2,1)S(1)}, u32[]{:S(2)}, u32[]{:S(2)}) collective-permute-start(bf16[4,4,192,128]{3,2,1,0:T(8,128)(2,1)S(1)} %pad_maximum_fusion.own), channel_id=1, source_target_pairs={{0,1},{1,0},{2,3},{3,2},{4,5},{5,4},{6,7},{7,6},{8,9},{9,8},{10,11... | collective-permute-start | bytes 2359304 | tf_op jit(solution)/shard_map/ppermute | solution.py:1152
  29.3 2.7 %collective-permute-start.10 = (bf16[4,288,128]{2,1,0:T(8,128)(2,1)S(1)}, bf16[4,288,128]{2,1,0:T(8,128)(2,1)S(1)}, u32[]{:S(2)}, u32[]{:S(2)}) collective-permute-start(bf16[4,288,128]{2,1,0:T(8,128)(2,1)S(1)} %pad_maximum_fusion.2), channel_id=1, source_target_pairs={{0,1},{1,0},{2,3},{3,2},{4,5},{5,4},{6,7},{7,6},{8,9},{9,8},{10,11... | collective-permute-start | bytes 884744 | tf_op jit(solution)/shard_map/ppermute | solution.py:1152
  32.1 29.9 %copy-start.10 = (bf16[2,4,288,128]{3,2,1,0:T(8,128)(2,1)}, bf16[2,4,288,128]{3,2,1,0:T(8,128)(2,1)S(1)}, u32[]{:S(2)}) copy-start(bf16[2,4,288,128]{3,2,1,0:T(8,128)(2,1)S(1)} %pad_maximum_fusion.1.refs_0_) | copy-start | bytes 1769476
  32.1 3.6 %copy-start.12 = (bf16[4,4,192,128]{3,2,1,0:T(8,128)(2,1)}, bf16[4,4,192,128]{3,2,1,0:T(8,128)(2,1)S(1)}, u32[]{:S(2)}) copy-start(bf16[4,4,192,128]{3,2,1,0:T(8,128)(2,1)S(1)} %collective-permute-done.9.oth) | copy-start | bytes 2359300
  32.1 29.9 %collective-permute-start.13 = (bf16[2,4,288,128]{3,2,1,0:T(8,128)(2,1)S(1)}, bf16[2,4,288,128]{3,2,1,0:T(8,128)(2,1)S(1)}, u32[]{:S(2)}, u32[]{:S(2)}) collective-permute-start(bf16[2,4,288,128]{3,2,1,0:T(8,128)(2,1)S(1)} %pad_maximum_fusion.1.refs_0_), channel_id=1, source_target_pairs={{0,6},{1,7},{2,4},{3,5},{4,2},{5,3},{6,0},{7,1},{8,14},{9,15},{10,... | collective-permute-start | bytes 1769480 | tf_op jit(solution)/shard_map/ppermute | solution.py:1152
  33.8 28.2 %collective-permute-start.12 = (bf16[2,4,288,128]{3,2,1,0:T(8,128)(2,1)S(1)}, bf16[2,4,288,128]{3,2,1,0:T(8,128)(2,1)S(1)}, u32[]{:S(2)}, u32[]{:S(2)}) collective-permute-start(bf16[2,4,288,128]{3,2,1,0:T(8,128)(2,1)S(1)} %pad_maximum_fusion.1.refs_0_), channel_id=1, source_target_pairs={{0,4},{1,5},{2,6},{3,7},{4,0},{5,1},{6,2},{7,3},{8,12},{9,13},{10,... | collective-permute-start | bytes 1769480 | tf_op jit(solution)/shard_map/ppermute | solution.py:1152
  35.1 26.9 %collective-permute-start.11 = (bf16[2,4,288,128]{3,2,1,0:T(8,128)(2,1)S(1)}, bf16[2,4,288,128]{3,2,1,0:T(8,128)(2,1)S(1)}, u32[]{:S(2)}, u32[]{:S(2)}) collective-permute-start(bf16[2,4,288,128]{3,2,1,0:T(8,128)(2,1)S(1)} %pad_maximum_fusion.1.refs_0_), channel_id=1, source_target_pairs={{0,2},{1,3},{2,0},{3,1},{4,6},{5,7},{6,4},{7,5},{8,10},{9,11},{10,... | collective-permute-start | bytes 1769480 | tf_op jit(solution)/shard_map/ppermute | solution.py:1152
  62.0 0.8 copy-start.13
  62.0 1.0 copy-start.14
  62.1 1.1 copy-start.15
  104.3 3.1 %collective-permute-start.14 = (bf16[4,4,288,128]{3,2,1,0:T(8,128)(2,1)}, bf16[4,4,288,128]{3,2,1,0:T(8,128)(2,1)S(1)}, u32[]{:S(2)}, u32[]{:S(2)}) collective-permute-start(bf16[4,4,288,128]{3,2,1,0:T(8,128)(2,1)} %get-tuple-element.130), channel_id=1, source_target_pairs={{0,1},{1,0},{2,3},{3,2},{4,5},{5,4},{6,7},{7,6},{8,9},{9,8},{10,11... | collective-permute-start | bytes 3538952 | tf_op jit(solution)/shard_map/ppermute | solution.py:1152
  107.4 1.3 copy-start
  108.9 29.2 %collective-permute-start.15 = (bf16[4,288,128]{2,1,0:T(8,128)(2,1)S(1)}, bf16[4,288,128]{2,1,0:T(8,128)(2,1)S(1)}, u32[]{:S(2)}, u32[]{:S(2)}) collective-permute-start(bf16[4,288,128]{2,1,0:T(8,128)(2,1)S(1)} %get-tuple-element.137), channel_id=1, source_target_pairs={{0,2},{1,3},{2,0},{3,1},{4,6},{5,7},{6,4},{7,5},{8,10},{9,11},{10,... | collective-permute-start | bytes 884744 | tf_op jit(solution)/shard_map/ppermute | solution.py:1152
  110.5 27.6 %collective-permute-start.16 = (bf16[4,288,128]{2,1,0:T(8,128)(2,1)S(1)}, bf16[4,288,128]{2,1,0:T(8,128)(2,1)S(1)}, u32[]{:S(2)}, u32[]{:S(2)}) collective-permute-start(bf16[4,288,128]{2,1,0:T(8,128)(2,1)S(1)} %get-tuple-element.138), channel_id=1, source_target_pairs={{0,4},{1,5},{2,6},{3,7},{4,0},{5,1},{6,2},{7,3},{8,12},{9,13},{10,... | collective-permute-start | bytes 884744 | tf_op jit(solution)/shard_map/ppermute | solution.py:1152
  111.2 26.9 %collective-permute-start.17 = (bf16[4,288,128]{2,1,0:T(8,128)(2,1)S(1)}, bf16[4,288,128]{2,1,0:T(8,128)(2,1)S(1)}, u32[]{:S(2)}, u32[]{:S(2)}) collective-permute-start(bf16[4,288,128]{2,1,0:T(8,128)(2,1)S(1)} %get-tuple-element.139), channel_id=1, source_target_pairs={{0,6},{1,7},{2,4},{3,5},{4,2},{5,3},{6,0},{7,1},{8,14},{9,15},{10,... | collective-permute-start | bytes 884744 | tf_op jit(solution)/shard_map/ppermute | solution.py:1152
  138.1 4.8 %copy-start.1 = (bf16[4,4,192,128]{3,2,1,0:T(8,128)(2,1)S(1)}, bf16[4,4,192,128]{3,2,1,0:T(8,128)(2,1)}, u32[]{:S(2)}) copy-start(bf16[4,4,192,128]{3,2,1,0:T(8,128)(2,1)} %get-tuple-element.156.refs_0_) | copy-start | bytes 2359300
  138.1 4.8 %collective-permute-start.18 = (bf16[4,4,192,128]{3,2,1,0:T(8,128)(2,1)}, bf16[4,4,192,128]{3,2,1,0:T(8,128)(2,1)S(1)}, u32[]{:S(2)}, u32[]{:S(2)}) collective-permute-start(bf16[4,4,192,128]{3,2,1,0:T(8,128)(2,1)} %get-tuple-element.157), channel_id=1, source_target_pairs={{0,1},{1,0},{2,3},{3,2},{4,5},{5,4},{6,7},{7,6},{8,9},{9,8},{10,11... | collective-permute-start | bytes 2359304 | tf_op jit(solution)/shard_map/ppermute | solution.py:1152
  138.2 8.4 %copy-start.3 = (f32[2304,384]{1,0:T(8,128)S(1)}, f32[2304,384]{1,0:T(8,128)}, u32[]{:S(2)}) copy-start(f32[2304,384]{1,0:T(8,128)} %get-tuple-element.171.dmid) | copy-start | bytes 10616836
  138.2 8.4 %copy-start.7 = (bf16[384,896]{1,0:T(8,128)(2,1)S(1)}, bf16[384,896]{1,0:T(8,128)(2,1)}, u32[]{:S(2)}) copy-start(bf16[384,896]{1,0:T(8,128)(2,1)} %get-tuple-element.151.wf_far.wf) | copy-start | bytes 2064388
  138.4 7.0 %collective-permute-start.22 = (bf16[288,128]{1,0:T(8,128)(2,1)S(1)}, bf16[288,128]{1,0:T(8,128)(2,1)S(1)}, u32[]{:S(2)}, u32[]{:S(2)}) collective-permute-start(bf16[288,128]{1,0:T(8,128)(2,1)S(1)} %get-tuple-element.167), channel_id=1, source_target_pairs={{0,8},{1,9},{2,10},{3,11},{4,12},{5,13},{6,14},{7,15},{8,0},{9,1},... | collective-permute-start | bytes 221192 | tf_op jit(solution)/shard_map/ppermute | solution.py:1152
  139.8 13.7 %collective-permute-start.23 = (bf16[288,128]{1,0:T(8,128)(2,1)S(1)}, bf16[288,128]{1,0:T(8,128)(2,1)S(1)}, u32[]{:S(2)}, u32[]{:S(2)}) collective-permute-start(bf16[288,128]{1,0:T(8,128)(2,1)S(1)} %get-tuple-element.168), channel_id=1, source_target_pairs={{0,16},{1,17},{2,18},{3,19},{4,20},{5,21},{6,22},{7,23},{8,24},{9,... | collective-permute-start | bytes 221192 | tf_op jit(solution)/shard_map/ppermute | solution.py:1152
  142.4 4.2 %copy-start.2 = (bf16[2304,896]{1,0:T(8,128)(2,1)S(1)}, bf16[2304,896]{1,0:T(8,128)(2,1)}, u32[]{:S(2)}) copy-start(bf16[2304,896]{1,0:T(8,128)(2,1)} %get-tuple-element.170.dmer) | copy-start | bytes 12386308
  142.4 4.2 %copy-start.4 = (bf16[2304,384]{1,0:T(8,128)(2,1)S(1)}, bf16[2304,384]{1,0:T(8,128)(2,1)}, u32[]{:S(2)}) copy-start(bf16[2304,384]{1,0:T(8,128)(2,1)} %get-tuple-element.103.x_ref) | copy-start | bytes 5308420
  142.5 4.2 %copy-start.6 = (f32[2304,128]{1,0:T(8,128)S(1)}, f32[2304,128]{1,0:T(8,128)}, u32[]{:S(2)}) copy-start(f32[2304,128]{1,0:T(8,128)} %get-tuple-element.116.stat) | copy-start | bytes 3538948
  142.5 4.2 %copy-start.8 = (f32[16,384]{1,0:T(8,128)S(1)}, f32[16,384]{1,0:T(8,128)}, u32[]{:S(2)}) copy-start(f32[16,384]{1,0:T(8,128)} %get-tuple-element.123.vec) | copy-start | bytes 73732
  142.5 11.0 %collective-permute-start.24 = (bf16[288,128]{1,0:T(8,128)(2,1)S(1)}, bf16[288,128]{1,0:T(8,128)(2,1)S(1)}, u32[]{:S(2)}, u32[]{:S(2)}) collective-permute-start(bf16[288,128]{1,0:T(8,128)(2,1)S(1)} %get-tuple-element.169), channel_id=1, source_target_pairs={{0,24},{1,25},{2,26},{3,27},{4,28},{5,29},{6,30},{7,31},{8,16},{9,... | collective-permute-start | bytes 221192 | tf_op jit(solution)/shard_map/ppermute | solution.py:1152
  143.1 10.4 %collective-permute-start.19 = (bf16[4,192,128]{2,1,0:T(8,128)(2,1)S(1)}, bf16[4,192,128]{2,1,0:T(8,128)(2,1)S(1)}, u32[]{:S(2)}, u32[]{:S(2)}) collective-permute-start(bf16[4,192,128]{2,1,0:T(8,128)(2,1)S(1)} %get-tuple-element.159), channel_id=1, source_target_pairs={{0,2},{1,3},{2,0},{3,1},{4,6},{5,7},{6,4},{7,5},{8,10},{9,11},{10,... | collective-permute-start | bytes 589832 | tf_op jit(solution)/shard_map/ppermute | solution.py:1152
  144.6 10.4 %collective-permute-start.20 = (bf16[4,192,128]{2,1,0:T(8,128)(2,1)S(1)}, bf16[4,192,128]{2,1,0:T(8,128)(2,1)S(1)}, u32[]{:S(2)}, u32[]{:S(2)}) collective-permute-start(bf16[4,192,128]{2,1,0:T(8,128)(2,1)S(1)} %get-tuple-element.160), channel_id=1, source_target_pairs={{0,4},{1,5},{2,6},{3,7},{4,0},{5,1},{6,2},{7,3},{8,12},{9,13},{10,... | collective-permute-start | bytes 589832 | tf_op jit(solution)/shard_map/ppermute | solution.py:1152
  145.3 9.7 %collective-permute-start.21 = (bf16[4,192,128]{2,1,0:T(8,128)(2,1)S(1)}, bf16[4,192,128]{2,1,0:T(8,128)(2,1)S(1)}, u32[]{:S(2)}, u32[]{:S(2)}) collective-permute-start(bf16[4,192,128]{2,1,0:T(8,128)(2,1)S(1)} %get-tuple-element.161), channel_id=1, source_target_pairs={{0,6},{1,7},{2,4},{3,5},{4,2},{5,3},{6,0},{7,1},{8,14},{9,15},{10,... | collective-permute-start | bytes 589832 | tf_op jit(solution)/shard_map/ppermute | solution.py:1152
  155.0 4.6 %copy-start.5 = (bf16[2304,384]{1,0:T(8,128)(2,1)S(1)}, bf16[2304,384]{1,0:T(8,128)(2,1)}, u32[]{:S(2)}) copy-start(bf16[2304,384]{1,0:T(8,128)(2,1)} %get-tuple-element.181.rows_ref) | copy-start | bytes 5308420
  155.1 7.8 %collective-permute-start.25 = (bf16[192,128]{1,0:T(8,128)(2,1)S(1)}, bf16[192,128]{1,0:T(8,128)(2,1)S(1)}, u32[]{:S(2)}, u32[]{:S(2)}) collective-permute-start(bf16[192,128]{1,0:T(8,128)(2,1)S(1)} %get-tuple-element.178), channel_id=1, source_target_pairs={{0,8},{1,9},{2,10},{3,11},{4,12},{5,13},{6,14},{7,15},{8,0},{9,1},... | collective-permute-start | bytes 147464 | tf_op jit(solution)/shard_map/ppermute | solution.py:1152
  155.7 7.2 %collective-permute-start.26 = (bf16[192,128]{1,0:T(8,128)(2,1)S(1)}, bf16[192,128]{1,0:T(8,128)(2,1)S(1)}, u32[]{:S(2)}, u32[]{:S(2)}) collective-permute-start(bf16[192,128]{1,0:T(8,128)(2,1)S(1)} %get-tuple-element.179), channel_id=1, source_target_pairs={{0,16},{1,17},{2,18},{3,19},{4,20},{5,21},{6,22},{7,23},{8,24},{9,... | collective-permute-start | bytes 147464 | tf_op jit(solution)/shard_map/ppermute | solution.py:1152
  159.2 5.9 %collective-permute-start.27 = (bf16[192,128]{1,0:T(8,128)(2,1)S(1)}, bf16[192,128]{1,0:T(8,128)(2,1)S(1)}, u32[]{:S(2)}, u32[]{:S(2)}) collective-permute-start(bf16[192,128]{1,0:T(8,128)(2,1)S(1)} %get-tuple-element.180), channel_id=1, source_target_pairs={{0,24},{1,25},{2,26},{3,27},{4,28},{5,29},{6,30},{7,31},{8,16},{9,... | collective-permute-start | bytes 147464 | tf_op jit(solution)/shard_map/ppermute | solution.py:1152

commit v3 on v2

--- a/solution.py
+++ b/solution.py
@@ -288,31 +288,38 @@
     spread_gates(gates_o, wide)
     lbs = [[level * 2 + bucket[step * 2 + im] for im in range(2)] for level in range(3)]
 
-    def put_pair(ls, i, top, bot):
-        e_hi, e_lo = split(top + bot)
-        o_hi, o_lo = split(top - bot)
-        for base, ev, ov in ((0, e_hi, o_hi), (HALF, e_lo, o_lo)):
-            ecat[at(base, i), ls] = ev
-            ocat[at(base, i), ls] = ov
+    def put(dst, off, width, ls, i, val, level):
+        if level == 2:
+            dst[at(off, i), ls] = val.astype(bf16)
+            return
+        hi, lo = split(val)
+        dst[at(off, i), ls] = hi
+        dst[at(off + width, i), ls] = lo
+
+    def put_pair(ls, i, top, bot, level):
+        put(ecat, 0, HALF, ls, i, top + bot, level)
+        put(ocat, 0, HALF, ls, i, top - bot, level)
 
     def first(t):
         for im, ls, hs in sub_tiles(t):
             for i in range(HALF // 16):
-                put_pair(ls, i, ctx[at(im * IMG, i), hs], ctx[at(im * IMG + HALF, i), hs])
-
-    def terms(ref, width, ts):
+                put_pair(ls, i, ctx[at(im * IMG, i), hs], ctx[at(im * IMG + HALF, i), hs], 0)
+
+    def product(mat, ref, width, ts, level):
         hi = ref[:width, ts]
-        return jnp.concatenate([hi, hi, ref[width:, ts]], axis=0)
-
-    def transform(t):
+        if level == 2:
+            return dot(mat[:, :width], hi)
+        return dot(mat[...], jnp.concatenate([hi, hi, ref[width:, ts]], axis=0))
+
+    def transform(t, level):
         ts = slice(t * CHAIN, (t + 1) * CHAIN)
-        s_a[:, ts] = dot(fe[...], terms(ecat, HALF, ts))
-        s_b[:, ts] = dot(fo[...], terms(ocat, HALF, ts))
-
-    def back(t):
+        s_a[:, ts] = product(fe, ecat, HALF, ts, level)
+        s_b[:, ts] = product(fo, ocat, HALF, ts, level)
+
+    def back(t, level):
         ts = slice(t * CHAIN, (t + 1) * CHAIN)
-        s_e[:, ts] = dot(ge[...], terms(yca, AR, ts))
-        s_o[:, ts] = dot(go[...], terms(ycb, BR, ts))
+        s_e[:, ts] = product(ge, yca, AR, ts, level)
+        s_o[:, ts] = product(go, ycb, BR, ts, level)
 
     def filt(t, level):
         base = level * SR
@@ -337,17 +344,13 @@
                     (ycb, 0, BR, ym_im - yp_im),
                     (ycb, Q, BR, yp_re - ym_re),
                 ):
-                    hi, lo = split(val)
-                    dst[at(off, i), ls] = hi
-                    dst[at(off + width, i), ls] = lo
+                    put(dst, off, width, ls, i, val, level)
             x_re, x_im = s_a[Q : Q + 16, ls], s_a[2 * Q + 16 : 2 * Q + 32, ls]
             spec_o[base + 4 * Q : base + 4 * Q + 16, ls] = x_re.astype(bf16)
             spec_o[base + 4 * Q + 16 : base + 4 * Q + 32, ls] = x_im.astype(bf16)
             p_re, p_im = h_o[lb, 4 * Q : 4 * Q + 16, hs], h_o[lb, 4 * Q + 16 : 4 * Q + 32, hs]
             for off, val in ((Q, p_re * x_re - p_im * x_im), (2 * Q + 16, p_re * x_im + p_im * x_re)):
-                hi, lo = split(val)
-                yca[off : off + 16, ls] = hi
-                yca[off + AR : off + AR + 16, ls] = lo
+                put(yca, off, AR, ls, 0, val, level)
 
     def act(t, level):
         for im, ls, hs in sub_tiles(t):
@@ -364,7 +367,7 @@
                     mix[s, hs] = part if level == 0 else mix[s, hs] + part
                     both.append(z)
                 if level < 2:
-                    put_pair(ls, i, both[0], both[1])
+                    put_pair(ls, i, both[0], both[1], level + 1)
                 else:
                     total = total + sum8(both[0]) + sum8(both[1])
             if level == 2:
@@ -379,9 +382,9 @@
         steps = [lambda: first(t)]
         for level in range(3):
             steps += [
-                lambda: transform(t),
+                lambda level=level: transform(t, level),
                 lambda level=level: filt(t, level),
-                lambda: back(t),
+                lambda level=level: back(t, level),
                 lambda level=level: act(t, level),
             ]
         return steps
@@ -1164,6 +1167,20 @@
     return [parts[0]] + [swap(p, step * k, ndev) for k, p in enumerate(parts) if k]
 
 
+def kernel_add_parts(n, *refs):
+    for k, o in enumerate(refs[n + 1 :]):
+        o[...] = (refs[k][...].astype(f32) + refs[n][k].astype(f32)).astype(o.dtype)
+
+
+def sum_core_parts(own, oth, gx, gy, name):
+    got = swap(oth, 1, gx * gy)
+    n = gy // 2
+    parts = add([own], [sds(own.shape[1:], bf16)] * n, name + "_own")
+    outs = [sds(own.shape[1:], f32 if k == 0 else bf16) for k in range(n)]
+    kernel = functools.partial(kernel_add_parts, n)
+    return call(kernel, name + "_sum_core", (), whole(*parts, got), [(o, full(o.shape)) for o in outs], [], 24, 1)
+
+
 def sum_core(own, oth, gx, gy, name):
     got = swap(oth, 1, gx * gy)
     return add([own, got], [sds(own.shape[1:], f32 if k == 0 else bf16) for k in range(gy // 2)], name + "_sum_core")
@@ -1215,7 +1232,7 @@
     dmid, out_rows, dq, dmix, own, oth, gwh, gwp, sums, bsum = middle(
         gx, gy, pos, xrow, up, mixed, q, wh, wp, vec, bm1, mlp_blocks, mlp_len
     )
-    parts = sum_core(own, oth, gx, gy, "mlp")
+    parts = sum_core_parts(own, oth, gx, gy, "mlp")
     parts, dmix = after((parts, dmix))
     mlp_plane = travel(parts, 2, ndev)
     dmer, own, oth = backward(

time: 167 us -> 164 us (0.982)
    pallas_call x13 -> x14, Pallas kernels: 113 us -> 112 us  [call(): pl.pallas_call(kernel, grid=grid, in_specs=[s for _, s in ins], out_shape...]
  transfers between devices with their start and end apart: 28 -> 28, of which waited for: 7 -> 8; matrix products, arithmetic and copies ran while one was open for 0% -> 0% of each run, Pallas kernels for 43% -> 43%
where the time goes in v3:
time: 164 us
  Pallas kernels  112 us (68%)
  starting transfers between devices  34.1 us (21%)
  waiting for transfers between devices  10.1 us (6%)
  local copies, waits for them, and re-layouts  5.83 us (4%)
    pallas_call x14, Pallas kernels, call(): pl.pallas_call(kernel, grid=grid, in_specs=[s for _, s in ins], out_shape...  112 us
    ppermute x28, starting transfers between devices, swap(): return lax.ppermute(x, AXES, [(k, k ^ mask) for k in range(ndev)])  34.1 us
    ppermute x28, waiting for transfers between devices, swap(): return lax.ppermute(x, AXES, [(k, k ^ mask) for k in range(ndev)])  10.1 us
  transfers between devices with their start and end apart: 28, of which 8 were waited for; matrix products, arithmetic and copies ran while one was open for 0% of the time, Pallas kernels for 43%

profile of v3, /device:TPU:0, one launch (start us, length us, event | category | flops | bytes accessed | tf_op | source)
XLA Modules:
  0.0 164.1 jit_solution(4442653574739518021)
XLA Ops:
  0.7 0.9 dynamic_update_slice.7
  1.6 1.1 dynamic_update_slice.6
  2.8 5.1 %collective-permute-start.2 = (bf16[192,128]{1,0:T(8,128)(2,1)S(1)}, bf16[192,128]{1,0:T(8,128)(2,1)S(1)}, u32[]{:S(2)}, u32[]{:S(2)}) collective-permute-start(bf16[192,128]{1,0:T(8,128)(2,1)S(1)} %maximum_maximum_fusion), channel_id=1, source_target_pairs={{0,24},{1,25},{2,26},{3,27},{4,28},{5,29},{6,30},{7,31},{8,16},{9,... | collective-permute-start | bytes 147464 | tf_op jit(solution)/shard_map/ppermute | solution.py:1155
  8.0 0.6 collective-permute-start
  8.6 4.8 %prep.1 = (bf16[2304,384]{1,0:T(8,128)(2,1)}, bf16[2304,384]{1,0:T(8,128)(2,1)}, f32[2304,128]{1,0:T(8,128)}) custom-call(bf16[14,20,8,384]{3,2,1,0:T(8,128)(2,1)} %bitcast.47), custom_call_target="tpu_custom_call" | custom-call | flops 4000000000 | bytes 4000000 | tf_op jit(solution)/shard_map/prep/pallas_call | solution.py:1018
  14.1 3.8 %collective-permute-start.8 = (bf16[288,128]{1,0:T(8,128)(2,1)S(1)}, bf16[288,128]{1,0:T(8,128)(2,1)S(1)}, u32[]{:S(2)}, u32[]{:S(2)}) collective-permute-start(bf16[288,128]{1,0:T(8,128)(2,1)S(1)} %bitcast.36), channel_id=1, source_target_pairs={{0,24},{1,25},{2,26},{3,27},{4,28},{5,29},{6,30},{7,31},{8,16},{9,... | collective-permute-start | bytes 221192 | tf_op jit(solution)/shard_map/ppermute | solution.py:1155
  17.9 0.6 collective-permute-start.6
  18.6 2.7 %collective-permute-start.5 = (bf16[4,192,128]{2,1,0:T(8,128)(2,1)S(1)}, bf16[4,192,128]{2,1,0:T(8,128)(2,1)S(1)}, u32[]{:S(2)}, u32[]{:S(2)}) collective-permute-start(bf16[4,192,128]{2,1,0:T(8,128)(2,1)S(1)} %pad_maximum_fusion.3), channel_id=1, source_target_pairs={{0,6},{1,7},{2,4},{3,5},{4,2},{5,3},{6,0},{7,1},{8,14},{9,15},{10,... | collective-permute-start | bytes 589832 | tf_op jit(solution)/shard_map/ppermute | solution.py:1155
  21.3 0.5 collective-permute-start.4
  21.8 0.4 collective-permute-start.3
  22.2 3.8 %upstream.1.up = bf16[2304,384]{1,0:T(8,128)(2,1)} custom-call(s32[1]{0:T(128)S(6)} %copy.25.counts, bf16[14,20,8,384]{3,2,1,0:T(8,128)(2,1)} %bitcast.48), custom_call_target="tpu_custom_call" | custom-call | flops 3000000000 | bytes 3000000 | tf_op jit(solution)/shard_map/upstream/pallas_call | solution.py:1018
  26.1 1.2 collective-permute-done.5
  27.3 1.7 %collective-permute-done.4 = bf16[4,192,128]{2,1,0:T(8,128)(2,1)S(1)} collective-permute-done((bf16[4,192,128]{2,1,0:T(8,128)(2,1)S(1)}, bf16[4,192,128]{2,1,0:T(8,128)(2,1)S(1)}, u32[]{:S(2)}, u32[]{:S(2)}) %collective-permute-start.4) | collective-permute-done | bytes 196640 | tf_op jit(solution)/shard_map/ppermute | solution.py:1155
  29.3 0.5 collective-permute-start.10
  29.8 0.6 pad_add_fusion.pos
  30.4 1.6 collective-permute-done.10
  32.1 1.7 %collective-permute-start.13 = (bf16[2,4,288,128]{3,2,1,0:T(8,128)(2,1)S(1)}, bf16[2,4,288,128]{3,2,1,0:T(8,128)(2,1)S(1)}, u32[]{:S(2)}, u32[]{:S(2)}) collective-permute-start(bf16[2,4,288,128]{3,2,1,0:T(8,128)(2,1)S(1)} %pad_maximum_fusion.1.refs_0_), channel_id=1, source_target_pairs={{0,6},{1,7},{2,4},{3,5},{4,2},{5,3},{6,0},{7,1},{8,14},{9,15},{10,... | collective-permute-start | bytes 1769480 | tf_op jit(solution)/shard_map/ppermute | solution.py:1155
  33.8 1.3 collective-permute-start.12
  35.1 0.5 collective-permute-start.11
  35.7 25.2 %focal_forward.1 = (f32[2304,384]{1,0:T(8,128)}, f32[2304,128]{1,0:T(8,128)}, bf16[2304,384]{1,0:T(8,128)(2,1)}, bf16[3456,768]{1,0:T(8,128)(2,1)}, bf16[3456,76...) custom-call(s32[8]{0:T(128)} %bucket.3, ...), custom_call_target="tpu_custom_call" | custom-call | flops 28000000000 | bytes 28000000 | tf_op jit(solution)/shard_map/focal_forward/pallas_call | solution.py:1018
  61.1 0.6 copy-done.13
  61.7 0.2 copy-done.14
  61.9 0.2 copy-done.15
  62.1 41.0 %middle.1 = (f32[2304,384]{1,0:T(8,128)}, bf16[2304,384]{1,0:T(8,128)(2,1)}, bf16[2304,384]{1,0:T(8,128)(2,1)}, f32[2304,384]{1,0:T(8,128)}, bf16[4,4,288,128]{3...) custom-call(s32[2]{0:T(128)} %pad_add_fusion.pos, ...), custom_call_target="tpu_custom_call" | custom-call | flops 41999998976 | bytes 42000000 | tf_op jit(solution)/shard_map/middle/pallas_call | solution.py:1018
  103.2 1.3 copy-done
  104.5 0.2 mlp_own.1
  104.7 1.6 collective-permute-done.14.refs_4_
  106.3 0.3 mlp_sum_core.1
  106.5 1.6 collective-permute-start.15
  108.1 0.7 collective-permute-start.16
  108.8 1.3 collective-permute-start.17
  110.1 25.6 %focal_backward.1 = (bf16[2304,896]{1,0:T(8,128)(2,1)}, bf16[4,4,192,128]{3,2,1,0:T(8,128)(2,1)}, bf16[4,4,192,128]{3,2,1,0:T(8,128)(2,1)}) custom-call(s32[8]{0:T(128)} %bucket.3, s32[2]{0:T(128)} %pad_add_fusion.pos, bf16[2304,384]{1,0:T(8,128)(2,1)} %get-tuple-element.148.nb_ref, bf16[2304,384]{1,0:T(8,128)(2,1)} %get-tuple-element.149.dq_ref, ...), custom_call_target="tpu_custom_call" | custom-call | flops 28000000000 | bytes 28000000 | tf_op jit(solution)/shard_map/focal_backward/pallas_call | solution.py:1018
  136.0 1.4 collective-permute-start.22
  137.4 2.6 %collective-permute-start.23 = (bf16[288,128]{1,0:T(8,128)(2,1)S(1)}, bf16[288,128]{1,0:T(8,128)(2,1)S(1)}, u32[]{:S(2)}, u32[]{:S(2)}) collective-permute-start(bf16[288,128]{1,0:T(8,128)(2,1)S(1)} %get-tuple-element.176), channel_id=1, source_target_pairs={{0,16},{1,17},{2,18},{3,19},{4,20},{5,21},{6,22},{7,23},{8,24},{9,... | collective-permute-start | bytes 221192 | tf_op jit(solution)/shard_map/ppermute | solution.py:1155
  140.1 0.4 collective-permute-start.24
  140.7 1.6 collective-permute-start.19
  142.2 0.7 collective-permute-start.20
  143.0 1.3 collective-permute-start.21
  144.3 6.8 %tail.1 = f32[14,20,8,384]{3,2,1,0:T(8,128)} custom-call(bf16[2304,896]{1,0:T(8,128)(2,1)S(1)} %copy-done.2, bf16[384,896]{1,0:T(8,128)(2,1)S(1)} %copy-done.7, bf16[2304,384]{1,0:T(8,128)(2,1)S(1)} %copy-done.4, f32[2304,128]{1,0:T(8,128)S(1)} %copy-done.6, f32[2304,384]{1,0:T(8,128)S(1)} %copy-done.3, f32[16,384]{1,0:T(8,128)S(1)} %copy-done.8), custom_call_target="tpu_custom_call" | custom-call | flops 8000000000 | bytes 8000000 | tf_op jit(solution)/shard_map/tail/pallas_call | solution.py:1018
  151.1 1.5 collective-permute-done.20.refs_2_
  152.7 0.6 collective-permute-start.25
  153.3 3.5 %collective-permute-start.26 = (bf16[192,128]{1,0:T(8,128)(2,1)S(1)}, bf16[192,128]{1,0:T(8,128)(2,1)S(1)}, u32[]{:S(2)}, u32[]{:S(2)}) collective-permute-start(bf16[192,128]{1,0:T(8,128)(2,1)S(1)} %get-tuple-element.187), channel_id=1, source_target_pairs={{0,16},{1,17},{2,18},{3,19},{4,20},{5,21},{6,22},{7,23},{8,24},{9,... | collective-permute-start | bytes 147464 | tf_op jit(solution)/shard_map/ppermute | solution.py:1155
  156.8 0.4 collective-permute-start.27
  157.2 2.6 %out_tokens.1 = bf16[14,20,8,384]{3,2,1,0:T(8,128)(2,1)} custom-call(s32[1]{0:T(128)S(6)} %copy.25.counts, bf16[2304,384]{1,0:T(8,128)(2,1)S(1)} %copy-done.5), custom_call_target="tpu_custom_call" | custom-call | flops 5000000000 | bytes 5000000 | tf_op jit(solution)/shard_map/out_tokens/pallas_call | solution.py:1018
  159.8 0.7 mlp_sum_line.1
  160.5 2.2 %collective-permute-done.27.refs_3_ = bf16[192,128]{1,0:T(8,128)(2,1)S(1)} collective-permute-done((bf16[192,128]{1,0:T(8,128)(2,1)S(1)}, bf16[192,128]{1,0:T(8,128)(2,1)S(1)}, u32[]{:S(2)}, u32[]{:S(2)}) %collective-permute-start.27) | collective-permute-done | bytes 49184 | tf_op jit(solution)/shard_map/ppermute | solution.py:1155
  162.7 0.7 dynamic_slice.6
  163.5 0.7 dynamic_slice.7
  (68 shorter events, 1.4 us)
Async XLA Ops:
  2.8 11.2 %collective-permute-start.2 = (bf16[192,128]{1,0:T(8,128)(2,1)S(1)}, bf16[192,128]{1,0:T(8,128)(2,1)S(1)}, u32[]{:S(2)}, u32[]{:S(2)}) collective-permute-start(bf16[192,128]{1,0:T(8,128)(2,1)S(1)} %maximum_maximum_fusion), channel_id=1, source_target_pairs={{0,24},{1,25},{2,26},{3,27},{4,28},{5,29},{6,30},{7,31},{8,16},{9,... | collective-permute-start | bytes 147464 | tf_op jit(solution)/shard_map/ppermute | solution.py:1155
  8.0 6.1 %collective-permute-start.1 = (bf16[192,128]{1,0:T(8,128)(2,1)S(1)}, bf16[192,128]{1,0:T(8,128)(2,1)S(1)}, u32[]{:S(2)}, u32[]{:S(2)}) collective-permute-start(bf16[192,128]{1,0:T(8,128)(2,1)S(1)} %maximum_maximum_fusion), channel_id=1, source_target_pairs={{0,16},{1,17},{2,18},{3,19},{4,20},{5,21},{6,22},{7,23},{8,24},{9,... | collective-permute-start | bytes 147464 | tf_op jit(solution)/shard_map/ppermute | solution.py:1155
  8.0 6.1 %collective-permute-start = (bf16[192,128]{1,0:T(8,128)(2,1)S(1)}, bf16[192,128]{1,0:T(8,128)(2,1)S(1)}, u32[]{:S(2)}, u32[]{:S(2)}) collective-permute-start(bf16[192,128]{1,0:T(8,128)(2,1)S(1)} %maximum_maximum_fusion), channel_id=1, source_target_pairs={{0,8},{1,9},{2,10},{3,11},{4,12},{5,13},{6,14},{7,15},{8,0},{9,1},... | collective-permute-start | bytes 147464 | tf_op jit(solution)/shard_map/ppermute | solution.py:1155
  8.6 5.5 %copy-start.11 = (bf16[36864]{0:T(1024)(128)(2,1)S(1)}, bf16[36864]{0:T(1024)(128)(2,1)}, u32[]{:S(2)}) copy-start(bf16[36864]{0:T(1024)(128)(2,1)} %param.22) | copy-start | bytes 221188
  14.1 7.7 %collective-permute-start.8 = (bf16[288,128]{1,0:T(8,128)(2,1)S(1)}, bf16[288,128]{1,0:T(8,128)(2,1)S(1)}, u32[]{:S(2)}, u32[]{:S(2)}) collective-permute-start(bf16[288,128]{1,0:T(8,128)(2,1)S(1)} %bitcast.36), channel_id=1, source_target_pairs={{0,24},{1,25},{2,26},{3,27},{4,28},{5,29},{6,30},{7,31},{8,16},{9,... | collective-permute-start | bytes 221192 | tf_op jit(solution)/shard_map/ppermute | solution.py:1155
  17.9 8.1 %collective-permute-start.7 = (bf16[288,128]{1,0:T(8,128)(2,1)S(1)}, bf16[288,128]{1,0:T(8,128)(2,1)S(1)}, u32[]{:S(2)}, u32[]{:S(2)}) collective-permute-start(bf16[288,128]{1,0:T(8,128)(2,1)S(1)} %bitcast.37), channel_id=1, source_target_pairs={{0,16},{1,17},{2,18},{3,19},{4,20},{5,21},{6,22},{7,23},{8,24},{9,... | collective-permute-start | bytes 221192 | tf_op jit(solution)/shard_map/ppermute | solution.py:1155
  17.9 8.1 %collective-permute-start.6 = (bf16[288,128]{1,0:T(8,128)(2,1)S(1)}, bf16[288,128]{1,0:T(8,128)(2,1)S(1)}, u32[]{:S(2)}, u32[]{:S(2)}) collective-permute-start(bf16[288,128]{1,0:T(8,128)(2,1)S(1)} %bitcast.38), channel_id=1, source_target_pairs={{0,8},{1,9},{2,10},{3,11},{4,12},{5,13},{6,14},{7,15},{8,0},{9,1},... | collective-permute-start | bytes 221192 | tf_op jit(solution)/shard_map/ppermute | solution.py:1155
  18.6 8.7 %collective-permute-start.5 = (bf16[4,192,128]{2,1,0:T(8,128)(2,1)S(1)}, bf16[4,192,128]{2,1,0:T(8,128)(2,1)S(1)}, u32[]{:S(2)}, u32[]{:S(2)}) collective-permute-start(bf16[4,192,128]{2,1,0:T(8,128)(2,1)S(1)} %pad_maximum_fusion.3), channel_id=1, source_target_pairs={{0,6},{1,7},{2,4},{3,5},{4,2},{5,3},{6,0},{7,1},{8,14},{9,15},{10,... | collective-permute-start | bytes 589832 | tf_op jit(solution)/shard_map/ppermute | solution.py:1155
  21.3 7.8 %collective-permute-start.4 = (bf16[4,192,128]{2,1,0:T(8,128)(2,1)S(1)}, bf16[4,192,128]{2,1,0:T(8,128)(2,1)S(1)}, u32[]{:S(2)}, u32[]{:S(2)}) collective-permute-start(bf16[4,192,128]{2,1,0:T(8,128)(2,1)S(1)} %pad_maximum_fusion.3), channel_id=1, source_target_pairs={{0,4},{1,5},{2,6},{3,7},{4,0},{5,1},{6,2},{7,3},{8,12},{9,13},{10,... | collective-permute-start | bytes 589832 | tf_op jit(solution)/shard_map/ppermute | solution.py:1155
  21.8 7.3 %collective-permute-start.3 = (bf16[4,192,128]{2,1,0:T(8,128)(2,1)S(1)}, bf16[4,192,128]{2,1,0:T(8,128)(2,1)S(1)}, u32[]{:S(2)}, u32[]{:S(2)}) collective-permute-start(bf16[4,192,128]{2,1,0:T(8,128)(2,1)S(1)} %pad_maximum_fusion.3), channel_id=1, source_target_pairs={{0,2},{1,3},{2,0},{3,1},{4,6},{5,7},{6,4},{7,5},{8,10},{9,11},{10,... | collective-permute-start | bytes 589832 | tf_op jit(solution)/shard_map/ppermute | solution.py:1155
  29.2 6.4 %copy-start.9 = (bf16[4,4,192,128]{3,2,1,0:T(8,128)(2,1)}, bf16[4,4,192,128]{3,2,1,0:T(8,128)(2,1)S(1)}, u32[]{:S(2)}) copy-start(bf16[4,4,192,128]{3,2,1,0:T(8,128)(2,1)S(1)} %pad_maximum_fusion.own) | copy-start | bytes 2359300
  29.2 2.8 %collective-permute-start.9 = (bf16[4,4,192,128]{3,2,1,0:T(8,128)(2,1)S(1)}, bf16[4,4,192,128]{3,2,1,0:T(8,128)(2,1)S(1)}, u32[]{:S(2)}, u32[]{:S(2)}) collective-permute-start(bf16[4,4,192,128]{3,2,1,0:T(8,128)(2,1)S(1)} %pad_maximum_fusion.own), channel_id=1, source_target_pairs={{0,1},{1,0},{2,3},{3,2},{4,5},{5,4},{6,7},{7,6},{8,9},{9,8},{10,11... | collective-permute-start | bytes 2359304 | tf_op jit(solution)/shard_map/ppermute | solution.py:1155
  29.3 2.7 %collective-permute-start.10 = (bf16[4,288,128]{2,1,0:T(8,128)(2,1)S(1)}, bf16[4,288,128]{2,1,0:T(8,128)(2,1)S(1)}, u32[]{:S(2)}, u32[]{:S(2)}) collective-permute-start(bf16[4,288,128]{2,1,0:T(8,128)(2,1)S(1)} %pad_maximum_fusion.2), channel_id=1, source_target_pairs={{0,1},{1,0},{2,3},{3,2},{4,5},{5,4},{6,7},{7,6},{8,9},{9,8},{10,11... | collective-permute-start | bytes 884744 | tf_op jit(solution)/shard_map/ppermute | solution.py:1155
  32.1 28.8 %copy-start.10 = (bf16[2,4,288,128]{3,2,1,0:T(8,128)(2,1)}, bf16[2,4,288,128]{3,2,1,0:T(8,128)(2,1)S(1)}, u32[]{:S(2)}) copy-start(bf16[2,4,288,128]{3,2,1,0:T(8,128)(2,1)S(1)} %pad_maximum_fusion.1.refs_0_) | copy-start | bytes 1769476
  32.1 3.6 %copy-start.12 = (bf16[4,4,192,128]{3,2,1,0:T(8,128)(2,1)}, bf16[4,4,192,128]{3,2,1,0:T(8,128)(2,1)S(1)}, u32[]{:S(2)}) copy-start(bf16[4,4,192,128]{3,2,1,0:T(8,128)(2,1)S(1)} %collective-permute-done.9.oth) | copy-start | bytes 2359300
  32.1 28.8 %collective-permute-start.13 = (bf16[2,4,288,128]{3,2,1,0:T(8,128)(2,1)S(1)}, bf16[2,4,288,128]{3,2,1,0:T(8,128)(2,1)S(1)}, u32[]{:S(2)}, u32[]{:S(2)}) collective-permute-start(bf16[2,4,288,128]{3,2,1,0:T(8,128)(2,1)S(1)} %pad_maximum_fusion.1.refs_0_), channel_id=1, source_target_pairs={{0,6},{1,7},{2,4},{3,5},{4,2},{5,3},{6,0},{7,1},{8,14},{9,15},{10,... | collective-permute-start | bytes 1769480 | tf_op jit(solution)/shard_map/ppermute | solution.py:1155
  33.8 27.3 %collective-permute-start.12 = (bf16[2,4,288,128]{3,2,1,0:T(8,128)(2,1)S(1)}, bf16[2,4,288,128]{3,2,1,0:T(8,128)(2,1)S(1)}, u32[]{:S(2)}, u32[]{:S(2)}) collective-permute-start(bf16[2,4,288,128]{3,2,1,0:T(8,128)(2,1)S(1)} %pad_maximum_fusion.1.refs_0_), channel_id=1, source_target_pairs={{0,4},{1,5},{2,6},{3,7},{4,0},{5,1},{6,2},{7,3},{8,12},{9,13},{10,... | collective-permute-start | bytes 1769480 | tf_op jit(solution)/shard_map/ppermute | solution.py:1155
  35.1 26.0 %collective-permute-start.11 = (bf16[2,4,288,128]{3,2,1,0:T(8,128)(2,1)S(1)}, bf16[2,4,288,128]{3,2,1,0:T(8,128)(2,1)S(1)}, u32[]{:S(2)}, u32[]{:S(2)}) collective-permute-start(bf16[2,4,288,128]{3,2,1,0:T(8,128)(2,1)S(1)} %pad_maximum_fusion.1.refs_0_), channel_id=1, source_target_pairs={{0,2},{1,3},{2,0},{3,1},{4,6},{5,7},{6,4},{7,5},{8,10},{9,11},{10,... | collective-permute-start | bytes 1769480 | tf_op jit(solution)/shard_map/ppermute | solution.py:1155
  60.9 0.8 copy-start.13
  61.1 0.8 copy-start.14
  61.1 1.0 copy-start.15
  103.1 3.1 %collective-permute-start.14 = (bf16[4,4,288,128]{3,2,1,0:T(8,128)(2,1)}, bf16[4,4,288,128]{3,2,1,0:T(8,128)(2,1)S(1)}, u32[]{:S(2)}, u32[]{:S(2)}) collective-permute-start(bf16[4,4,288,128]{3,2,1,0:T(8,128)(2,1)} %get-tuple-element.138), channel_id=1, source_target_pairs={{0,1},{1,0},{2,3},{3,2},{4,5},{5,4},{6,7},{7,6},{8,9},{9,8},{10,11... | collective-permute-start | bytes 3538952 | tf_op jit(solution)/shard_map/ppermute | solution.py:1155
  103.2 1.3 copy-start
  106.5 29.2 %collective-permute-start.15 = (bf16[4,288,128]{2,1,0:T(8,128)(2,1)S(1)}, bf16[4,288,128]{2,1,0:T(8,128)(2,1)S(1)}, u32[]{:S(2)}, u32[]{:S(2)}) collective-permute-start(bf16[4,288,128]{2,1,0:T(8,128)(2,1)S(1)} %get-tuple-element.145), channel_id=1, source_target_pairs={{0,2},{1,3},{2,0},{3,1},{4,6},{5,7},{6,4},{7,5},{8,10},{9,11},{10,... | collective-permute-start | bytes 884744 | tf_op jit(solution)/shard_map/ppermute | solution.py:1155
  108.1 27.6 %collective-permute-start.16 = (bf16[4,288,128]{2,1,0:T(8,128)(2,1)S(1)}, bf16[4,288,128]{2,1,0:T(8,128)(2,1)S(1)}, u32[]{:S(2)}, u32[]{:S(2)}) collective-permute-start(bf16[4,288,128]{2,1,0:T(8,128)(2,1)S(1)} %get-tuple-element.146), channel_id=1, source_target_pairs={{0,4},{1,5},{2,6},{3,7},{4,0},{5,1},{6,2},{7,3},{8,12},{9,13},{10,... | collective-permute-start | bytes 884744 | tf_op jit(solution)/shard_map/ppermute | solution.py:1155
  108.8 26.9 %collective-permute-start.17 = (bf16[4,288,128]{2,1,0:T(8,128)(2,1)S(1)}, bf16[4,288,128]{2,1,0:T(8,128)(2,1)S(1)}, u32[]{:S(2)}, u32[]{:S(2)}) collective-permute-start(bf16[4,288,128]{2,1,0:T(8,128)(2,1)S(1)} %get-tuple-element.147), channel_id=1, source_target_pairs={{0,6},{1,7},{2,4},{3,5},{4,2},{5,3},{6,0},{7,1},{8,14},{9,15},{10,... | collective-permute-start | bytes 884744 | tf_op jit(solution)/shard_map/ppermute | solution.py:1155
  135.7 4.8 %copy-start.1 = (bf16[4,4,192,128]{3,2,1,0:T(8,128)(2,1)S(1)}, bf16[4,4,192,128]{3,2,1,0:T(8,128)(2,1)}, u32[]{:S(2)}) copy-start(bf16[4,4,192,128]{3,2,1,0:T(8,128)(2,1)} %get-tuple-element.164.refs_0_) | copy-start | bytes 2359300
  135.7 4.8 %collective-permute-start.18 = (bf16[4,4,192,128]{3,2,1,0:T(8,128)(2,1)}, bf16[4,4,192,128]{3,2,1,0:T(8,128)(2,1)S(1)}, u32[]{:S(2)}, u32[]{:S(2)}) collective-permute-start(bf16[4,4,192,128]{3,2,1,0:T(8,128)(2,1)} %get-tuple-element.165), channel_id=1, source_target_pairs={{0,1},{1,0},{2,3},{3,2},{4,5},{5,4},{6,7},{7,6},{8,9},{9,8},{10,11... | collective-permute-start | bytes 2359304 | tf_op jit(solution)/shard_map/ppermute | solution.py:1155
  135.8 8.4 %copy-start.3 = (f32[2304,384]{1,0:T(8,128)S(1)}, f32[2304,384]{1,0:T(8,128)}, u32[]{:S(2)}) copy-start(f32[2304,384]{1,0:T(8,128)} %get-tuple-element.179.dmid) | copy-start | bytes 10616836
  135.8 8.4 %copy-start.7 = (bf16[384,896]{1,0:T(8,128)(2,1)S(1)}, bf16[384,896]{1,0:T(8,128)(2,1)}, u32[]{:S(2)}) copy-start(bf16[384,896]{1,0:T(8,128)(2,1)} %get-tuple-element.159.wf_far.wf) | copy-start | bytes 2064388
  136.0 7.0 %collective-permute-start.22 = (bf16[288,128]{1,0:T(8,128)(2,1)S(1)}, bf16[288,128]{1,0:T(8,128)(2,1)S(1)}, u32[]{:S(2)}, u32[]{:S(2)}) collective-permute-start(bf16[288,128]{1,0:T(8,128)(2,1)S(1)} %get-tuple-element.175), channel_id=1, source_target_pairs={{0,8},{1,9},{2,10},{3,11},{4,12},{5,13},{6,14},{7,15},{8,0},{9,1},... | collective-permute-start | bytes 221192 | tf_op jit(solution)/shard_map/ppermute | solution.py:1155
  137.4 13.7 %collective-permute-start.23 = (bf16[288,128]{1,0:T(8,128)(2,1)S(1)}, bf16[288,128]{1,0:T(8,128)(2,1)S(1)}, u32[]{:S(2)}, u32[]{:S(2)}) collective-permute-start(bf16[288,128]{1,0:T(8,128)(2,1)S(1)} %get-tuple-element.176), channel_id=1, source_target_pairs={{0,16},{1,17},{2,18},{3,19},{4,20},{5,21},{6,22},{7,23},{8,24},{9,... | collective-permute-start | bytes 221192 | tf_op jit(solution)/shard_map/ppermute | solution.py:1155
  140.1 4.2 %copy-start.2 = (bf16[2304,896]{1,0:T(8,128)(2,1)S(1)}, bf16[2304,896]{1,0:T(8,128)(2,1)}, u32[]{:S(2)}) copy-start(bf16[2304,896]{1,0:T(8,128)(2,1)} %get-tuple-element.178.dmer) | copy-start | bytes 12386308
  140.1 4.2 %copy-start.4 = (bf16[2304,384]{1,0:T(8,128)(2,1)S(1)}, bf16[2304,384]{1,0:T(8,128)(2,1)}, u32[]{:S(2)}) copy-start(bf16[2304,384]{1,0:T(8,128)(2,1)} %get-tuple-element.107.x_ref) | copy-start | bytes 5308420
  140.1 4.2 %copy-start.6 = (f32[2304,128]{1,0:T(8,128)S(1)}, f32[2304,128]{1,0:T(8,128)}, u32[]{:S(2)}) copy-start(f32[2304,128]{1,0:T(8,128)} %get-tuple-element.120.stat) | copy-start | bytes 3538948
  140.1 4.2 %copy-start.8 = (f32[16,384]{1,0:T(8,128)S(1)}, f32[16,384]{1,0:T(8,128)}, u32[]{:S(2)}) copy-start(f32[16,384]{1,0:T(8,128)} %get-tuple-element.127.vec) | copy-start | bytes 73732
  140.1 11.0 %collective-permute-start.24 = (bf16[288,128]{1,0:T(8,128)(2,1)S(1)}, bf16[288,128]{1,0:T(8,128)(2,1)S(1)}, u32[]{:S(2)}, u32[]{:S(2)}) collective-permute-start(bf16[288,128]{1,0:T(8,128)(2,1)S(1)} %get-tuple-element.177), channel_id=1, source_target_pairs={{0,24},{1,25},{2,26},{3,27},{4,28},{5,29},{6,30},{7,31},{8,16},{9,... | collective-permute-start | bytes 221192 | tf_op jit(solution)/shard_map/ppermute | solution.py:1155
  140.7 10.4 %collective-permute-start.19 = (bf16[4,192,128]{2,1,0:T(8,128)(2,1)S(1)}, bf16[4,192,128]{2,1,0:T(8,128)(2,1)S(1)}, u32[]{:S(2)}, u32[]{:S(2)}) collective-permute-start(bf16[4,192,128]{2,1,0:T(8,128)(2,1)S(1)} %get-tuple-element.167), channel_id=1, source_target_pairs={{0,2},{1,3},{2,0},{3,1},{4,6},{5,7},{6,4},{7,5},{8,10},{9,11},{10,... | collective-permute-start | bytes 589832 | tf_op jit(solution)/shard_map/ppermute | solution.py:1155
  142.2 10.4 %collective-permute-start.20 = (bf16[4,192,128]{2,1,0:T(8,128)(2,1)S(1)}, bf16[4,192,128]{2,1,0:T(8,128)(2,1)S(1)}, u32[]{:S(2)}, u32[]{:S(2)}) collective-permute-start(bf16[4,192,128]{2,1,0:T(8,128)(2,1)S(1)} %get-tuple-element.168), channel_id=1, source_target_pairs={{0,4},{1,5},{2,6},{3,7},{4,0},{5,1},{6,2},{7,3},{8,12},{9,13},{10,... | collective-permute-start | bytes 589832 | tf_op jit(solution)/shard_map/ppermute | solution.py:1155
  143.0 9.6 %collective-permute-start.21 = (bf16[4,192,128]{2,1,0:T(8,128)(2,1)S(1)}, bf16[4,192,128]{2,1,0:T(8,128)(2,1)S(1)}, u32[]{:S(2)}, u32[]{:S(2)}) collective-permute-start(bf16[4,192,128]{2,1,0:T(8,128)(2,1)S(1)} %get-tuple-element.169), channel_id=1, source_target_pairs={{0,6},{1,7},{2,4},{3,5},{4,2},{5,3},{6,0},{7,1},{8,14},{9,15},{10,... | collective-permute-start | bytes 589832 | tf_op jit(solution)/shard_map/ppermute | solution.py:1155
  152.6 4.6 %copy-start.5 = (bf16[2304,384]{1,0:T(8,128)(2,1)S(1)}, bf16[2304,384]{1,0:T(8,128)(2,1)}, u32[]{:S(2)}) copy-start(bf16[2304,384]{1,0:T(8,128)(2,1)} %get-tuple-element.189.rows_ref) | copy-start | bytes 5308420
  152.7 7.8 %collective-permute-start.25 = (bf16[192,128]{1,0:T(8,128)(2,1)S(1)}, bf16[192,128]{1,0:T(8,128)(2,1)S(1)}, u32[]{:S(2)}, u32[]{:S(2)}) collective-permute-start(bf16[192,128]{1,0:T(8,128)(2,1)S(1)} %get-tuple-element.186), channel_id=1, source_target_pairs={{0,8},{1,9},{2,10},{3,11},{4,12},{5,13},{6,14},{7,15},{8,0},{9,1},... | collective-permute-start | bytes 147464 | tf_op jit(solution)/shard_map/ppermute | solution.py:1155
  153.3 7.2 %collective-permute-start.26 = (bf16[192,128]{1,0:T(8,128)(2,1)S(1)}, bf16[192,128]{1,0:T(8,128)(2,1)S(1)}, u32[]{:S(2)}, u32[]{:S(2)}) collective-permute-start(bf16[192,128]{1,0:T(8,128)(2,1)S(1)} %get-tuple-element.187), channel_id=1, source_target_pairs={{0,16},{1,17},{2,18},{3,19},{4,20},{5,21},{6,22},{7,23},{8,24},{9,... | collective-permute-start | bytes 147464 | tf_op jit(solution)/shard_map/ppermute | solution.py:1155
  156.8 5.9 %collective-permute-start.27 = (bf16[192,128]{1,0:T(8,128)(2,1)S(1)}, bf16[192,128]{1,0:T(8,128)(2,1)S(1)}, u32[]{:S(2)}, u32[]{:S(2)}) collective-permute-start(bf16[192,128]{1,0:T(8,128)(2,1)S(1)} %get-tuple-element.188), channel_id=1, source_target_pairs={{0,24},{1,25},{2,26},{3,27},{4,28},{5,29},{6,30},{7,31},{8,16},{9,... | collective-permute-start | bytes 147464 | tf_op jit(solution)/shard_map/ppermute | solution.py:1155

commit v4 on v3

--- a/solution.py
+++ b/solution.py
@@ -397,9 +397,9 @@
 ):
     blocks = refs[: gy // 2]
     (
-        dmid_o, out_o, dq_o, dmix_o, own, oth, gwh, gwp, sums, bsum,
+        dmid_o, out_o, dq_o, dmix_o, own, oth, gwh_o, gwp_o, sums, bsum,
         mod, modulated, branch, mid, second, dshr, shr, dsec, act, dexp, hid, dact, dbr, dm2, dmod, vacc, bacc, gw1, gw2, flat,
-        w1, w2,
+        w1, w2, gwh, gwp,
     ) = refs[gy // 2 :]
     step = pl.program_id(0)
     start = step == 0
@@ -531,6 +531,8 @@
         for k in range(8):
             sums[k : k + 1, :] = jnp.sum(vacc[k], axis=0, keepdims=True)
         bsum[...] = jnp.broadcast_to(jnp.sum(bacc[...], axis=0, keepdims=True), bsum.shape)
+        gwh_o[...] = gwh[...].astype(bf16)
+        gwp_o[...] = gwp[...].astype(bf16)
         pack_mlp(gx, gy, mlp_len, pos, gw1, gw2, own, oth, flat)
 
 
@@ -682,12 +684,11 @@
         facc[:, :C] = jnp.broadcast_to(sums[S_BQ : S_BQ + 1, :] * 0.125, (8, C))
         colsum = jnp.sum(facc[...], axis=0, keepdims=True)
         fsum[...] = jnp.broadcast_to(colsum, fsum.shape)
-        wide = wf[...].astype(f32)
-        t_hi, t_lo = split(wide * gwf[...])
-        ones = jnp.ones((8, MERGED), bf16)
-        gb[0:8, :] = dot_nt(ones, t_hi) + dot_nt(ones, t_lo)
+        col = jnp.sum(wf[...].astype(f32) * gwf[...], axis=-1, keepdims=True)
+        gb[0:8, :] = jnp.transpose(jnp.broadcast_to(col, (C, 128)))[0:8, :]
         c_hi, c_lo = split(fsum[...])
-        gb[8:16, :] = dot_nt(c_hi, wf[...]) + dot_nt(c_lo, wf[...])
+        both = dot_nt(jnp.concatenate([c_hi, c_lo], axis=0), wf[...])
+        gb[8:16, :] = both[0:8, :] + both[8:16, :]
         g1 = jnp.transpose(jnp.broadcast_to(vec[V_G1 : V_G1 + 1, :], (128, C)))
         b1 = jnp.transpose(jnp.broadcast_to(vec[V_B1 : V_B1 + 1, :], (128, C)))
         for t in range(MERGED // 128):
@@ -941,8 +942,8 @@
         flat[pl.ds(f, 16, stride=STRIDE), :] = v
     for j in range(3):
         ls = slice(128 * j, 128 * j + 128)
-        flat[pl.ds(WF_ROWS + j, C, stride=3), :] = gwh[:, ls]
-        flat[pl.ds(WF_ROWS + W_ROWS + j, C, stride=3), :] = gwp[:, ls]
+        flat[pl.ds(WF_ROWS + j, C, stride=3), :] = gwh[:, ls].astype(f32)
+        flat[pl.ds(WF_ROWS + W_ROWS + j, C, stride=3), :] = gwp[:, ls].astype(f32)
     moved[...] = jnp.zeros_like(moved)
     small[...] = jnp.zeros_like(small)
     start = 0
@@ -1095,14 +1096,14 @@
     ]
     slots = (gy // 2, gx, block_rows(mlp_len), 128)
     outs += [(sds(slots, bf16), full(slots))] * 2
-    outs += [(sds(s, f32), full(s)) for s in ((C, C), (C, C), (8, C), (8, HID))]
+    outs += [(sds(s, t), full(s)) for s, t in (((C, C), bf16), ((C, C), bf16), ((8, C), f32), ((8, HID), f32))]
     ins = [(pos, smem())] + by_rows(BROWS, xrow, up, mixed, q) + whole(wh, wp, vec, bm1, *mlp_blocks)
     blk = (BROWS, C)
     scratch = [
         (blk, f32), (blk, bf16), (blk, f32), (blk, f32), (blk, bf16), (blk, bf16), (blk, f32), (blk, f32),
         ((BROWS, HID), bf16), ((BROWS, HID), bf16), ((2, BROWS, HCHUNK), f32), ((2, BROWS, HCHUNK), f32), (blk, bf16), (blk, bf16), (blk, f32),
         ((8, 8, C), f32), ((8, HID), f32),
-        ((C, HID), f32), ((HID, C), f32), ((span(mlp_len, gx * gy), 128), f32), ((C, HID), bf16), ((HID, C), bf16),
+        ((C, HID), f32), ((HID, C), f32), ((span(mlp_len, gx * gy), 128), f32), ((C, HID), bf16), ((HID, C), bf16), ((C, C), f32), ((C, C), f32),
     ]
     kernel = functools.partial(kernel_middle, gx, gy, mlp_len)
     return call(kernel, "middle", (n // BROWS,), ins, outs, scratch, 60, 42)

time: 164 us -> 164 us (level)
  no operation moved by 1% of the time
where the time goes in v4:
time: 164 us
  Pallas kernels  111 us (68%)
  starting transfers between devices  34.1 us (21%)
  waiting for transfers between devices  10.1 us (6%)
  local copies, waits for them, and re-layouts  5.85 us (4%)
    pallas_call x14, Pallas kernels, call(): pl.pallas_call(kernel, grid=grid, in_specs=[s for _, s in ins], out_shape...  111 us
    ppermute x28, starting transfers between devices, swap(): return lax.ppermute(x, AXES, [(k, k ^ mask) for k in range(ndev)])  34.1 us
    ppermute x28, waiting for transfers between devices, swap(): return lax.ppermute(x, AXES, [(k, k ^ mask) for k in range(ndev)])  10.1 us
  transfers between devices with their start and end apart: 28, of which 8 were waited for; matrix products, arithmetic and copies ran while one was open for 0% of the time, Pallas kernels for 43%

profile of v4, /device:TPU:0, one launch (start us, length us, event | category | flops | bytes accessed | tf_op | source)
XLA Modules:
  0.0 163.8 jit_solution(4213011574303116604)
XLA Ops:
  0.7 0.9 dynamic_update_slice.7
  1.6 1.1 dynamic_update_slice.6
  2.8 5.1 %collective-permute-start.2 = (bf16[192,128]{1,0:T(8,128)(2,1)S(1)}, bf16[192,128]{1,0:T(8,128)(2,1)S(1)}, u32[]{:S(2)}, u32[]{:S(2)}) collective-permute-start(bf16[192,128]{1,0:T(8,128)(2,1)S(1)} %maximum_maximum_fusion), channel_id=1, source_target_pairs={{0,24},{1,25},{2,26},{3,27},{4,28},{5,29},{6,30},{7,31},{8,16},{9,... | collective-permute-start | bytes 147464 | tf_op jit(solution)/shard_map/ppermute | solution.py:1156
  8.0 0.6 collective-permute-start
  8.6 4.8 %prep.1 = (bf16[2304,384]{1,0:T(8,128)(2,1)}, bf16[2304,384]{1,0:T(8,128)(2,1)}, f32[2304,128]{1,0:T(8,128)}) custom-call(bf16[14,20,8,384]{3,2,1,0:T(8,128)(2,1)} %bitcast.47), custom_call_target="tpu_custom_call" | custom-call | flops 4000000000 | bytes 4000000 | tf_op jit(solution)/shard_map/prep/pallas_call | solution.py:1019
  14.1 3.8 %collective-permute-start.8 = (bf16[288,128]{1,0:T(8,128)(2,1)S(1)}, bf16[288,128]{1,0:T(8,128)(2,1)S(1)}, u32[]{:S(2)}, u32[]{:S(2)}) collective-permute-start(bf16[288,128]{1,0:T(8,128)(2,1)S(1)} %bitcast.36), channel_id=1, source_target_pairs={{0,24},{1,25},{2,26},{3,27},{4,28},{5,29},{6,30},{7,31},{8,16},{9,... | collective-permute-start | bytes 221192 | tf_op jit(solution)/shard_map/ppermute | solution.py:1156
  17.9 0.6 collective-permute-start.6
  18.6 2.7 %collective-permute-start.5 = (bf16[4,192,128]{2,1,0:T(8,128)(2,1)S(1)}, bf16[4,192,128]{2,1,0:T(8,128)(2,1)S(1)}, u32[]{:S(2)}, u32[]{:S(2)}) collective-permute-start(bf16[4,192,128]{2,1,0:T(8,128)(2,1)S(1)} %pad_maximum_fusion.3), channel_id=1, source_target_pairs={{0,6},{1,7},{2,4},{3,5},{4,2},{5,3},{6,0},{7,1},{8,14},{9,15},{10,... | collective-permute-start | bytes 589832 | tf_op jit(solution)/shard_map/ppermute | solution.py:1156
  21.3 0.5 collective-permute-start.4
  21.8 0.4 collective-permute-start.3
  22.2 3.8 %upstream.1.up = bf16[2304,384]{1,0:T(8,128)(2,1)} custom-call(s32[1]{0:T(128)S(6)} %copy.25.counts, bf16[14,20,8,384]{3,2,1,0:T(8,128)(2,1)} %bitcast.48), custom_call_target="tpu_custom_call" | custom-call | flops 3000000000 | bytes 3000000 | tf_op jit(solution)/shard_map/upstream/pallas_call | solution.py:1019
  26.1 1.2 collective-permute-done.5
  27.3 1.7 %collective-permute-done.4 = bf16[4,192,128]{2,1,0:T(8,128)(2,1)S(1)} collective-permute-done((bf16[4,192,128]{2,1,0:T(8,128)(2,1)S(1)}, bf16[4,192,128]{2,1,0:T(8,128)(2,1)S(1)}, u32[]{:S(2)}, u32[]{:S(2)}) %collective-permute-start.4) | collective-permute-done | bytes 196640 | tf_op jit(solution)/shard_map/ppermute | solution.py:1156
  29.3 0.5 collective-permute-start.10
  29.8 0.6 pad_add_fusion.pos
  30.4 1.6 collective-permute-done.10
  32.1 1.7 %collective-permute-start.13 = (bf16[2,4,288,128]{3,2,1,0:T(8,128)(2,1)S(1)}, bf16[2,4,288,128]{3,2,1,0:T(8,128)(2,1)S(1)}, u32[]{:S(2)}, u32[]{:S(2)}) collective-permute-start(bf16[2,4,288,128]{3,2,1,0:T(8,128)(2,1)S(1)} %pad_maximum_fusion.1.refs_0_), channel_id=1, source_target_pairs={{0,6},{1,7},{2,4},{3,5},{4,2},{5,3},{6,0},{7,1},{8,14},{9,15},{10,... | collective-permute-start | bytes 1769480 | tf_op jit(solution)/shard_map/ppermute | solution.py:1156
  33.8 1.3 collective-permute-start.12
  35.1 0.5 collective-permute-start.11
  35.7 25.2 %focal_forward.1 = (f32[2304,384]{1,0:T(8,128)}, f32[2304,128]{1,0:T(8,128)}, bf16[2304,384]{1,0:T(8,128)(2,1)}, bf16[3456,768]{1,0:T(8,128)(2,1)}, bf16[3456,76...) custom-call(s32[8]{0:T(128)} %bucket.3, ...), custom_call_target="tpu_custom_call" | custom-call | flops 28000000000 | bytes 28000000 | tf_op jit(solution)/shard_map/focal_forward/pallas_call | solution.py:1019
  61.1 0.6 copy-done.13
  61.7 0.2 copy-done.14
  61.9 0.2 copy-done.15
  62.1 40.9 %middle.1 = (f32[2304,384]{1,0:T(8,128)}, bf16[2304,384]{1,0:T(8,128)(2,1)}, bf16[2304,384]{1,0:T(8,128)(2,1)}, f32[2304,384]{1,0:T(8,128)}, bf16[4,4,288,128]{3...) custom-call(s32[2]{0:T(128)} %pad_add_fusion.pos, ...), custom_call_target="tpu_custom_call" | custom-call | flops 41999998976 | bytes 42000000 | tf_op jit(solution)/shard_map/middle/pallas_call | solution.py:1019
  103.1 1.3 copy-done
  104.4 0.2 mlp_own.1
  104.6 1.6 collective-permute-done.14.refs_4_
  106.2 0.3 mlp_sum_core.1
  106.4 1.6 collective-permute-start.15
  108.0 0.7 collective-permute-start.16
  108.7 1.3 collective-permute-start.17
  110.0 25.4 %focal_backward.1 = (bf16[2304,896]{1,0:T(8,128)(2,1)}, bf16[4,4,192,128]{3,2,1,0:T(8,128)(2,1)}, bf16[4,4,192,128]{3,2,1,0:T(8,128)(2,1)}) custom-call(s32[8]{0:T(128)} %bucket.3, s32[2]{0:T(128)} %pad_add_fusion.pos, bf16[2304,384]{1,0:T(8,128)(2,1)} %get-tuple-element.148.nb_ref, bf16[2304,384]{1,0:T(8,128)(2,1)} %get-tuple-element.149.dq_ref, ...), custom_call_target="tpu_custom_call" | custom-call | flops 28000000000 | bytes 28000000 | tf_op jit(solution)/shard_map/focal_backward/pallas_call | solution.py:1019
  135.7 1.4 collective-permute-start.22
  137.1 2.6 %collective-permute-start.23 = (bf16[288,128]{1,0:T(8,128)(2,1)S(1)}, bf16[288,128]{1,0:T(8,128)(2,1)S(1)}, u32[]{:S(2)}, u32[]{:S(2)}) collective-permute-start(bf16[288,128]{1,0:T(8,128)(2,1)S(1)} %get-tuple-element.176), channel_id=1, source_target_pairs={{0,16},{1,17},{2,18},{3,19},{4,20},{5,21},{6,22},{7,23},{8,24},{9,... | collective-permute-start | bytes 221192 | tf_op jit(solution)/shard_map/ppermute | solution.py:1156
  139.8 0.4 collective-permute-start.24
  140.4 1.6 collective-permute-start.19
  141.9 0.7 collective-permute-start.20
  142.7 1.3 collective-permute-start.21
  144.0 6.8 %tail.1 = f32[14,20,8,384]{3,2,1,0:T(8,128)} custom-call(bf16[2304,896]{1,0:T(8,128)(2,1)S(1)} %copy-done.2, bf16[384,896]{1,0:T(8,128)(2,1)S(1)} %copy-done.7, bf16[2304,384]{1,0:T(8,128)(2,1)S(1)} %copy-done.4, f32[2304,128]{1,0:T(8,128)S(1)} %copy-done.6, f32[2304,384]{1,0:T(8,128)S(1)} %copy-done.3, f32[16,384]{1,0:T(8,128)S(1)} %copy-done.8), custom_call_target="tpu_custom_call" | custom-call | flops 8000000000 | bytes 8000000 | tf_op jit(solution)/shard_map/tail/pallas_call | solution.py:1019
  150.8 1.5 collective-permute-done.20.refs_2_
  152.4 0.6 collective-permute-start.25
  153.0 3.5 %collective-permute-start.26 = (bf16[192,128]{1,0:T(8,128)(2,1)S(1)}, bf16[192,128]{1,0:T(8,128)(2,1)S(1)}, u32[]{:S(2)}, u32[]{:S(2)}) collective-permute-start(bf16[192,128]{1,0:T(8,128)(2,1)S(1)} %get-tuple-element.187), channel_id=1, source_target_pairs={{0,16},{1,17},{2,18},{3,19},{4,20},{5,21},{6,22},{7,23},{8,24},{9,... | collective-permute-start | bytes 147464 | tf_op jit(solution)/shard_map/ppermute | solution.py:1156
  156.5 0.4 collective-permute-start.27
  156.9 2.6 %out_tokens.1 = bf16[14,20,8,384]{3,2,1,0:T(8,128)(2,1)} custom-call(s32[1]{0:T(128)S(6)} %copy.25.counts, bf16[2304,384]{1,0:T(8,128)(2,1)S(1)} %copy-done.5), custom_call_target="tpu_custom_call" | custom-call | flops 5000000000 | bytes 5000000 | tf_op jit(solution)/shard_map/out_tokens/pallas_call | solution.py:1019
  159.5 0.7 mlp_sum_line.1
  160.2 2.2 %collective-permute-done.27.refs_3_ = bf16[192,128]{1,0:T(8,128)(2,1)S(1)} collective-permute-done((bf16[192,128]{1,0:T(8,128)(2,1)S(1)}, bf16[192,128]{1,0:T(8,128)(2,1)S(1)}, u32[]{:S(2)}, u32[]{:S(2)}) %collective-permute-start.27) | collective-permute-done | bytes 49184 | tf_op jit(solution)/shard_map/ppermute | solution.py:1156
  162.4 0.7 dynamic_slice.6
  163.2 0.7 dynamic_slice.7
  (68 shorter events, 1.4 us)
Async XLA Ops:
  2.8 11.2 %collective-permute-start.2 = (bf16[192,128]{1,0:T(8,128)(2,1)S(1)}, bf16[192,128]{1,0:T(8,128)(2,1)S(1)}, u32[]{:S(2)}, u32[]{:S(2)}) collective-permute-start(bf16[192,128]{1,0:T(8,128)(2,1)S(1)} %maximum_maximum_fusion), channel_id=1, source_target_pairs={{0,24},{1,25},{2,26},{3,27},{4,28},{5,29},{6,30},{7,31},{8,16},{9,... | collective-permute-start | bytes 147464 | tf_op jit(solution)/shard_map/ppermute | solution.py:1156
  8.0 6.1 %collective-permute-start.1 = (bf16[192,128]{1,0:T(8,128)(2,1)S(1)}, bf16[192,128]{1,0:T(8,128)(2,1)S(1)}, u32[]{:S(2)}, u32[]{:S(2)}) collective-permute-start(bf16[192,128]{1,0:T(8,128)(2,1)S(1)} %maximum_maximum_fusion), channel_id=1, source_target_pairs={{0,16},{1,17},{2,18},{3,19},{4,20},{5,21},{6,22},{7,23},{8,24},{9,... | collective-permute-start | bytes 147464 | tf_op jit(solution)/shard_map/ppermute | solution.py:1156
  8.0 6.1 %collective-permute-start = (bf16[192,128]{1,0:T(8,128)(2,1)S(1)}, bf16[192,128]{1,0:T(8,128)(2,1)S(1)}, u32[]{:S(2)}, u32[]{:S(2)}) collective-permute-start(bf16[192,128]{1,0:T(8,128)(2,1)S(1)} %maximum_maximum_fusion), channel_id=1, source_target_pairs={{0,8},{1,9},{2,10},{3,11},{4,12},{5,13},{6,14},{7,15},{8,0},{9,1},... | collective-permute-start | bytes 147464 | tf_op jit(solution)/shard_map/ppermute | solution.py:1156
  8.6 5.5 %copy-start.11 = (bf16[36864]{0:T(1024)(128)(2,1)S(1)}, bf16[36864]{0:T(1024)(128)(2,1)}, u32[]{:S(2)}) copy-start(bf16[36864]{0:T(1024)(128)(2,1)} %param.22) | copy-start | bytes 221188
  14.1 7.7 %collective-permute-start.8 = (bf16[288,128]{1,0:T(8,128)(2,1)S(1)}, bf16[288,128]{1,0:T(8,128)(2,1)S(1)}, u32[]{:S(2)}, u32[]{:S(2)}) collective-permute-start(bf16[288,128]{1,0:T(8,128)(2,1)S(1)} %bitcast.36), channel_id=1, source_target_pairs={{0,24},{1,25},{2,26},{3,27},{4,28},{5,29},{6,30},{7,31},{8,16},{9,... | collective-permute-start | bytes 221192 | tf_op jit(solution)/shard_map/ppermute | solution.py:1156
  17.9 8.1 %collective-permute-start.7 = (bf16[288,128]{1,0:T(8,128)(2,1)S(1)}, bf16[288,128]{1,0:T(8,128)(2,1)S(1)}, u32[]{:S(2)}, u32[]{:S(2)}) collective-permute-start(bf16[288,128]{1,0:T(8,128)(2,1)S(1)} %bitcast.37), channel_id=1, source_target_pairs={{0,16},{1,17},{2,18},{3,19},{4,20},{5,21},{6,22},{7,23},{8,24},{9,... | collective-permute-start | bytes 221192 | tf_op jit(solution)/shard_map/ppermute | solution.py:1156
  17.9 8.1 %collective-permute-start.6 = (bf16[288,128]{1,0:T(8,128)(2,1)S(1)}, bf16[288,128]{1,0:T(8,128)(2,1)S(1)}, u32[]{:S(2)}, u32[]{:S(2)}) collective-permute-start(bf16[288,128]{1,0:T(8,128)(2,1)S(1)} %bitcast.38), channel_id=1, source_target_pairs={{0,8},{1,9},{2,10},{3,11},{4,12},{5,13},{6,14},{7,15},{8,0},{9,1},... | collective-permute-start | bytes 221192 | tf_op jit(solution)/shard_map/ppermute | solution.py:1156
  18.6 8.7 %collective-permute-start.5 = (bf16[4,192,128]{2,1,0:T(8,128)(2,1)S(1)}, bf16[4,192,128]{2,1,0:T(8,128)(2,1)S(1)}, u32[]{:S(2)}, u32[]{:S(2)}) collective-permute-start(bf16[4,192,128]{2,1,0:T(8,128)(2,1)S(1)} %pad_maximum_fusion.3), channel_id=1, source_target_pairs={{0,6},{1,7},{2,4},{3,5},{4,2},{5,3},{6,0},{7,1},{8,14},{9,15},{10,... | collective-permute-start | bytes 589832 | tf_op jit(solution)/shard_map/ppermute | solution.py:1156
  21.3 7.8 %collective-permute-start.4 = (bf16[4,192,128]{2,1,0:T(8,128)(2,1)S(1)}, bf16[4,192,128]{2,1,0:T(8,128)(2,1)S(1)}, u32[]{:S(2)}, u32[]{:S(2)}) collective-permute-start(bf16[4,192,128]{2,1,0:T(8,128)(2,1)S(1)} %pad_maximum_fusion.3), channel_id=1, source_target_pairs={{0,4},{1,5},{2,6},{3,7},{4,0},{5,1},{6,2},{7,3},{8,12},{9,13},{10,... | collective-permute-start | bytes 589832 | tf_op jit(solution)/shard_map/ppermute | solution.py:1156
  21.8 7.3 %collective-permute-start.3 = (bf16[4,192,128]{2,1,0:T(8,128)(2,1)S(1)}, bf16[4,192,128]{2,1,0:T(8,128)(2,1)S(1)}, u32[]{:S(2)}, u32[]{:S(2)}) collective-permute-start(bf16[4,192,128]{2,1,0:T(8,128)(2,1)S(1)} %pad_maximum_fusion.3), channel_id=1, source_target_pairs={{0,2},{1,3},{2,0},{3,1},{4,6},{5,7},{6,4},{7,5},{8,10},{9,11},{10,... | collective-permute-start | bytes 589832 | tf_op jit(solution)/shard_map/ppermute | solution.py:1156
  29.2 6.4 %copy-start.9 = (bf16[4,4,192,128]{3,2,1,0:T(8,128)(2,1)}, bf16[4,4,192,128]{3,2,1,0:T(8,128)(2,1)S(1)}, u32[]{:S(2)}) copy-start(bf16[4,4,192,128]{3,2,1,0:T(8,128)(2,1)S(1)} %pad_maximum_fusion.own) | copy-start | bytes 2359300
  29.2 2.8 %collective-permute-start.9 = (bf16[4,4,192,128]{3,2,1,0:T(8,128)(2,1)S(1)}, bf16[4,4,192,128]{3,2,1,0:T(8,128)(2,1)S(1)}, u32[]{:S(2)}, u32[]{:S(2)}) collective-permute-start(bf16[4,4,192,128]{3,2,1,0:T(8,128)(2,1)S(1)} %pad_maximum_fusion.own), channel_id=1, source_target_pairs={{0,1},{1,0},{2,3},{3,2},{4,5},{5,4},{6,7},{7,6},{8,9},{9,8},{10,11... | collective-permute-start | bytes 2359304 | tf_op jit(solution)/shard_map/ppermute | solution.py:1156
  29.3 2.7 %collective-permute-start.10 = (bf16[4,288,128]{2,1,0:T(8,128)(2,1)S(1)}, bf16[4,288,128]{2,1,0:T(8,128)(2,1)S(1)}, u32[]{:S(2)}, u32[]{:S(2)}) collective-permute-start(bf16[4,288,128]{2,1,0:T(8,128)(2,1)S(1)} %pad_maximum_fusion.2), channel_id=1, source_target_pairs={{0,1},{1,0},{2,3},{3,2},{4,5},{5,4},{6,7},{7,6},{8,9},{9,8},{10,11... | collective-permute-start | bytes 884744 | tf_op jit(solution)/shard_map/ppermute | solution.py:1156
  32.1 28.8 %copy-start.10 = (bf16[2,4,288,128]{3,2,1,0:T(8,128)(2,1)}, bf16[2,4,288,128]{3,2,1,0:T(8,128)(2,1)S(1)}, u32[]{:S(2)}) copy-start(bf16[2,4,288,128]{3,2,1,0:T(8,128)(2,1)S(1)} %pad_maximum_fusion.1.refs_0_) | copy-start | bytes 1769476
  32.1 3.6 %copy-start.12 = (bf16[4,4,192,128]{3,2,1,0:T(8,128)(2,1)}, bf16[4,4,192,128]{3,2,1,0:T(8,128)(2,1)S(1)}, u32[]{:S(2)}) copy-start(bf16[4,4,192,128]{3,2,1,0:T(8,128)(2,1)S(1)} %collective-permute-done.9.oth) | copy-start | bytes 2359300
  32.1 28.8 %collective-permute-start.13 = (bf16[2,4,288,128]{3,2,1,0:T(8,128)(2,1)S(1)}, bf16[2,4,288,128]{3,2,1,0:T(8,128)(2,1)S(1)}, u32[]{:S(2)}, u32[]{:S(2)}) collective-permute-start(bf16[2,4,288,128]{3,2,1,0:T(8,128)(2,1)S(1)} %pad_maximum_fusion.1.refs_0_), channel_id=1, source_target_pairs={{0,6},{1,7},{2,4},{3,5},{4,2},{5,3},{6,0},{7,1},{8,14},{9,15},{10,... | collective-permute-start | bytes 1769480 | tf_op jit(solution)/shard_map/ppermute | solution.py:1156
  33.8 27.3 %collective-permute-start.12 = (bf16[2,4,288,128]{3,2,1,0:T(8,128)(2,1)S(1)}, bf16[2,4,288,128]{3,2,1,0:T(8,128)(2,1)S(1)}, u32[]{:S(2)}, u32[]{:S(2)}) collective-permute-start(bf16[2,4,288,128]{3,2,1,0:T(8,128)(2,1)S(1)} %pad_maximum_fusion.1.refs_0_), channel_id=1, source_target_pairs={{0,4},{1,5},{2,6},{3,7},{4,0},{5,1},{6,2},{7,3},{8,12},{9,13},{10,... | collective-permute-start | bytes 1769480 | tf_op jit(solution)/shard_map/ppermute | solution.py:1156
  35.1 26.0 %collective-permute-start.11 = (bf16[2,4,288,128]{3,2,1,0:T(8,128)(2,1)S(1)}, bf16[2,4,288,128]{3,2,1,0:T(8,128)(2,1)S(1)}, u32[]{:S(2)}, u32[]{:S(2)}) collective-permute-start(bf16[2,4,288,128]{3,2,1,0:T(8,128)(2,1)S(1)} %pad_maximum_fusion.1.refs_0_), channel_id=1, source_target_pairs={{0,2},{1,3},{2,0},{3,1},{4,6},{5,7},{6,4},{7,5},{8,10},{9,11},{10,... | collective-permute-start | bytes 1769480 | tf_op jit(solution)/shard_map/ppermute | solution.py:1156
  60.9 0.8 copy-start.13
  61.1 0.9 copy-start.14
  61.1 1.0 copy-start.15
  103.0 3.1 %collective-permute-start.14 = (bf16[4,4,288,128]{3,2,1,0:T(8,128)(2,1)}, bf16[4,4,288,128]{3,2,1,0:T(8,128)(2,1)S(1)}, u32[]{:S(2)}, u32[]{:S(2)}) collective-permute-start(bf16[4,4,288,128]{3,2,1,0:T(8,128)(2,1)} %get-tuple-element.138), channel_id=1, source_target_pairs={{0,1},{1,0},{2,3},{3,2},{4,5},{5,4},{6,7},{7,6},{8,9},{9,8},{10,11... | collective-permute-start | bytes 3538952 | tf_op jit(solution)/shard_map/ppermute | solution.py:1156
  103.1 1.3 copy-start
  106.4 29.0 %collective-permute-start.15 = (bf16[4,288,128]{2,1,0:T(8,128)(2,1)S(1)}, bf16[4,288,128]{2,1,0:T(8,128)(2,1)S(1)}, u32[]{:S(2)}, u32[]{:S(2)}) collective-permute-start(bf16[4,288,128]{2,1,0:T(8,128)(2,1)S(1)} %get-tuple-element.145), channel_id=1, source_target_pairs={{0,2},{1,3},{2,0},{3,1},{4,6},{5,7},{6,4},{7,5},{8,10},{9,11},{10,... | collective-permute-start | bytes 884744 | tf_op jit(solution)/shard_map/ppermute | solution.py:1156
  108.0 27.4 %collective-permute-start.16 = (bf16[4,288,128]{2,1,0:T(8,128)(2,1)S(1)}, bf16[4,288,128]{2,1,0:T(8,128)(2,1)S(1)}, u32[]{:S(2)}, u32[]{:S(2)}) collective-permute-start(bf16[4,288,128]{2,1,0:T(8,128)(2,1)S(1)} %get-tuple-element.146), channel_id=1, source_target_pairs={{0,4},{1,5},{2,6},{3,7},{4,0},{5,1},{6,2},{7,3},{8,12},{9,13},{10,... | collective-permute-start | bytes 884744 | tf_op jit(solution)/shard_map/ppermute | solution.py:1156
  108.7 26.7 %collective-permute-start.17 = (bf16[4,288,128]{2,1,0:T(8,128)(2,1)S(1)}, bf16[4,288,128]{2,1,0:T(8,128)(2,1)S(1)}, u32[]{:S(2)}, u32[]{:S(2)}) collective-permute-start(bf16[4,288,128]{2,1,0:T(8,128)(2,1)S(1)} %get-tuple-element.147), channel_id=1, source_target_pairs={{0,6},{1,7},{2,4},{3,5},{4,2},{5,3},{6,0},{7,1},{8,14},{9,15},{10,... | collective-permute-start | bytes 884744 | tf_op jit(solution)/shard_map/ppermute | solution.py:1156
  135.4 4.8 %copy-start.1 = (bf16[4,4,192,128]{3,2,1,0:T(8,128)(2,1)S(1)}, bf16[4,4,192,128]{3,2,1,0:T(8,128)(2,1)}, u32[]{:S(2)}) copy-start(bf16[4,4,192,128]{3,2,1,0:T(8,128)(2,1)} %get-tuple-element.164.refs_0_) | copy-start | bytes 2359300
  135.4 4.8 %collective-permute-start.18 = (bf16[4,4,192,128]{3,2,1,0:T(8,128)(2,1)}, bf16[4,4,192,128]{3,2,1,0:T(8,128)(2,1)S(1)}, u32[]{:S(2)}, u32[]{:S(2)}) collective-permute-start(bf16[4,4,192,128]{3,2,1,0:T(8,128)(2,1)} %get-tuple-element.165), channel_id=1, source_target_pairs={{0,1},{1,0},{2,3},{3,2},{4,5},{5,4},{6,7},{7,6},{8,9},{9,8},{10,11... | collective-permute-start | bytes 2359304 | tf_op jit(solution)/shard_map/ppermute | solution.py:1156
  135.5 8.4 %copy-start.3 = (f32[2304,384]{1,0:T(8,128)S(1)}, f32[2304,384]{1,0:T(8,128)}, u32[]{:S(2)}) copy-start(f32[2304,384]{1,0:T(8,128)} %get-tuple-element.179.dmid) | copy-start | bytes 10616836
  135.5 8.4 %copy-start.7 = (bf16[384,896]{1,0:T(8,128)(2,1)S(1)}, bf16[384,896]{1,0:T(8,128)(2,1)}, u32[]{:S(2)}) copy-start(bf16[384,896]{1,0:T(8,128)(2,1)} %get-tuple-element.159.wf_far.wf) | copy-start | bytes 2064388
  135.7 7.0 %collective-permute-start.22 = (bf16[288,128]{1,0:T(8,128)(2,1)S(1)}, bf16[288,128]{1,0:T(8,128)(2,1)S(1)}, u32[]{:S(2)}, u32[]{:S(2)}) collective-permute-start(bf16[288,128]{1,0:T(8,128)(2,1)S(1)} %get-tuple-element.175), channel_id=1, source_target_pairs={{0,8},{1,9},{2,10},{3,11},{4,12},{5,13},{6,14},{7,15},{8,0},{9,1},... | collective-permute-start | bytes 221192 | tf_op jit(solution)/shard_map/ppermute | solution.py:1156
  137.1 13.7 %collective-permute-start.23 = (bf16[288,128]{1,0:T(8,128)(2,1)S(1)}, bf16[288,128]{1,0:T(8,128)(2,1)S(1)}, u32[]{:S(2)}, u32[]{:S(2)}) collective-permute-start(bf16[288,128]{1,0:T(8,128)(2,1)S(1)} %get-tuple-element.176), channel_id=1, source_target_pairs={{0,16},{1,17},{2,18},{3,19},{4,20},{5,21},{6,22},{7,23},{8,24},{9,... | collective-permute-start | bytes 221192 | tf_op jit(solution)/shard_map/ppermute | solution.py:1156
  139.8 4.2 %copy-start.2 = (bf16[2304,896]{1,0:T(8,128)(2,1)S(1)}, bf16[2304,896]{1,0:T(8,128)(2,1)}, u32[]{:S(2)}) copy-start(bf16[2304,896]{1,0:T(8,128)(2,1)} %get-tuple-element.178.dmer) | copy-start | bytes 12386308
  139.8 4.2 %copy-start.4 = (bf16[2304,384]{1,0:T(8,128)(2,1)S(1)}, bf16[2304,384]{1,0:T(8,128)(2,1)}, u32[]{:S(2)}) copy-start(bf16[2304,384]{1,0:T(8,128)(2,1)} %get-tuple-element.107.x_ref) | copy-start | bytes 5308420
  139.8 4.2 %copy-start.6 = (f32[2304,128]{1,0:T(8,128)S(1)}, f32[2304,128]{1,0:T(8,128)}, u32[]{:S(2)}) copy-start(f32[2304,128]{1,0:T(8,128)} %get-tuple-element.120.stat) | copy-start | bytes 3538948
  139.8 4.2 %copy-start.8 = (f32[16,384]{1,0:T(8,128)S(1)}, f32[16,384]{1,0:T(8,128)}, u32[]{:S(2)}) copy-start(f32[16,384]{1,0:T(8,128)} %get-tuple-element.127.vec) | copy-start | bytes 73732
  139.8 11.0 %collective-permute-start.24 = (bf16[288,128]{1,0:T(8,128)(2,1)S(1)}, bf16[288,128]{1,0:T(8,128)(2,1)S(1)}, u32[]{:S(2)}, u32[]{:S(2)}) collective-permute-start(bf16[288,128]{1,0:T(8,128)(2,1)S(1)} %get-tuple-element.177), channel_id=1, source_target_pairs={{0,24},{1,25},{2,26},{3,27},{4,28},{5,29},{6,30},{7,31},{8,16},{9,... | collective-permute-start | bytes 221192 | tf_op jit(solution)/shard_map/ppermute | solution.py:1156
  140.4 10.4 %collective-permute-start.19 = (bf16[4,192,128]{2,1,0:T(8,128)(2,1)S(1)}, bf16[4,192,128]{2,1,0:T(8,128)(2,1)S(1)}, u32[]{:S(2)}, u32[]{:S(2)}) collective-permute-start(bf16[4,192,128]{2,1,0:T(8,128)(2,1)S(1)} %get-tuple-element.167), channel_id=1, source_target_pairs={{0,2},{1,3},{2,0},{3,1},{4,6},{5,7},{6,4},{7,5},{8,10},{9,11},{10,... | collective-permute-start | bytes 589832 | tf_op jit(solution)/shard_map/ppermute | solution.py:1156
  141.9 10.4 %collective-permute-start.20 = (bf16[4,192,128]{2,1,0:T(8,128)(2,1)S(1)}, bf16[4,192,128]{2,1,0:T(8,128)(2,1)S(1)}, u32[]{:S(2)}, u32[]{:S(2)}) collective-permute-start(bf16[4,192,128]{2,1,0:T(8,128)(2,1)S(1)} %get-tuple-element.168), channel_id=1, source_target_pairs={{0,4},{1,5},{2,6},{3,7},{4,0},{5,1},{6,2},{7,3},{8,12},{9,13},{10,... | collective-permute-start | bytes 589832 | tf_op jit(solution)/shard_map/ppermute | solution.py:1156
  142.7 9.6 %collective-permute-start.21 = (bf16[4,192,128]{2,1,0:T(8,128)(2,1)S(1)}, bf16[4,192,128]{2,1,0:T(8,128)(2,1)S(1)}, u32[]{:S(2)}, u32[]{:S(2)}) collective-permute-start(bf16[4,192,128]{2,1,0:T(8,128)(2,1)S(1)} %get-tuple-element.169), channel_id=1, source_target_pairs={{0,6},{1,7},{2,4},{3,5},{4,2},{5,3},{6,0},{7,1},{8,14},{9,15},{10,... | collective-permute-start | bytes 589832 | tf_op jit(solution)/shard_map/ppermute | solution.py:1156
  152.3 4.6 %copy-start.5 = (bf16[2304,384]{1,0:T(8,128)(2,1)S(1)}, bf16[2304,384]{1,0:T(8,128)(2,1)}, u32[]{:S(2)}) copy-start(bf16[2304,384]{1,0:T(8,128)(2,1)} %get-tuple-element.189.rows_ref) | copy-start | bytes 5308420
  152.4 7.8 %collective-permute-start.25 = (bf16[192,128]{1,0:T(8,128)(2,1)S(1)}, bf16[192,128]{1,0:T(8,128)(2,1)S(1)}, u32[]{:S(2)}, u32[]{:S(2)}) collective-permute-start(bf16[192,128]{1,0:T(8,128)(2,1)S(1)} %get-tuple-element.186), channel_id=1, source_target_pairs={{0,8},{1,9},{2,10},{3,11},{4,12},{5,13},{6,14},{7,15},{8,0},{9,1},... | collective-permute-start | bytes 147464 | tf_op jit(solution)/shard_map/ppermute | solution.py:1156
  153.0 7.2 %collective-permute-start.26 = (bf16[192,128]{1,0:T(8,128)(2,1)S(1)}, bf16[192,128]{1,0:T(8,128)(2,1)S(1)}, u32[]{:S(2)}, u32[]{:S(2)}) collective-permute-start(bf16[192,128]{1,0:T(8,128)(2,1)S(1)} %get-tuple-element.187), channel_id=1, source_target_pairs={{0,16},{1,17},{2,18},{3,19},{4,20},{5,21},{6,22},{7,23},{8,24},{9,... | collective-permute-start | bytes 147464 | tf_op jit(solution)/shard_map/ppermute | solution.py:1156
  156.5 5.9 %collective-permute-start.27 = (bf16[192,128]{1,0:T(8,128)(2,1)S(1)}, bf16[192,128]{1,0:T(8,128)(2,1)S(1)}, u32[]{:S(2)}, u32[]{:S(2)}) collective-permute-start(bf16[192,128]{1,0:T(8,128)(2,1)S(1)} %get-tuple-element.188), channel_id=1, source_target_pairs={{0,24},{1,25},{2,26},{3,27},{4,28},{5,29},{6,30},{7,31},{8,16},{9,... | collective-permute-start | bytes 147464 | tf_op jit(solution)/shard_map/ppermute | solution.py:1156
